TPU v7x, 32 devices: a whole 2x2x4 slice. The times are simulated.
32 devices in a mesh: dp: 8 (over y, x, core), tensor: 4 (over z).
Axes of the slice: x: 2, y: 2, z: 4, core: 2. Of those that a mesh axis runs over, the one named last changes fastest.
Arguments:
- media_tokens: bfloat16 [32, 1280, 1024], P('dp'), may hold values from -6 to 6
- latents: bfloat16 [32, 64, 1024], P('dp'), may hold values from -6 to 6
- image_counts: int32 [32], P('dp'), may hold values from 1 to 5, as said below
- media_gain: float32 [1024], replicated, may hold values from 0.1 to 1.9
- media_shift: float32 [1024], replicated, may hold values from -1.2 to 1.2
- latent_gain: float32 [1024], replicated, may hold values from 0.1 to 1.9
- latent_shift: float32 [1024], replicated, may hold values from -1.2 to 1.2
- feed_gain: float32 [1024], replicated, may hold values from 0.1 to 1.9
- feed_shift: float32 [1024], replicated, may hold values from -1.2 to 1.2
- query_weight: bfloat16 [1024, 512], P(None, 'tensor'), may hold values from -0.1875 to 0.1875
- key_weight: bfloat16 [1024, 512], P(None, 'tensor'), may hold values from -0.1875 to 0.1875
- value_weight: bfloat16 [1024, 512], P(None, 'tensor'), may hold values from -0.1875 to 0.1875
- output_weight: bfloat16 [512, 1024], P('tensor'), may hold values from -4 to 4
- up_weight: bfloat16 [1024, 4096], P('dp', 'tensor'), may hold values from -0.1875 to 0.1875
- down_weight: bfloat16 [4096, 1024], P('tensor', 'dp'), may hold values from -0.09375 to 0.09375
- cotangent: bfloat16 [32, 64, 1024], P('dp'), may hold values from -6 to 6
Outputs:
- new_latents: bfloat16 [32, 64, 1024], P('dp')
- media_grad: bfloat16 [32, 1280, 1024], P('dp', 'tensor')
- latent_grad: bfloat16 [32, 64, 1024], P('dp')
- query_grad: float32 [1024, 512], P('dp', 'tensor')
- key_grad: float32 [1024, 512], P('dp', 'tensor')
- value_grad: float32 [1024, 512], P('dp', 'tensor')
- output_grad: float32 [512, 1024], P('tensor', 'dp')
- up_grad: float32 [1024, 4096], P('dp', 'tensor')
- down_grad: float32 [4096, 1024], P('tensor', 'dp')
- media_gain_grad: float32 [1024], replicated
- media_shift_grad: float32 [1024], replicated
- latent_gain_grad: float32 [1024], P('dp')
- latent_shift_grad: float32 [1024], P('dp')
- feed_gain_grad: float32 [1024], P('dp')
- feed_shift_grad: float32 [1024], P('dp')
Inputs may be any that keep to these rules, and one draw needn't show every extreme that they name: `image_counts`: images of each sample; in every draw all 4 samples of some index of dp hold 5 images and some sample holds 1.
All inputs are finite; a program needn't handle non-finite values.
Results may differ from a plain program's by a relative error of at most 0.014.
Values may be sent and summed in bfloat16 or wider, within the bound.
A program may use at most 192 MiB of HBM per device.

v0:
```python
import jax
import jax.numpy as jnp
from jax import lax
from jax.sharding import PartitionSpec as P

HEAD_DIM = 64
PATCH = 256


EPSILON = 1e-05
NEGATIVE = -1e30
SQRT_HALF = 0.7071067811865476
INV_ROOT_TWO_PI = 0.3989422804014327


def across(left, right):
    return lax.dot_general(
        left, right, (((0,), (0,)), ((), ())), preferred_element_type=jnp.float32
    )


def against(left, right):
    return lax.dot_general(
        left, right, (((left.ndim - 1,), (1,)), ((), ())), preferred_element_type=jnp.float32
    )


def normalize(inputs):
    centre = inputs - jnp.mean(inputs, axis=-1, keepdims=True)
    scale_inv = lax.rsqrt(jnp.mean(centre * centre, axis=-1, keepdims=True) + EPSILON)
    return (centre * scale_inv, scale_inv)


def norm_back(unit, scale_inv, gain, upstream):
    scaled = upstream * gain
    inner_part = scaled - jnp.mean(scaled, axis=-1, keepdims=True)
    inner_part = inner_part - unit * jnp.mean(scaled * unit, axis=-1, keepdims=True)
    return inner_part * scale_inv


def score_table(queries, keys_all, slot_valid, scale_factor):
    raw = (
        jnp.einsum("slhd,skhd->shlk", queries, keys_all, preferred_element_type=jnp.float32)
        * scale_factor
    )
    return jnp.where(slot_valid[:, None, None, :], raw, NEGATIVE)


def on_device(
    media_tokens,
    latents,
    image_counts,
    media_gain,
    media_shift,
    latent_gain,
    latent_shift,
    feed_gain,
    feed_shift,
    query_weight,
    key_weight,
    value_weight,
    output_weight,
    up_weight,
    down_weight,
    cotangent,
):
    samples, slots, width = media_tokens.shape
    latent_rows = latents.shape[1]
    inner = query_weight.shape[1]
    local_heads = inner // HEAD_DIM
    rows = samples * latent_rows
    scale_factor = HEAD_DIM ** (-0.5)
    media_unit, media_scale = normalize(media_tokens.astype(jnp.float32))
    media_normed = (media_unit * media_gain + media_shift).astype(jnp.bfloat16)
    latent_float = latents.astype(jnp.float32)
    latent_unit, latent_scale = normalize(latent_float)
    latent_normed = (latent_unit * latent_gain + latent_shift).astype(jnp.bfloat16)
    context = jnp.concatenate([media_normed, latent_normed], axis=1)
    pair_weight = jnp.concatenate([key_weight, value_weight], axis=1)
    queries = jnp.dot(latent_normed, query_weight, preferred_element_type=jnp.float32).astype(
        jnp.bfloat16
    )
    queries = queries.reshape(samples, latent_rows, local_heads, HEAD_DIM)
    key_value = jnp.dot(context, pair_weight, preferred_element_type=jnp.float32).astype(
        jnp.bfloat16
    )
    keys_all = key_value[..., :inner].reshape(samples, -1, local_heads, HEAD_DIM)
    values_all = key_value[..., inner:].reshape(samples, -1, local_heads, HEAD_DIM)
    slot_ids = jnp.arange(slots + latent_rows)
    slot_valid = (slot_ids[None, :] < image_counts[:, None] * PATCH) | (slot_ids[None, :] >= slots)
    raw = score_table(queries, keys_all, slot_valid, scale_factor)
    largest = jnp.max(raw, axis=-1, keepdims=True)
    log_total = largest + jnp.log(jnp.sum(jnp.exp(raw - largest), axis=-1, keepdims=True))
    probs = jnp.exp(raw - log_total).astype(jnp.bfloat16)
    attended = jnp.einsum("shlk,skhd->slhd", probs, values_all, preferred_element_type=jnp.float32)
    attended = attended.astype(jnp.bfloat16).reshape(samples, latent_rows, inner)
    head_part = jnp.dot(attended, output_weight, preferred_element_type=jnp.float32)
    residual = latent_float + lax.psum(head_part, "tensor")
    up_full, down_full = (
        lax.all_gather(up_weight, "dp", axis=0, tiled=True),
        lax.all_gather(down_weight, "dp", axis=1, tiled=True),
    )
    feed_unit, feed_scale = normalize(residual)
    hidden_in = (feed_unit * feed_gain + feed_shift).astype(jnp.bfloat16)
    before = jnp.dot(hidden_in, up_full, preferred_element_type=jnp.float32)
    activated = jax.nn.gelu(before, approximate=False).astype(jnp.bfloat16)
    feed_part = jnp.dot(activated, down_full, preferred_element_type=jnp.float32)
    new_latents = residual + lax.psum(feed_part.astype(jnp.bfloat16), "tensor").astype(jnp.float32)
    upstream = cotangent.astype(jnp.float32)
    down_grad = across(activated.reshape(rows, -1), cotangent.reshape(rows, width))
    act_grad = against(cotangent, down_full).astype(jnp.bfloat16)
    slope = 0.5 * (1.0 + lax.erf(before * SQRT_HALF)) + before * INV_ROOT_TWO_PI * jnp.exp(
        -0.5 * before * before
    )
    before_grad = (act_grad.astype(jnp.float32) * slope).astype(jnp.bfloat16)
    up_grad = across(hidden_in.reshape(rows, width), before_grad.reshape(rows, -1))
    hidden_grad = lax.psum(against(before_grad, up_full), "tensor")
    residual_grad = upstream + norm_back(feed_unit, feed_scale, feed_gain, hidden_grad)
    feed_gain_grad = jnp.sum(hidden_grad * feed_unit, axis=(0, 1))
    feed_shift_grad = jnp.sum(hidden_grad, axis=(0, 1))
    out_grad = residual_grad.astype(jnp.bfloat16)
    output_grad = across(attended.reshape(rows, inner), out_grad.reshape(rows, width))
    attended_grad = against(out_grad, output_weight).astype(jnp.bfloat16)
    attended_grad = attended_grad.reshape(samples, latent_rows, local_heads, HEAD_DIM)
    raw_again = score_table(queries, keys_all, slot_valid, scale_factor)
    probs_exact = jnp.exp(raw_again - log_total)
    probs_grad = jnp.einsum(
        "slhd,skhd->shlk", attended_grad, values_all, preferred_element_type=jnp.float32
    )
    inner_sum = jnp.sum(probs_grad * probs_exact, axis=-1, keepdims=True)
    score_grad = (probs_exact * (probs_grad - inner_sum)).astype(jnp.bfloat16)
    query_head_grad = jnp.einsum(
        "shlk,skhd->slhd", score_grad, keys_all, preferred_element_type=jnp.float32
    )
    query_head_grad = (
        (query_head_grad * scale_factor).astype(jnp.bfloat16).reshape(samples, latent_rows, inner)
    )
    key_head_grad = jnp.einsum(
        "shlk,slhd->skhd", score_grad, queries, preferred_element_type=jnp.float32
    )
    key_head_grad = (key_head_grad * scale_factor).astype(jnp.bfloat16).reshape(samples, -1, inner)
    value_head_grad = jnp.einsum(
        "shlk,slhd->skhd", probs, attended_grad, preferred_element_type=jnp.float32
    )
    value_head_grad = value_head_grad.astype(jnp.bfloat16).reshape(samples, -1, inner)
    pair_grad = jnp.concatenate([key_head_grad, value_head_grad], axis=2)
    query_grad = across(latent_normed.reshape(rows, width), query_head_grad.reshape(rows, inner))
    pair_weight_grad = across(context.reshape(-1, width), pair_grad.reshape(-1, 2 * inner))
    key_grad = pair_weight_grad[:, :inner]
    value_grad = pair_weight_grad[:, inner:]
    latent_part = against(query_head_grad, query_weight) + against(
        pair_grad[:, slots:], pair_weight
    )
    latent_normed_grad = lax.psum(latent_part, "tensor")
    media_pairs = pair_grad[:, :slots]
    media_normed_grad = lax.psum_scatter(
        against(media_pairs, pair_weight), "tensor", scatter_dimension=1, tiled=True
    )
    share = slots // lax.axis_size("tensor")
    start = lax.axis_index("tensor") * share
    media_share = lax.dynamic_slice_in_dim(media_tokens, start, share, 1).astype(jnp.float32)
    share_unit, share_scale = normalize(media_share)
    media_grad = norm_back(share_unit, share_scale, media_gain, media_normed_grad).astype(
        jnp.bfloat16
    )
    media_gain_part = jnp.sum(media_normed_grad * share_unit, axis=(0, 1))
    media_shift_part = jnp.sum(media_normed_grad, axis=(0, 1))
    media_gain_grad, media_shift_grad = lax.psum(
        (media_gain_part, media_shift_part), ("dp", "tensor")
    )
    latent_grad = residual_grad + norm_back(
        latent_unit, latent_scale, latent_gain, latent_normed_grad
    )
    latent_grad = latent_grad.astype(jnp.bfloat16)
    latent_gain_part = jnp.sum(latent_normed_grad * latent_unit, axis=(0, 1))
    latent_shift_part = jnp.sum(latent_normed_grad, axis=(0, 1))
    reduced = (
        lax.psum_scatter(query_grad, "dp", scatter_dimension=0, tiled=True),
        lax.psum_scatter(key_grad, "dp", scatter_dimension=0, tiled=True),
        lax.psum_scatter(value_grad, "dp", scatter_dimension=0, tiled=True),
        lax.psum_scatter(output_grad, "dp", scatter_dimension=1, tiled=True),
        lax.psum_scatter(up_grad, "dp", scatter_dimension=0, tiled=True),
        lax.psum_scatter(down_grad, "dp", scatter_dimension=1, tiled=True),
        lax.psum_scatter(latent_gain_part, "dp", scatter_dimension=0, tiled=True),
        lax.psum_scatter(latent_shift_part, "dp", scatter_dimension=0, tiled=True),
        lax.psum_scatter(feed_gain_grad, "dp", scatter_dimension=0, tiled=True),
        lax.psum_scatter(feed_shift_grad, "dp", scatter_dimension=0, tiled=True),
    )
    return (
        new_latents.astype(jnp.bfloat16),
        media_grad,
        latent_grad,
        reduced[0],
        reduced[1],
        reduced[2],
        reduced[3],
        reduced[4],
        reduced[5],
        media_gain_grad,
        media_shift_grad,
        reduced[6],
        reduced[7],
        reduced[8],
        reduced[9],
    )


def solution(mesh):
    placed = (
        P("dp", None, None),
        P("dp", None, None),
        P("dp"),
        P(),
        P(),
        P(),
        P(),
        P(),
        P(),
        P(None, "tensor"),
        P(None, "tensor"),
        P(None, "tensor"),
        P("tensor", None),
        P("dp", "tensor"),
        P("tensor", "dp"),
        P("dp", None, None),
    )
    return jax.shard_map(
        on_device,
        mesh=mesh,
        in_specs=placed,
        out_specs=(
            P("dp", None, None),
            P("dp", "tensor", None),
            P("dp", None, None),
            P("dp", "tensor"),
            P("dp", "tensor"),
            P("dp", "tensor"),
            P("tensor", "dp"),
            P("dp", "tensor"),
            P("tensor", "dp"),
            P(),
            P(),
            P("dp"),
            P("dp"),
            P("dp"),
            P("dp"),
        ),
        check_vma=False,
    )
```

profile of v0, /device:TPU:0, one launch (start us, length us, event | category | flops | bytes accessed | tf_op | source)
XLA Modules:
  0.0 896.0 jit_solution(9154847443472154064)
XLA Ops:
  8.8 1.2 convert_reduce_fusion.2
  10.0 1.3 fusion.65
  11.3 5.6 convert_reduce_fusion
  16.9 1.4 copy-done.2
  18.3 3.5 fusion.2
  22.7 7.4 fusion.5
  30.1 4.7 fusion.19
  35.4 1.5 copy.56
  36.9 1.5 copy.55
  38.5 2.1 fusion.99
  42.6 1.3 fusion.81
  45.3 53.3 %all-reduce.11.cloned.1.call-done = f32[4,64,1024]{2,1,0:T(8,128)} async-done(((f32[4,64,1024]{2,1,0:T(8,128)}), f32[4,64,1024]{2,1,0:T(8,128)}) %all-reduce.11.cloned.1.call-update) | async-done | bytes 1048592 | tf_op jit(solution)/shard_map/psum | solution.py:98
  98.6 1.5 fusion.96
  102.0 4.6 fusion.87
  106.9 3.1 fusion.47
  110.8 1.7 fusion.30
  112.6 51.9 %all-reduce.15.cloned.1.call-done = f32[4,64,1024]{2,1,0:T(8,128)} async-done(((f32[4,64,1024]{2,1,0:T(8,128)}), f32[4,64,1024]{2,1,0:T(8,128)}) %all-reduce.15.cloned.1.call-update) | async-done | bytes 1048592 | tf_op jit(solution)/shard_map/psum | solution.py:117
  164.5 2.6 multiply_reduce_fusion.2
  167.1 2.1 fusion.95
  172.0 1.7 convolution_convert_fusion
  176.4 1.6 fusion.21
  178.9 1.9 copy.62
  180.8 1.3 fusion.83
  182.1 1.3 convolution_add_fusion
  183.5 3.4 fusion.68
  187.7 3.2 fusion.35
  191.0 8.7 fusion.23
  202.5 2.1 fusion.101
  204.9 5.8 fusion.34
  212.9 1.2 fusion.100
  214.2 2.8 convolution_bitcast_fusion.1
  218.3 2.7 convolution_bitcast_fusion
  223.0 2.3 convert_reduce_fusion.1
  225.2 2.6 fusion.18
  227.9 7.0 all-reduce.17.cloned.1.call-done
  234.8 1.7 fusion.64
  236.6 25.0 %all-reduce.5 = (f32[1024]{0:T(1024)S(1)}, f32[1024]{0:T(1024)S(1)}, f32[1024]{0:T(1024)S(1)}, f32[1024]{0:T(1024)S(1)}) all-reduce(f32[1024]{0:T(1024)S(1)} %get-tuple-element.21, f32[1024]{0:T(1024)S(1)} %get-tuple-element.26, f32[1024]{0:T(1024)S(1)} %copy-done.42, ...), channel_id=9, replica_groups=mesh['dp'=8,'tensor'=4] {'dp'}, use_global_device_ids=true, to_apply=%region_33.34.clone | all-reduce | flops 4096 | bytes 32768
  263.9 11.5 %all-reduce.13.cloned.1.call-done = bf16[4,64,1024]{2,1,0:T(8,128)(2,1)} async-done(((bf16[4,64,1024]{2,1,0:T(8,128)(2,1)}), bf16[4,64,1024]{2,1,0:T(8,128)(2,1)}) %all-reduce.13.cloned.1.call-update) | async-done | bytes 524304 | tf_op jit(solution)/shard_map/psum | solution.py:108
  275.4 3.0 fusion.63
  278.4 346.5 %reduce-scatter.8.cloned.1.call-done = f32[4,320,1024]{2,1,0:T(8,128)} async-done(((f32[4,1280,1024]{2,1,0:T(8,128)}), f32[4,320,1024]{2,1,0:T(8,128)}) %reduce-scatter.8.cloned.1.call-update) | async-done | bytes 5242896 | tf_op jit(solution)/shard_map/reduce_scatter | solution.py:156
  625.0 4.8 fusion.17
  629.8 41.8 %all-reduce.4 = (f32[1024]{0:T(1024)}, f32[1024]{0:T(1024)}) all-reduce(f32[1024]{0:T(1024)S(1)} %get-tuple-element.15, f32[1024]{0:T(1024)S(1)} %get-tuple-element.18), channel_id=1, replica_groups=mesh['dp'=8,'tensor'=4] {'dp','tensor'}, use_global_device_ids=true, to_apply=%region_29.30 | all-reduce | flops 2048 | bytes 16384 | tf_op jit(solution)/shard_map/psum | solution.py:168
  671.6 5.3 fusion.16
  676.9 25.3 %reduce-scatter.14.cloned.1.call-done = f32[128,128]{1,0:T(8,128)} async-done(((f32[1024,128]{1,0:T(8,128)}), f32[128,128]{1,0:T(8,128)}) %reduce-scatter.14.cloned.1.call-update) | async-done | bytes 65552 | tf_op jit(solution)/shard_map/reduce_scatter | solution.py:180
  702.2 37.8 %reduce-scatter.12.cloned.1.call-done = f32[128,128]{1,0:T(8,128)} async-done(((f32[1024,128]{1,0:T(8,128)}), f32[128,128]{1,0:T(8,128)}) %reduce-scatter.12.cloned.1.call-update) | async-done | bytes 65552 | tf_op jit(solution)/shard_map/reduce_scatter | solution.py:179
  740.0 38.1 %reduce-scatter.10.cloned.1.call-done = f32[128,128]{1,0:T(8,128)} async-done(((f32[1024,128]{1,0:T(8,128)}), f32[128,128]{1,0:T(8,128)}) %reduce-scatter.10.cloned.1.call-update) | async-done | bytes 65552 | tf_op jit(solution)/shard_map/reduce_scatter | solution.py:178
  778.1 55.1 %reduce-scatter.18.cloned.1.call-done = f32[128,1024]{1,0:T(8,128)} async-done(((f32[1024,1024]{1,0:T(8,128)}), f32[128,1024]{1,0:T(8,128)}) %reduce-scatter.18.cloned.1.call-update) | async-done | bytes 524304 | tf_op jit(solution)/shard_map/reduce_scatter | solution.py:182
  833.2 55.7 %reduce-scatter.20.cloned.1.call-done = f32[1024,128]{1,0:T(8,128)} async-done(((f32[1024,1024]{1,0:T(8,128)}), f32[1024,128]{1,0:T(8,128)}) %reduce-scatter.20.cloned.1.call-update) | async-done | bytes 524304 | tf_op jit(solution)/shard_map/reduce_scatter | solution.py:183
  (164 shorter events, 25.5 us)
Async XLA Ops:
  8.0 34.6 %copy-start = (bf16[128,1024]{1,0:T(8,128)(2,1)S(1)}, bf16[128,1024]{1,0:T(8,128)(2,1)}, u32[]{:S(2)}) copy-start(bf16[128,1024]{1,0:T(8,128)(2,1)} %param.28) | copy-start | bytes 786436
  8.0 90.6 %all-reduce.11.cloned.1.call-start = ((), (), s32[]{:S(2)}) async-start(), calls=%async_computation.7 | async-start | bytes 2097152 | tf_op jit(solution)/shard_map/psum | solution.py:98
  11.3 10.5 %copy-start.34 = (f32[4,64]{1,0:T(4,128)}, f32[4,64]{1,0:T(4,128)S(1)}, u32[]{:S(2)}) copy-start(f32[4,64]{1,0:T(4,128)S(1)} %add_rsqrt_fusion.3) | copy-start | bytes 3076
  11.3 7.0 copy-start.2
  18.3 3.6 copy-start.5
  18.3 3.6 copy-start.31
  18.3 3.6 copy-start.44
  18.3 3.9 copy-start.23
  18.3 4.3 copy-start.30
  18.3 4.3 copy-start.45
  22.2 7.9 copy-start.13
  22.6 7.4 copy-start.20
  22.7 7.4 copy-start.21
  30.1 4.7 copy-start.10
  38.5 2.7 copy-start.7
  43.9 58.0 %all-gather.3.cloned.1.call-start = ((), (), s32[]{:S(2)}) async-start(), calls=%async_computation.8 | async-start | bytes 2359296 | tf_op jit(solution)/shard_map/all_gather | solution.py:100
  44.5 62.3 %all-gather.5.cloned.1.call-start = ((), (), s32[]{:S(2)}) async-start(), calls=%async_computation.9 | async-start | bytes 2359296 | tf_op jit(solution)/shard_map/all_gather | solution.py:101
  45.1 119.4 %all-reduce.15.cloned.1.call-start = ((), (), s32[]{:S(2)}) async-start(), calls=%async_computation.11 | async-start | bytes 2097152 | tf_op jit(solution)/shard_map/psum | solution.py:117
  106.9 3.9 copy-start.16
  112.6 122.3 %all-reduce.17.cloned.1.call-start = ((), (), s32[]{:S(2)}) async-start(), calls=%async_computation.13 | async-start | bytes 2097152 | tf_op jit(solution)/shard_map/psum | solution.py:154
  167.1 2.1 copy-start.38
  167.1 2.1 copy-start.40
  175.9 2.2 copy-start.12
  178.9 3.2 copy-start.22
  183.5 91.9 %all-reduce.13.cloned.1.call-start = ((), (), s32[]{:S(2)}) async-start(), calls=%async_computation.10 | async-start | bytes 1048576 | tf_op jit(solution)/shard_map/psum | solution.py:108
  190.9 434.0 %reduce-scatter.8.cloned.1.call-start = ((), (), s32[]{:S(2)}) async-start(), calls=%async_computation.12 | async-start | bytes 26214400 | tf_op jit(solution)/shard_map/reduce_scatter | solution.py:156
  199.8 5.1 copy-start.14
  199.8 477.1 %reduce-scatter.16.cloned.1.call-start = ((), (), s32[]{:S(2)}) async-start(), calls=%async_computation.17 | async-start | bytes 589824 | tf_op jit(solution)/shard_map/reduce_scatter | solution.py:181
  204.6 497.6 %reduce-scatter.14.cloned.1.call-start = ((), (), s32[]{:S(2)}) async-start(), calls=%async_computation.16 | async-start | bytes 589824 | tf_op jit(solution)/shard_map/reduce_scatter | solution.py:180
  210.7 3.5 copy-start.4
  210.8 3.5 copy-start.25
  210.8 3.4 copy-start.33
  210.8 3.4 copy-start.36
  210.8 3.4 copy-start.46
  211.9 528.1 %reduce-scatter.12.cloned.1.call-start = ((), (), s32[]{:S(2)}) async-start(), calls=%async_computation.15 | async-start | bytes 589824 | tf_op jit(solution)/shard_map/reduce_scatter | solution.py:179
  212.6 565.5 %reduce-scatter.10.cloned.1.call-start = ((), (), s32[]{:S(2)}) async-start(), calls=%async_computation.14 | async-start | bytes 589824 | tf_op jit(solution)/shard_map/reduce_scatter | solution.py:178
  214.1 619.1 %reduce-scatter.18.cloned.1.call-start = ((), (), s32[]{:S(2)}) async-start(), calls=%async_computation.18 | async-start | bytes 4718592 | tf_op jit(solution)/shard_map/reduce_scatter | solution.py:182
  217.1 671.8 %reduce-scatter.20.cloned.1.call-start = ((), (), s32[]{:S(2)}) async-start(), calls=%async_computation.19 | async-start | bytes 4718592 | tf_op jit(solution)/shard_map/reduce_scatter | solution.py:183
  221.0 13.8 %copy-start.6 = (bf16[4,64,1024]{2,1,0:T(8,128)(2,1)S(1)}, bf16[4,64,1024]{2,1,0:T(8,128)(2,1)}, u32[]{:S(2)}) copy-start(bf16[4,64,1024]{2,1,0:T(8,128)(2,1)} %param.17) | copy-start | bytes 1572868
  221.0 13.8 %copy-start.32 = (f32[1024]{0:T(1024)S(1)}, f32[1024]{0:T(1024)}, u32[]{:S(2)}) copy-start(f32[1024]{0:T(1024)} %param.21) | copy-start | bytes 12292
  221.1 13.8 %copy-start.35 = (f32[4,64]{1,0:T(4,128)S(1)}, f32[4,64]{1,0:T(4,128)}, u32[]{:S(2)}) copy-start(f32[4,64]{1,0:T(4,128)} %copy-done.34) | copy-start | bytes 3076
  222.9 13.7 %copy-start.42 = (f32[1024]{0:T(1024)S(1)}, f32[1024]{0:T(1024)}, u32[]{:S(2)}) copy-start(f32[1024]{0:T(1024)} %get-tuple-element.19) | copy-start | bytes 12292
  222.9 13.7 %copy-start.43 = (f32[1024]{0:T(1024)S(1)}, f32[1024]{0:T(1024)}, u32[]{:S(2)}) copy-start(f32[1024]{0:T(1024)} %get-tuple-element.25) | copy-start | bytes 12292
  222.9 52.5 %copy-start.11 = (f32[4,64,1024]{2,1,0:T(8,128)S(1)}, f32[4,64,1024]{2,1,0:T(8,128)}, u32[]{:S(2)}) copy-start(f32[4,64,1024]{2,1,0:T(8,128)} %all-reduce.15.cloned.1.call-done) | copy-start | bytes 3145732
  222.9 52.5 %copy-start.37 = (f32[4,64]{1,0:T(4,128)S(1)}, f32[4,64]{1,0:T(4,128)}, u32[]{:S(2)}) copy-start(f32[4,64]{1,0:T(4,128)} %add_rsqrt_fusion.2) | copy-start | bytes 3076
  222.9 52.5 %copy-start.39 = (f32[4,64]{1,0:T(4,128)S(1)}, f32[4,64]{1,0:T(4,128)}, u32[]{:S(2)}) copy-start(f32[4,64]{1,0:T(4,128)} %copy-done.38) | copy-start | bytes 3076
  223.0 52.4 %copy-start.41 = (f32[4,64]{1,0:T(4,128)S(1)}, f32[4,64]{1,0:T(4,128)}, u32[]{:S(2)}) copy-start(f32[4,64]{1,0:T(4,128)} %copy-done.40) | copy-start | bytes 3076
  671.6 217.4 %copy-start.1 = (bf16[128,1024]{1,0:T(8,128)(2,1)S(1)}, bf16[128,1024]{1,0:T(8,128)(2,1)}, u32[]{:S(2)}) copy-start(bf16[128,1024]{1,0:T(8,128)(2,1)} %param.28) | copy-start | bytes 786436
  (13 other events, 13.7 us)
Sparse Core Ops, SparseCore 0:
  44.1 54.5 all-reduce.10
  112.7 51.7 all-reduce.14
  183.6 51.1 all-reduce.16
  237.7 37.6 all-reduce.12
  277.7 347.1 reduce-scatter.7
  628.5 35.5 reduce-scatter.15
  668.0 34.1 reduce-scatter.13
  705.8 34.1 reduce-scatter.11
  743.9 34.1 reduce-scatter.9
  781.9 51.3 reduce-scatter.17
  837.6 51.3 reduce-scatter.19
Sparse Core Ops, SparseCore 1:
  46.5 30.4 all-gather.2
  78.8 28.0 all-gather.4
where the time goes:
time: 897 us; the launch traced here: 896 us
  waiting for transfers between devices  684 us (76%)
  blocking collectives  66.8 us (7%)
  matrix products  53.5 us (6%)
  other arithmetic  51.6 us (6%)
  local copies, waits for them, and re-layouts  22.2 us (2%)
  between operations  16.7 us (2%)
    reduce_scatter x1, waiting for transfers between devices, on_device(): lax.psum_scatter(against(media_pairs, pair_weight), 'tensor', scatter_dim...  347 us
    reduce_scatter x1, waiting for transfers between devices, on_device(): lax.psum_scatter(down_grad, 'dp', scatter_dimension=1, tiled=True)  55.7 us
    reduce_scatter x1, waiting for transfers between devices, on_device(): lax.psum_scatter(up_grad, 'dp', scatter_dimension=0, tiled=True)  55.1 us
    psum x1, waiting for transfers between devices, on_device(): residual = latent_float + lax.psum(head_part, 'tensor')  53.3 us
    psum x1, waiting for transfers between devices, on_device(): hidden_grad = lax.psum(against(before_grad, up_full), 'tensor')  51.9 us
    psum x1, blocking collectives, on_device(): lax.psum((media_gain_part, media_shift_part), ('dp', 'tensor'))  41.8 us
    reduce_scatter x1, waiting for transfers between devices, on_device(): lax.psum_scatter(query_grad, 'dp', scatter_dimension=0, tiled=True)  38.1 us
    reduce_scatter x1, waiting for transfers between devices, on_device(): lax.psum_scatter(key_grad, 'dp', scatter_dimension=0, tiled=True)  37.8 us
  transfers between devices with their start and end apart: 13, of which 11 were waited for; matrix products, arithmetic and copies ran while one was open for 7% of the time, Pallas kernels for 0%

commit v1 on v0

v1 whole, which is shorter than its diff:
```python
import functools

import jax
import jax.numpy as jnp
from jax import lax
from jax.experimental import pallas as pl
from jax.experimental.pallas import tpu as pltpu
from jax.sharding import PartitionSpec as P

HEAD_DIM = 64
PATCH = 256
EPSILON = 1e-05
NEGATIVE = -1e30
SQRT_HALF = 0.7071067811865476
INV_ROOT_TWO_PI = 0.3989422804014327
F32 = jnp.float32
BF16 = jnp.bfloat16
MESH = pl.DeviceIdType.MESH
BLOCK = 256
ROWS = 32
SLOTS_IN_FLIGHT = 3


def nn(left, right):
    return lax.dot_general(left, right, (((1,), (0,)), ((), ())), preferred_element_type=F32)


def nt(left, right):
    return lax.dot_general(left, right, (((1,), (1,)), ((), ())), preferred_element_type=F32)


def tn(left, right):
    return lax.dot_general(left, right, (((0,), (0,)), ((), ())), preferred_element_type=F32)


def unit_rows(x):
    centre = x - jnp.mean(x, axis=-1, keepdims=True)
    scale_inv = lax.rsqrt(jnp.mean(centre * centre, axis=-1, keepdims=True) + EPSILON)
    return centre * scale_inv, scale_inv


def norm_back(unit, scale_inv, gain, upstream):
    scaled = upstream * gain
    inner = scaled - jnp.mean(scaled, axis=-1, keepdims=True)
    inner = inner - unit * jnp.mean(scaled * unit, axis=-1, keepdims=True)
    return inner * scale_inv


def fold(x):
    return jnp.sum(x.reshape(x.shape[0] // 8, 8, x.shape[1]), axis=0)


class Sizes:
    def __init__(self, tensor, dp, samples, lat, slots, width, hidden, inner):
        self.T, self.N, self.C = tensor, dp, dp // 2
        self.S, self.L, self.M, self.D = samples, lat, slots, width
        self.F, self.I = hidden, inner
        self.R = width // dp
        self.Lt, self.Mt = lat // tensor, slots // tensor
        self.Kt = self.Lt + self.Mt
        self.K = lat + slots
        self.H = inner // HEAD_DIM
        self.q = self.H * lat


def layer_kernel(
    z,
    counts,
    media,
    lat,
    cot,
    mgain,
    mshift,
    lgain,
    lshift,
    fgain,
    fshift,
    wqkv,
    wo,
    up,
    dn,
    new_lat,
    media_grad,
    lat_grad,
    g_qkv,
    g_o,
    g_up,
    g_dn,
    g_vec,
    wq_b,
    wo_b,
    up_b,
    dn_b,
    mbuf,
    mown,
    xn,
    kvown,
    ctx,
    latn,
    att,
    lse,
    qall,
    kvall,
    pall,
    dkv,
    res,
    hin,
    act,
    bgr,
    hg,
    hgr,
    fp,
    fpr,
    og,
    rgr,
    dob,
    dqb,
    dqr,
    st_up,
    st_dn,
    st_o,
    st_qkv,
    cr_up,
    cr_dn,
    cr_o,
    cr_qkv,
    xr_up,
    xr_dn,
    xr_o,
    xr_qkv,
    zr_o,
    zr_qkv,
    mg,
    mgl,
    acc,
    vst,
    vcr,
    vx,
    vz,
    msem,
    osem,
    zs,
    zr,
    xs,
    xr,
    cs,
    cr,
):
    T, N, C, S, L, M, D = z.T, z.N, z.C, z.S, z.L, z.M, z.D
    F, I, R, Lt, Mt, Kt, H = z.F, z.I, z.R, z.Lt, z.Mt, z.Kt, z.H
    scale_factor = HEAD_DIM ** (-0.5)
    t = lax.axis_index("tensor")
    d = lax.axis_index("dp")
    c = lax.div(d, 2)
    core = lax.rem(d, 2)
    other = 1 - core
    sib = d + 1 - 2 * core
    n = BLOCK // (2 * R)

    def z_dev(k):
        return (d, lax.rem(t + k, T))

    def x_chip(j):
        return lax.rem(c + j, C)

    def x_dev(j):
        return (2 * x_chip(j) + core, t)

    core_dev = (sib, t)

    def head(k):
        return lax.rem(t - k + T, T)

    def my_rows(k=0):
        return pl.ds(pl.multiple_of(lax.rem(t + k, T) * Lt, Lt), Lt)

    def remote(src, dst, send, recv, dev):
        return pltpu.make_async_remote_copy(
            src_ref=src, dst_ref=dst, send_sem=send, recv_sem=recv, device_id=dev, device_id_type=MESH
        )

    def over_chips(body):
        lax.fori_loop(1, C, lambda j, carry: (body(j), carry)[1], 0)

    def gather_z(i, src, buf):
        return [
            remote(src.at[c, core], buf.at[k, c, core], zs.at[i, k - 1], zr.at[i, k - 1], z_dev(k))
            for k in range(1, T)
        ]

    def gather_x(i, src, dst):
        def one(j):
            return remote(src, dst, xs.at[i, j - 1], xr.at[i, j - 1], x_dev(j))

        return one

    wo_z = gather_z(0, wo, wo_b)
    wq_z = gather_z(1, wqkv, wq_b)
    wo_x = gather_x(0, wo_b.at[pl.ds(1, T - 1), c, core], wo_b.at[pl.ds(1, T - 1), c, core])
    wq_x = gather_x(1, wq_b.at[pl.ds(1, T - 1), c, core], wq_b.at[pl.ds(1, T - 1), c, core])
    up_x = gather_x(2, up, up_b.at[c, core])
    dn_x = gather_x(3, dn, dn_b.at[c, core])

    def relay(i, ref):
        return remote(ref, ref, cs.at[i], cr.at[i], core_dev)

    wo_c = relay(0, wo_b.at[pl.ds(1, T - 1), :, core])
    wq_c = relay(1, wq_b.at[pl.ds(1, T - 1), :, core])
    up_c = relay(2, up_b.at[:, core])
    dn_c = relay(3, dn_b.at[:, core])

    n_tiles = S * T

    def tile_copy(i):
        slot = lax.rem(i, SLOTS_IN_FLIGHT)
        s, r = lax.div(i, T), lax.rem(i, T)
        return pltpu.make_async_copy(
            media.at[s, pl.ds(pl.multiple_of(r * Mt, Mt), Mt)], mbuf.at[slot], msem.at[slot]
        )

    own_copy = pltpu.make_async_copy(
        media.at[:, pl.ds(pl.multiple_of(t * Mt, Mt), Mt)], mown, msem.at[SLOTS_IN_FLIGHT]
    )
    for i in range(min(SLOTS_IN_FLIGHT, n_tiles)):
        tile_copy(i).start()
    own_copy.start()

    barrier = pltpu.get_barrier_semaphore()

    def greet(dev):
        pl.semaphore_signal(barrier, inc=1, device_id=dev, device_id_type=MESH)

    for k in range(1, T):
        greet(z_dev(k))
    over_chips(lambda j: greet(x_dev(j)))
    greet(core_dev)
    pl.semaphore_wait(barrier, T + C - 1)

    for copy in wo_z + wq_z:
        copy.start()
    over_chips(lambda j: up_x(j).start())
    over_chips(lambda j: dn_x(j).start())
    wo_b[0] = wo[...]
    wq_b[0] = wqkv[...]
    up_b[c, core] = up[...]
    dn_b[c, core] = dn[...]

    def lat_norm(b, carry):
        rows = pl.ds(pl.multiple_of(b * ROWS, ROWS), ROWS)
        unit, _ = unit_rows(lat[rows, :].astype(F32))
        latn[rows, :] = (unit * lgain[...] + lshift[...]).astype(BF16)
        return carry

    lax.fori_loop(0, S * L // ROWS, lat_norm, 0)
    own_w = wq_b[0].reshape(D, 3 * I)
    own_qkv = nn(latn[...], own_w).astype(BF16)
    qall[0] = own_qkv[:, :I]
    for s in range(S):
        kvown[s, pl.ds(M, L), :] = own_qkv[s * L : (s + 1) * L, I:]
        ctx[pl.ds(s * Kt + Mt, Lt), :] = latn[pl.ds(pl.multiple_of(s * L + t * Lt, Lt), Lt), :]

    def media_tile(i, carry):
        slot = lax.rem(i, SLOTS_IN_FLIGHT)
        s, r = lax.div(i, T), lax.rem(i, T)
        tile_copy(i).wait()

        def rows_norm(b, inner):
            rows = pl.ds(pl.multiple_of(b * ROWS, ROWS), ROWS)
            unit, _ = unit_rows(mbuf[slot, rows, :].astype(F32))
            xn[rows, :] = (unit * mgain[...] + mshift[...]).astype(BF16)
            return inner

        lax.fori_loop(0, Mt // ROWS, rows_norm, 0)

        @pl.when(i + SLOTS_IN_FLIGHT < n_tiles)
        def _():
            tile_copy(i + SLOTS_IN_FLIGHT).start()

        pair = nn(xn[...], wq_b[0].reshape(D, 3 * I)[:, I:])
        kvown[s, pl.ds(pl.multiple_of(r * Mt, Mt), Mt), :] = pair.astype(BF16)

        @pl.when(r == t)
        def _():
            ctx[pl.ds(pl.multiple_of(s * Kt, 16), Mt), :] = xn[...]

        @pl.when(i == n_tiles // 4)
        def _():
            for copy in wo_z:
                copy.wait_recv()
            over_chips(lambda j: wo_x(j).start())

        @pl.when(i == n_tiles // 2)
        def _():
            for copy in wq_z:
                copy.wait_recv()
            over_chips(lambda j: wq_x(j).start())

        return carry

    lax.fori_loop(0, n_tiles, media_tile, 0)

    lane_head = lax.broadcasted_iota(jnp.int32, (1, I), 1) // HEAD_DIM

    def spread(x):
        zero = jnp.zeros_like(x)
        return jnp.concatenate([jnp.where(lane_head == h, x, zero) for h in range(H)], axis=0)

    def gather_heads(x):
        out = x[:L]
        for h in range(1, H):
            out = jnp.where(lane_head == h, x[h * L : (h + 1) * L], out)
        return out

    def attend(s, carry):
        keys = kvown[s, :, pl.ds(0, I)]
        values = kvown[s, :, pl.ds(I, I)]
        queries = qall[0, pl.ds(pl.multiple_of(s * L, L), L), :]
        scores = nt(keys, spread(queries)) * scale_factor
        slot = lax.broadcasted_iota(jnp.int32, (z.K, 1), 0)
        valid = (slot < counts[s] * PATCH) | (slot >= M)
        scores = jnp.where(valid, scores, NEGATIVE)
        largest = jnp.max(scores, axis=0, keepdims=True)
        total = largest + jnp.log(jnp.sum(jnp.exp(scores - largest), axis=0, keepdims=True))
        probs = jnp.exp(scores - total).astype(BF16)
        att[0, s] = gather_heads(tn(probs, values)).astype(BF16)
        lse[0, pl.ds(s, 1), :] = total
        return carry

    lax.fori_loop(0, S, attend, 0)

    att_z = [remote(att.at[0], att.at[k], zs.at[2, k - 1], zr.at[2, k - 1], z_dev(k)) for k in range(1, T)]
    lse_z = [remote(lse.at[0], lse.at[k], zs.at[3, k - 1], zr.at[3, k - 1], z_dev(k)) for k in range(1, T)]
    for copy in att_z + lse_z:
        copy.start()

    over_chips(lambda j: wo_x(j).wait_recv())
    wo_c.start()
    over_chips(lambda j: up_x(j).wait_recv())
    up_c.start()
    over_chips(lambda j: dn_x(j).wait_recv())
    dn_c.start()

    wo_c.wait_recv()
    for copy in att_z:
        copy.wait_recv()

    def mat(ref, k, width):
        return ref[k].reshape(D, width)

    part = lat[...].astype(F32)
    for k in range(T):
        part = part + nt(att[k].reshape(S * L, I), mat(wo_b, k, I))
    res[...] = part

    def feed_norm(b, carry):
        rows = pl.ds(pl.multiple_of(b * ROWS, ROWS), ROWS)
        unit, _ = unit_rows(res[rows, :])
        hin[rows, :] = (unit * fgain[...] + fshift[...]).astype(BF16)
        return carry

    lax.fori_loop(0, S * L // ROWS, feed_norm, 0)

    up_c.wait_recv()
    dn_c.wait_recv()

    def feed(b, carry):
        cols = pl.ds(pl.multiple_of(b * BLOCK, BLOCK), BLOCK)
        before = nn(hin[...], up_b[:, :, :, cols].reshape(D, BLOCK))
        cdf = 0.5 * (1.0 + lax.erf(before * SQRT_HALF))
        act[:, cols] = (before * cdf).astype(BF16)
        slope = cdf + before * INV_ROOT_TWO_PI * jnp.exp(-0.5 * before * before)
        act_grad = nn(cot[...], dn_b[:, :, :, cols].reshape(D, BLOCK)).astype(BF16)
        bgr[:, cols] = (act_grad.astype(F32) * slope).astype(BF16)
        return carry

    lax.fori_loop(0, F // BLOCK, feed, 0)

    def back_to_width(left, weight, out):
        def one(b, carry):
            cols = pl.ds(pl.multiple_of(b * BLOCK, BLOCK), BLOCK)
            block = nt(left[...], weight[pl.ds(b * n, n)].reshape(BLOCK, F))
            out[:, :, cols] = block.astype(BF16).reshape(S, L, BLOCK)
            return carry

        lax.fori_loop(0, D // BLOCK, one, 0)

    back_to_width(bgr, up_b, hg)
    hg_z = [
        remote(hg.at[:, my_rows(k)], hgr.at[k - 1], zs.at[4, k - 1], zr.at[4, k - 1], z_dev(k)) for k in range(1, T)
    ]
    for copy in hg_z:
        copy.start()
    back_to_width(act, dn_b, fp)
    fp_z = [
        remote(fp.at[:, my_rows(k)], fpr.at[k - 1], zs.at[5, k - 1], zr.at[5, k - 1], z_dev(k)) for k in range(1, T)
    ]
    for copy in fp_z:
        copy.start()

    def feed_weights(left, right, out):
        def one(b, carry):
            cols = pl.ds(pl.multiple_of(b * BLOCK, BLOCK), BLOCK)
            block = tn(left[:, cols], right[...]).astype(BF16)
            out[pl.ds(b * n, n)] = block.reshape(n, 2, R, F)
            return carry

        lax.fori_loop(0, D // BLOCK, one, 0)

    def to_core(i, src, dst):
        return remote(src, dst, cs.at[i], cr.at[i], core_dev)

    feed_weights(hin, bgr, st_up)
    st_up_c = to_core(4, st_up.at[:, other], cr_up)
    st_up_c.start()
    feed_weights(cot, act, st_dn)
    st_dn_c = to_core(5, st_dn.at[:, other], cr_dn)
    st_dn_c.start()

    over_chips(lambda j: wq_x(j).wait_recv())
    wq_c.start()

    own_copy.wait()
    wq_c.wait_recv()

    def all_queries(k, carry):
        qall[k] = nn(latn[...], wq_b[k, :, :, :, pl.ds(0, I)].reshape(D, I)).astype(BF16)
        return carry

    lax.fori_loop(1, T, all_queries, 0)

    def all_pairs(i, carry):
        k, s = lax.div(i, S), lax.rem(i, S)
        rows = pl.ds(pl.multiple_of(s * Kt, 16), Kt)
        pair = nn(ctx[rows, :], wq_b[k, :, :, :, pl.ds(I, 2 * I)].reshape(D, 2 * I))
        kvall[k, rows, :] = pair.astype(BF16)
        return carry

    lax.fori_loop(0, T * S, all_pairs, 0)
    for copy in lse_z:
        copy.wait_recv()
    slot_of = lax.broadcasted_iota(jnp.int32, (Kt, 1), 0)

    def probabilities(i, carry):
        k, s = lax.div(i, S), lax.rem(i, S)
        rows = pl.ds(pl.multiple_of(s * Kt, 16), Kt)
        queries = qall[k, pl.ds(pl.multiple_of(s * L, L), L), :]
        scores = nt(kvall[k, rows, pl.ds(0, I)], spread(queries)) * scale_factor
        valid = (slot_of + t * Mt < counts[s] * PATCH) | (slot_of >= Mt)
        scores = jnp.where(valid, scores, NEGATIVE)
        pall[i] = jnp.exp(scores - lse[k, pl.ds(s, 1), :])
        return carry

    lax.fori_loop(0, T * S, probabilities, 0)

    for copy in hg_z:
        copy.wait_recv()
    feed_gain_part = jnp.zeros((1, D), F32)
    feed_shift_part = jnp.zeros((1, D), F32)
    for s in range(S):
        own = pl.ds(pl.multiple_of(s * L + t * Lt, Lt), Lt)
        unit, scale_inv = unit_rows(res[own, :])
        upstream = hg[s, my_rows(), :].astype(F32)
        for k in range(1, T):
            upstream = upstream + hgr[k - 1, s].astype(F32)
        back = cot[own, :].astype(F32) + norm_back(unit, scale_inv, fgain[...], upstream)
        feed_gain_part = feed_gain_part + jnp.sum(upstream * unit, axis=0, keepdims=True)
        feed_shift_part = feed_shift_part + jnp.sum(upstream, axis=0, keepdims=True)
        rgr[pl.ds(s * Lt, Lt), :] = back
        og[pl.ds(s * Lt, Lt), :] = back.astype(BF16)
    for k in range(T):
        grads = nn(og[...], mat(wo_b, k, I)).astype(BF16)
        dob[head(k), :, my_rows(), :] = grads.reshape(S, Lt, I)
    do_z = [
        remote(
            dob.at[:, :, my_rows(), :], dob.at[:, :, my_rows(), :], zs.at[6, k - 1], zr.at[6, k - 1], z_dev(k)
        )
        for k in range(1, T)
    ]
    do_in = [
        remote(
            dob.at[:, :, my_rows(T - k), :],
            dob.at[:, :, my_rows(T - k), :],
            zs.at[6, k - 1],
            zr.at[6, k - 1],
            z_dev(k),
        )
        for k in range(1, T)
    ]
    for copy in do_z:
        copy.start()

    for k in range(T):
        mine = att[k, :, my_rows(), :].reshape(S * Lt, I)

        def out_weights(b, carry, k=k, mine=mine):
            cols = pl.ds(pl.multiple_of(b * BLOCK, BLOCK), BLOCK)
            block = tn(og[:, cols], mine).astype(BF16)
            st_o[k, pl.ds(b * n, n)] = block.reshape(n, 2, R, I)
            return carry

        lax.fori_loop(0, D // BLOCK, out_weights, 0)
    st_o_c = to_core(6, st_o.at[:, :, other], cr_o)
    st_o_c.start()

    def plane_feed(i, arrive, st, came, land):
        arrive.wait_recv()

        def add(chip):
            st[chip, core] = (st[chip, core].astype(F32) + came[chip].astype(F32)).astype(BF16)

        def copy(j):
            return remote(st.at[x_chip(j), core], land.at[j - 1], xs.at[i, j - 1], xr.at[i, j - 1], x_dev(j))

        def one(j):
            add(x_chip(j))
            copy(j).start()

        over_chips(one)
        add(c)
        return copy

    def plane_heads(i, arrive, st, came, land):
        arrive.wait_recv()

        def add(chip):
            for k in range(T):
                st[k, chip, core] = (st[k, chip, core].astype(F32) + came[k, chip].astype(F32)).astype(BF16)

        def copy(j):
            return remote(st.at[:, x_chip(j), core], land.at[j - 1], xs.at[i, j - 1], xr.at[i, j - 1], x_dev(j))

        def one(j):
            add(x_chip(j))
            copy(j).start()

        over_chips(one)
        add(c)
        return copy

    x_up = plane_feed(4, st_up_c, st_up, cr_up, xr_up)
    x_dn = plane_feed(5, st_dn_c, st_dn, cr_dn, xr_dn)

    for copy in do_in:
        copy.wait_recv()

    def attend_back(i, carry):
        k, s = lax.div(i, S), lax.rem(i, S)
        rows = pl.ds(pl.multiple_of(s * Kt, 16), Kt)
        lanes = pl.multiple_of(k * 2 * I, 2 * I)
        keys = kvall[k, rows, pl.ds(0, I)]
        values = kvall[k, rows, pl.ds(I, I)]
        queries = spread(qall[k, pl.ds(pl.multiple_of(s * L, L), L), :])
        grads = spread(dob[head(k), s])
        outs = spread(att[k, s])
        product = grads.astype(F32) * outs.astype(F32)
        inner = lax.dot_general(
            jnp.ones((8, I), F32),
            product,
            (((1,), (1,)), ((), ())),
            preferred_element_type=F32,
            precision=lax.Precision.HIGHEST,
        )[:1]
        probs = pall[i]
        score_grad = (probs * (nt(values, grads) - inner)).astype(BF16)
        dkv[rows, pl.ds(lanes, I)] = (nn(score_grad, queries) * scale_factor).astype(BF16)
        dkv[rows, pl.ds(lanes + I, I)] = nn(probs.astype(BF16), grads).astype(BF16)
        dqb[head(k), s] = (gather_heads(tn(score_grad, keys)) * scale_factor).astype(BF16)
        return carry

    lax.fori_loop(0, T * S, attend_back, 0)
    dq_z = [
        remote(
            dqb.at[:, :, my_rows(k), :], dqr.at[k - 1], zs.at[7, k - 1], zr.at[7, k - 1], z_dev(k)
        )
        for k in range(1, T)
    ]
    for copy in dq_z:
        copy.start()

    def pair_weights(b, carry):
        cols = pl.ds(pl.multiple_of(b * BLOCK, BLOCK), BLOCK)
        block = tn(ctx[:, cols], dkv[...]).astype(BF16)
        for k in range(T):
            st_qkv[k, pl.ds(b * n, n), :, :, pl.ds(I, 2 * I)] = block[:, k * 2 * I : (k + 1) * 2 * I].reshape(
                n, 2, R, 2 * I
            )
        return carry

    lax.fori_loop(0, D // BLOCK, pair_weights, 0)
    for k in range(T):
        mine = dqb[head(k)].reshape(S * L, I)

        def query_weights(b, carry, k=k, mine=mine):
            cols = pl.ds(pl.multiple_of(b * BLOCK, BLOCK), BLOCK)
            block = tn(latn[:, cols], mine).astype(BF16)
            st_qkv[k, pl.ds(b * n, n), :, :, pl.ds(0, I)] = block.reshape(n, 2, R, I)
            return carry

        lax.fori_loop(0, D // BLOCK, query_weights, 0)
    st_qkv_c = to_core(7, st_qkv.at[:, :, other], cr_qkv)
    st_qkv_c.start()
    x_o = plane_heads(6, st_o_c, st_o, cr_o, xr_o)
    x_qkv = plane_heads(7, st_qkv_c, st_qkv, cr_qkv, xr_qkv)

    for copy in fp_z:
        copy.wait_recv()
    for s in range(S):
        own = pl.ds(pl.multiple_of(s * L + t * Lt, Lt), Lt)
        total = fp[s, my_rows(), :].astype(F32)
        for k in range(1, T):
            total = total + fpr[k - 1, s].astype(F32)
        new_lat[s, my_rows(), :] = (res[own, :] + total).astype(BF16)

    def share_rows(i, ref):
        out = [
            remote(ref.at[:, my_rows(), :], ref.at[:, my_rows(), :], zs.at[i, k - 1], zr.at[i, k - 1], z_dev(k))
            for k in range(1, T)
        ]
        came = [
            remote(
                ref.at[:, my_rows(T - k), :],
                ref.at[:, my_rows(T - k), :],
                zs.at[i, k - 1],
                zr.at[i, k - 1],
                z_dev(k),
            )
            for k in range(1, T)
        ]
        return out, came

    nl_z, nl_in = share_rows(8, new_lat)
    for copy in nl_z:
        copy.start()

    acc[...] = jnp.zeros_like(acc)

    def media_back(s, carry):
        base = pl.multiple_of(s * Kt, 16)

        def width_block(b, inner):
            cols = pl.ds(pl.multiple_of(b * BLOCK, BLOCK), BLOCK)
            weights = jnp.concatenate(
                [wq_b[k, pl.ds(b * n, n), :, :, pl.ds(I, 2 * I)].reshape(BLOCK, 2 * I) for k in range(T)], axis=1
            )
            mg[:, cols] = nt(dkv[pl.ds(base, Kt), :], weights)
            return inner

        lax.fori_loop(0, D // BLOCK, width_block, 0)

        def rows_back(b, inner):
            rows = pl.ds(pl.multiple_of(b * ROWS, ROWS), ROWS)
            unit, scale_inv = unit_rows(mown[s, rows, :].astype(F32))
            upstream = mg[rows, :]
            mown[s, rows, :] = norm_back(unit, scale_inv, mgain[...], upstream).astype(BF16)
            acc[0] += fold(upstream * unit)
            acc[1] += fold(upstream)
            return inner

        lax.fori_loop(0, Mt // ROWS, rows_back, 0)
        mgl[pl.ds(pl.multiple_of(s * Lt, Lt), Lt), :] = mg[pl.ds(Mt, Lt), :]
        pltpu.make_async_copy(mown.at[s], media_grad.at[s], osem.at[s]).start()
        return carry

    lax.fori_loop(0, S, media_back, 0)

    for copy in dq_z:
        copy.wait_recv()
    upstream_all = mgl[...]
    for k in range(T):
        total = dqb[head(k), :, my_rows(), :].astype(F32)
        for m in range(1, T):
            total = total + dqr[m - 1, head(k)].astype(F32)
        weights = wq_b[k, :, :, :, pl.ds(0, I)].reshape(D, I)
        upstream_all = upstream_all + nt(total.astype(BF16).reshape(S * Lt, I), weights)
    mgl[...] = upstream_all
    lat_gain_part = jnp.zeros((1, D), F32)
    lat_shift_part = jnp.zeros((1, D), F32)
    for s in range(S):
        own = pl.ds(pl.multiple_of(s * L + t * Lt, Lt), Lt)
        unit, scale_inv = unit_rows(lat[own, :].astype(F32))
        upstream = mgl[pl.ds(s * Lt, Lt), :]
        back = rgr[pl.ds(s * Lt, Lt), :] + norm_back(unit, scale_inv, lgain[...], upstream)
        lat_grad[s, my_rows(), :] = back.astype(BF16)
        lat_gain_part = lat_gain_part + jnp.sum(upstream * unit, axis=0, keepdims=True)
        lat_shift_part = lat_shift_part + jnp.sum(upstream, axis=0, keepdims=True)
    lg_z, lg_in = share_rows(9, lat_grad)
    for copy in lg_z:
        copy.start()

    vst[...] = jnp.concatenate(
        [
            jnp.sum(acc[0], axis=0, keepdims=True),
            jnp.sum(acc[1], axis=0, keepdims=True),
            lat_gain_part,
            lat_shift_part,
            feed_gain_part,
            feed_shift_part,
            jnp.zeros((2, D), F32),
        ],
        axis=0,
    )
    v_c = to_core(8, vst, vcr)
    v_c.start()
    v_c.wait_recv()
    vx[c] = vst[...] + vcr[...]

    def v_x(j):
        return remote(vx.at[c], vx.at[c], xs.at[8, j - 1], xr.at[8, j - 1], x_dev(j))

    def v_x_in(j):
        chip = lax.rem(c - j + C, C)
        return remote(vx.at[chip], vx.at[chip], xs.at[8, j - 1], xr.at[8, j - 1], x_dev(j))

    over_chips(lambda j: v_x(j).start())

    def sum_heads(x_copy, st, land):
        over_chips(lambda j: x_copy(j).wait_recv())
        for k in range(T):
            total = lax.fori_loop(
                1, C, lambda j, value, k=k: value + land[j - 1, k].astype(F32), st[k, c, core].astype(F32)
            )
            land[0, k] = total.astype(BF16)

    def z_sum(i, land, came):
        return [
            remote(land.at[0, k], came.at[T - k - 1], zs.at[i, k - 1], zr.at[i, T - k - 1], (d, head(k)))
            for k in range(1, T)
        ]

    sum_heads(x_o, st_o, xr_o)
    o_z = z_sum(10, xr_o, zr_o)
    for copy in o_z:
        copy.start()
    sum_heads(x_qkv, st_qkv, xr_qkv)
    q_z = z_sum(11, xr_qkv, zr_qkv)
    for copy in q_z:
        copy.start()

    over_chips(lambda j: v_x_in(j).wait_recv())
    vz[t] = lax.fori_loop(1, C, lambda j, value: value + vx[j], vx[0])
    v_z = [remote(vz.at[t], vz.at[t], zs.at[12, k - 1], zr.at[12, k - 1], z_dev(k)) for k in range(1, T)]
    v_z_in = [
        remote(vz.at[head(k)], vz.at[head(k)], zs.at[12, k - 1], zr.at[12, k - 1], z_dev(k)) for k in range(1, T)
    ]
    for copy in v_z:
        copy.start()

    def sum_feed(x_copy, st, land, out):
        over_chips(lambda j: x_copy(j).wait_recv())
        out[...] = lax.fori_loop(
            1, C, lambda j, value: value + land[j - 1].astype(F32), st[c, core].astype(F32)
        )

    sum_feed(x_up, st_up, xr_up, g_up)
    sum_feed(x_dn, st_dn, xr_dn, g_dn)

    for copy in v_z_in:
        copy.wait_recv()
    g_vec[...] = lax.fori_loop(1, T, lambda k, value: value + vz[k], vz[0])
    for copy in o_z:
        copy.wait_recv()
    total = xr_o[0, 0].astype(F32)
    for k in range(1, T):
        total = total + zr_o[k - 1].astype(F32)
    g_o[...] = total
    for copy in q_z:
        copy.wait_recv()
    total = xr_qkv[0, 0].astype(F32)
    for k in range(1, T):
        total = total + zr_qkv[k - 1].astype(F32)
    g_qkv[...] = total

    for copy in nl_in + lg_in:
        copy.wait_recv()
    for copy in wo_z + wq_z + att_z + lse_z + hg_z + fp_z + do_z + dq_z + nl_z + lg_z + o_z + q_z + v_z:
        copy.wait_send()
    for one in (wo_x, wq_x, up_x, dn_x, x_up, x_dn, x_o, x_qkv, v_x):
        over_chips(lambda j, one=one: one(j).wait_send())
    for copy in (wo_c, wq_c, up_c, dn_c, st_up_c, st_dn_c, st_o_c, st_qkv_c, v_c):
        copy.wait_send()
    for s in range(S):
        pltpu.make_async_copy(mown.at[s], media_grad.at[s], osem.at[s]).wait()


def solution(mesh):
    T, N = mesh.shape["tensor"], mesh.shape["dp"]

    def on_device(
        media_tokens,
        latents,
        image_counts,
        media_gain,
        media_shift,
        latent_gain,
        latent_shift,
        feed_gain,
        feed_shift,
        query_weight,
        key_weight,
        value_weight,
        output_weight,
        up_weight,
        down_weight,
        cotangent,
    ):
        samples, slots, width = media_tokens.shape
        z = Sizes(T, N, samples, latents.shape[1], slots, width, up_weight.shape[1], query_weight.shape[1])
        S, L, D, F, I, R, C = z.S, z.L, z.D, z.F, z.I, z.R, z.C
        row = lambda v: v.reshape(1, D)
        wqkv = jnp.concatenate([query_weight, key_weight, value_weight], axis=1).reshape(C, 2, R, 3 * I)
        wo = output_weight.T.reshape(C, 2, R, I)
        vmem = pl.BlockSpec(memory_space=pltpu.VMEM)
        hbm = pl.BlockSpec(memory_space=pl.ANY)
        V = pltpu.VMEM
        heads_rows = max(z.K, 1)
        scratch = [
            V((T, C, 2, R, 3 * I), BF16),
            V((T, C, 2, R, I), BF16),
            V((C, 2, R, F), BF16),
            V((C, 2, R, F), BF16),
            V((SLOTS_IN_FLIGHT, z.Mt, D), BF16),
            V((S, z.Mt, D), BF16),
            V((z.Mt, D), BF16),
            V((S, heads_rows, 2 * I), BF16),
            V((S * z.Kt, D), BF16),
            V((S * L, D), BF16),
            V((T, S, L, I), BF16),
            V((T, max(S, 8), z.q), F32),
            V((T, S * L, I), BF16),
            V((T, S * z.Kt, 2 * I), BF16),
            V((T * S, z.Kt, z.q), F32),
            V((S * z.Kt, T * 2 * I), BF16),
            V((S * L, D), F32),
            V((S * L, D), BF16),
            V((S * L, F), BF16),
            V((S * L, F), BF16),
            V((S, L, D), BF16),
            V((T - 1, S, z.Lt, D), BF16),
            V((S, L, D), BF16),
            V((T - 1, S, z.Lt, D), BF16),
            V((S * z.Lt, D), BF16),
            V((S * z.Lt, D), F32),
            V((T, S, L, I), BF16),
            V((T, S, L, I), BF16),
            V((T - 1, T, S, z.Lt, I), BF16),
            V((C, 2, R, F), BF16),
            V((C, 2, R, F), BF16),
            V((T, C, 2, R, I), BF16),
            V((T, C, 2, R, 3 * I), BF16),
            V((C, R, F), BF16),
            V((C, R, F), BF16),
            V((T, C, R, I), BF16),
            V((T, C, R, 3 * I), BF16),
            V((max(C - 1, 1), R, F), BF16),
            V((max(C - 1, 1), R, F), BF16),
            V((max(C - 1, 1), T, R, I), BF16),
            V((max(C - 1, 1), T, R, 3 * I), BF16),
            V((T - 1, R, I), BF16),
            V((T - 1, R, 3 * I), BF16),
            V((z.Kt, D), F32),
            V((S * z.Lt, D), F32),
            V((2, 8, D), F32),
            V((8, D), F32),
            V((8, D), F32),
            V((C, 8, D), F32),
            V((T, 8, D), F32),
            pltpu.SemaphoreType.DMA((SLOTS_IN_FLIGHT + 1,)),
            pltpu.SemaphoreType.DMA((S,)),
            pltpu.SemaphoreType.DMA((13, T - 1)),
            pltpu.SemaphoreType.DMA((13, T - 1)),
            pltpu.SemaphoreType.DMA((9, max(C - 1, 1))),
            pltpu.SemaphoreType.DMA((9, max(C - 1, 1))),
            pltpu.SemaphoreType.DMA((9,)),
            pltpu.SemaphoreType.DMA((9,)),
        ]
        shape = jax.ShapeDtypeStruct
        outs = pl.pallas_call(
            functools.partial(layer_kernel, z),
            out_shape=[
                shape((S, L, D), BF16),
                shape((S, z.Mt, D), BF16),
                shape((S, L, D), BF16),
                shape((R, 3 * I), F32),
                shape((R, I), F32),
                shape((R, F), F32),
                shape((R, F), F32),
                shape((8, D), F32),
            ],
            in_specs=[pl.BlockSpec(memory_space=pltpu.SMEM), hbm] + [vmem] * 12,
            out_specs=[vmem, hbm] + [vmem] * 6,
            scratch_shapes=scratch,
            compiler_params=pltpu.CompilerParams(
                collective_id=0, has_side_effects=True, vmem_limit_bytes=60 * 1024 * 1024
            ),
            name="resampler_layer",
        )(
            image_counts,
            media_tokens,
            latents.reshape(S * L, D),
            cotangent.reshape(S * L, D),
            row(media_gain),
            row(media_shift),
            row(latent_gain),
            row(latent_shift),
            row(feed_gain),
            row(feed_shift),
            wqkv,
            wo,
            up_weight,
            down_weight.T,
        )
        new_latents, media_grad, latent_grad, g_qkv, g_o, g_up, g_dn, g_vec = outs
        own = lax.dynamic_slice_in_dim(g_vec, lax.axis_index("dp") * R, R, 1)
        return (
            new_latents,
            media_grad,
            latent_grad,
            g_qkv[:, :I],
            g_qkv[:, I : 2 * I],
            g_qkv[:, 2 * I :],
            g_o.T,
            g_up,
            g_dn.T,
            g_vec[0],
            g_vec[1],
            own[2],
            own[3],
            own[4],
            own[5],
        )

    placed = (
        P("dp", None, None),
        P("dp", None, None),
        P("dp"),
        P(),
        P(),
        P(),
        P(),
        P(),
        P(),
        P(None, "tensor"),
        P(None, "tensor"),
        P(None, "tensor"),
        P("tensor", None),
        P("dp", "tensor"),
        P("tensor", "dp"),
        P("dp", None, None),
    )
    return jax.shard_map(
        on_device,
        mesh=mesh,
        in_specs=placed,
        out_specs=(
            P("dp", None, None),
            P("dp", "tensor", None),
            P("dp", None, None),
            P("dp", "tensor"),
            P("dp", "tensor"),
            P("dp", "tensor"),
            P("tensor", "dp"),
            P("dp", "tensor"),
            P("tensor", "dp"),
            P(),
            P(),
            P("dp"),
            P("dp"),
            P("dp"),
            P("dp"),
        ),
        check_vma=False,
    )
```

time: 897 us -> 181 us (0.20)
  waiting for transfers between devices: 684 us -> 0 us
  Pallas kernels: 0 us -> 161 us
  blocking collectives: 66.8 us -> 0 us
  matrix products: 53.5 us -> 0 us
  other arithmetic: 51.6 us -> 2.09 us
  between operations: 16.7 us -> 0.68 us
    reduce_scatter x7 -> x0, waiting for transfers between devices: 559 us -> none  [the longest x1 347 us: on_device(): lax.psum_scatter(against(media_pairs, pair_weight), 'tensor', scatter_dim...]
    pallas_call x0 -> x1, Pallas kernels: none -> 161 us  [on_device(): pl.pallas_call(functools.partial(layer_kernel, z), out_shape=[shape((S, L...]
    psum x4 -> x0, waiting for transfers between devices: 124 us -> none  [the longest x1 53.3 us: on_device(): residual = latent_float + lax.psum(head_part, 'tensor')]
    dot_general x22 -> x0, matrix products: 53.5 us -> none  [the longest x6 17.1 us: against(): lax.dot_general(left, right, (((left.ndim - 1,), (1,)), ((), ())), prefer...]
    psum x1 -> x0, blocking collectives: 41.8 us -> none  [on_device(): lax.psum((media_gain_part, media_shift_part), ('dp', 'tensor'))]
    reduce_sum x12 -> x0, other arithmetic: 28 us -> none  [the longest x4 10.6 us: normalize(): centre = inputs - jnp.mean(inputs, axis=-1, keepdims=True)]
    unnamed x1 -> x0, blocking collectives: 25 us -> none
    convert_element_type x7 -> x0, other arithmetic: 22.2 us -> none  [the longest x1 7.4 us: on_device(): media_normed = (media_unit * media_gain + media_shift).astype(jnp.bfloat16)]
  transfers between devices with their start and end apart: 13 -> 0, of which waited for: 11 -> 0; matrix products, arithmetic and copies ran while one was open for 7% -> 0% of each run, Pallas kernels for 0% -> 0%
where the time goes in v1:
time: 181 us; the launch traced here: 180 us
  Pallas kernels  161 us (89%)
  local copies, waits for them, and re-layouts  16.5 us (9%)
  other arithmetic  2.09 us (1%)
    pallas_call x1, Pallas kernels, on_device(): pl.pallas_call(functools.partial(layer_kernel, z), out_shape=[shape((S, L...  161 us
    unnamed x13, local copies, waits for them, and re-layouts  10.3 us

profile of v1, /device:TPU:0, one launch (start us, length us, event | category | flops | bytes accessed | tf_op | source)
XLA Modules:
  0.0 180.2 jit_solution(231317275082039324)
XLA Ops:
  0.7 1.8 copy.31
  2.4 1.8 copy.32
  4.2 2.1 %pad_maximum_fusion = bf16[1024,384]{1,0:T(8,128)(2,1)} fusion(bf16[1024,128]{1,0:T(8,128)(2,1)} %param.27, bf16[1024,128]{1,0:T(8,128)(2,1)} %param.26, bf16[1024,128]{1,0:T(8,128)(2,1)} %param.25), kind=kLoop, calls=%fused_computation | loop fusion | flops 2359296 | bytes 1572864 | tf_op jit(solution)/shard_map/concatenate | solution.py:810
  6.3 160.9 %resampler_layer.1 = (bf16[4,64,1024]{2,1,0:T(8,128)(2,1)}, bf16[4,320,1024]{2,1,0:T(8,128)(2,1)}, bf16[4,64,1024]{2,1,0:T(8,128)(2,1)}, f32[128,384]{1,0:T(8,12...) custom-call(s32[4]{0:T(128)} %counts.1, ...), custom_call_target="tpu_custom_call" | custom-call | tf_op jit(solution)/shard_map/resampler_layer/pallas_call | solution.py:877
  167.2 0.0 copy-start
  167.2 0.8 constant_dynamic-slice_fusion
  168.1 1.4 fusion.1
  169.5 0.5 slice_bitcast_fusion
  170.0 1.6 copy.33
  171.6 1.6 fusion
  173.2 2.0 %copy.34 = f32[1024,128]{1,0:T(8,128)} copy(f32[1024,128]{0,1:T(8,128)} %bitcast.29) | data formatting | bytes 1048576
  175.2 1.9 %copy.39 = bf16[4,64,1024]{2,1,0:T(8,128)(2,1)} copy(bf16[4,64,1024]{2,1,0:T(8,128)(2,1)} %get-tuple-element.70) | data formatting | bytes 1048576
  177.1 0.0 copy-done
  177.1 0.0 copy-start.2
  177.1 0.0 copy-start.1
  177.1 1.5 copy.40
  178.6 0.0 copy-done.2
  178.6 0.8 copy.41
  179.4 0.0 copy-done.1
  179.4 0.8 copy.42
Async XLA Ops:
  167.2 9.9 %copy-start = (bf16[4,320,1024]{2,1,0:T(8,128)(2,1)S(1)}, bf16[4,320,1024]{2,1,0:T(8,128)(2,1)}, u32[]{:S(2)}) copy-start(bf16[4,320,1024]{2,1,0:T(8,128)(2,1)} %get-tuple-element.71) | copy-start | bytes 7864324
  177.1 1.5 copy-start.2
  177.1 2.3 %copy-start.1 = (f32[128,1024]{1,0:T(8,128)S(1)}, f32[128,1024]{1,0:T(8,128)}, u32[]{:S(2)}) copy-start(f32[128,1024]{1,0:T(8,128)} %get-tuple-element.77) | copy-start | bytes 1572868

commit v2 on v1

--- a/solution.py
+++ b/solution.py
@@ -61,6 +61,7 @@
         self.K = lat + slots
         self.H = inner // HEAD_DIM
         self.q = self.H * lat
+        self.G = min(2, tensor)
 
 
 def layer_kernel(
@@ -75,7 +76,9 @@
     lshift,
     fgain,
     fshift,
-    wqkv,
+    wq,
+    wk,
+    wv,
     wo,
     up,
     dn,
@@ -94,15 +97,15 @@
     mbuf,
     mown,
     xn,
-    kvown,
     ctx,
     latn,
     att,
     lse,
     qall,
-    kvall,
+    kall,
+    vall,
     pall,
-    dkv,
+    pairs,
     res,
     hin,
     act,
@@ -130,7 +133,6 @@
     xr_qkv,
     zr_o,
     zr_qkv,
-    mg,
     mgl,
     acc,
     vst,
@@ -147,7 +149,8 @@
     cr,
 ):
     T, N, C, S, L, M, D = z.T, z.N, z.C, z.S, z.L, z.M, z.D
-    F, I, R, Lt, Mt, Kt, H = z.F, z.I, z.R, z.Lt, z.Mt, z.Kt, z.H
+    F, I, R, Lt, Mt, Kt, G = z.F, z.I, z.R, z.Lt, z.Mt, z.Kt, z.G
+    GI = G * I
     scale_factor = HEAD_DIM ** (-0.5)
     t = lax.axis_index("tensor")
     d = lax.axis_index("dp")
@@ -182,9 +185,9 @@
     def over_chips(body):
         lax.fori_loop(1, C, lambda j, carry: (body(j), carry)[1], 0)
 
-    def gather_z(i, src, buf):
+    def gather_z(i, buf):
         return [
-            remote(src.at[c, core], buf.at[k, c, core], zs.at[i, k - 1], zr.at[i, k - 1], z_dev(k))
+            remote(buf.at[0, c, core], buf.at[k, c, core], zs.at[i, k - 1], zr.at[i, k - 1], z_dev(k))
             for k in range(1, T)
         ]
 
@@ -194,12 +197,12 @@
 
         return one
 
-    wo_z = gather_z(0, wo, wo_b)
-    wq_z = gather_z(1, wqkv, wq_b)
+    wo_z = gather_z(0, wo_b)
+    wq_z = gather_z(1, wq_b)
     wo_x = gather_x(0, wo_b.at[pl.ds(1, T - 1), c, core], wo_b.at[pl.ds(1, T - 1), c, core])
     wq_x = gather_x(1, wq_b.at[pl.ds(1, T - 1), c, core], wq_b.at[pl.ds(1, T - 1), c, core])
     up_x = gather_x(2, up, up_b.at[c, core])
-    dn_x = gather_x(3, dn, dn_b.at[c, core])
+    dn_x = gather_x(3, dn_b.at[c, core], dn_b.at[c, core])
 
     def relay(i, ref):
         return remote(ref, ref, cs.at[i], cr.at[i], core_dev)
@@ -225,6 +228,11 @@
         tile_copy(i).start()
     own_copy.start()
 
+    wo_b[0] = wo[...].T.reshape(C, 2, R, I)
+    for m, weight in enumerate((wq, wk, wv)):
+        wq_b[0, :, :, :, pl.ds(m * I, I)] = weight[...].reshape(C, 2, R, I)
+    up_b[c, core] = up[...]
+    dn_b[c, core] = dn[...].T
     barrier = pltpu.get_barrier_semaphore()
 
     def greet(dev):
@@ -240,56 +248,70 @@
         copy.start()
     over_chips(lambda j: up_x(j).start())
     over_chips(lambda j: dn_x(j).start())
-    wo_b[0] = wo[...]
-    wq_b[0] = wqkv[...]
-    up_b[c, core] = up[...]
-    dn_b[c, core] = dn[...]
-
-    def lat_norm(b, carry):
-        rows = pl.ds(pl.multiple_of(b * ROWS, ROWS), ROWS)
+
+    for b in range(S * L // ROWS):
+        rows = pl.ds(b * ROWS, ROWS)
         unit, _ = unit_rows(lat[rows, :].astype(F32))
         latn[rows, :] = (unit * lgain[...] + lshift[...]).astype(BF16)
-        return carry
-
-    lax.fori_loop(0, S * L // ROWS, lat_norm, 0)
-    own_w = wq_b[0].reshape(D, 3 * I)
-    own_qkv = nn(latn[...], own_w).astype(BF16)
-    qall[0] = own_qkv[:, :I]
+    own_qkv = nn(latn[...], wq_b[0].reshape(D, 3 * I)).astype(BF16)
+    qall[:, pl.ds(0, I)] = own_qkv[:, :I]
     for s in range(S):
-        kvown[s, pl.ds(M, L), :] = own_qkv[s * L : (s + 1) * L, I:]
+        pairs[pl.ds(M, L), pl.ds(s * 2 * I, 2 * I)] = own_qkv[s * L : (s + 1) * L, I:]
         ctx[pl.ds(s * Kt + Mt, Lt), :] = latn[pl.ds(pl.multiple_of(s * L + t * Lt, Lt), Lt), :]
 
-    def media_tile(i, carry):
+    def tile_norm(i, half):
         slot = lax.rem(i, SLOTS_IN_FLIGHT)
+        for b in range(Mt // ROWS):
+            rows = pl.ds(b * ROWS, ROWS)
+            unit, _ = unit_rows(mbuf[slot, rows, :].astype(F32))
+            xn[half, rows, :] = (unit * mgain[...] + mshift[...]).astype(BF16)
+
+    def tile_pair(i, half):
         s, r = lax.div(i, T), lax.rem(i, T)
-        tile_copy(i).wait()
-
-        def rows_norm(b, inner):
-            rows = pl.ds(pl.multiple_of(b * ROWS, ROWS), ROWS)
-            unit, _ = unit_rows(mbuf[slot, rows, :].astype(F32))
-            xn[rows, :] = (unit * mgain[...] + mshift[...]).astype(BF16)
-            return inner
-
-        lax.fori_loop(0, Mt // ROWS, rows_norm, 0)
-
+        pair = nn(xn[half], wq_b[0, :, :, :, pl.ds(I, 2 * I)].reshape(D, 2 * I))
+        lanes = pl.ds(pl.multiple_of(s * 2 * I, 2 * I), 2 * I)
+        pairs[pl.ds(pl.multiple_of(r * Mt, Mt), Mt), lanes] = pair.astype(BF16)
+
+    def tile_keep(i, half):
+        s, r = lax.div(i, T), lax.rem(i, T)
+
+        @pl.when(r == t)
+        def _():
+            ctx[pl.ds(pl.multiple_of(s * Kt, 16), Mt), :] = xn[half]
+
+    def tile_next(i):
         @pl.when(i + SLOTS_IN_FLIGHT < n_tiles)
         def _():
             tile_copy(i + SLOTS_IN_FLIGHT).start()
 
-        pair = nn(xn[...], wq_b[0].reshape(D, 3 * I)[:, I:])
-        kvown[s, pl.ds(pl.multiple_of(r * Mt, Mt), Mt), :] = pair.astype(BF16)
-
-        @pl.when(r == t)
+    tile_copy(0).wait()
+    tile_norm(0, 0)
+    tile_next(0)
+
+    def two_tiles(j, carry):
+        i = 2 * j
+        tile_copy(i + 1).wait()
+
+        @pl.when(i + 2 < n_tiles)
         def _():
-            ctx[pl.ds(pl.multiple_of(s * Kt, 16), Mt), :] = xn[...]
-
-        @pl.when(i == n_tiles // 4)
+            tile_copy(i + 2).wait()
+
+        tile_keep(i, 0)
+        tile_pair(i, 0)
+        tile_norm(i + 1, 1)
+        tile_keep(i + 1, 1)
+        tile_pair(i + 1, 1)
+        tile_norm(lax.rem(i + 2, n_tiles), 0)
+        tile_next(i + 1)
+        tile_next(i + 2)
+
+        @pl.when(j == n_tiles // 8)
         def _():
             for copy in wo_z:
                 copy.wait_recv()
             over_chips(lambda j: wo_x(j).start())
 
-        @pl.when(i == n_tiles // 2)
+        @pl.when(j == n_tiles // 4)
         def _():
             for copy in wq_z:
                 copy.wait_recv()
@@ -297,25 +319,26 @@
 
         return carry
 
-    lax.fori_loop(0, n_tiles, media_tile, 0)
-
-    lane_head = lax.broadcasted_iota(jnp.int32, (1, I), 1) // HEAD_DIM
+    lax.fori_loop(0, n_tiles // 2, two_tiles, 0)
 
     def spread(x):
+        lane_head = lax.broadcasted_iota(jnp.int32, (1, x.shape[1]), 1) // HEAD_DIM
         zero = jnp.zeros_like(x)
-        return jnp.concatenate([jnp.where(lane_head == h, x, zero) for h in range(H)], axis=0)
+        return jnp.concatenate(
+            [jnp.where(lane_head == h, x, zero) for h in range(x.shape[1] // HEAD_DIM)], axis=0
+        )
 
     def gather_heads(x):
+        lane_head = lax.broadcasted_iota(jnp.int32, (1, x.shape[1]), 1) // HEAD_DIM
         out = x[:L]
-        for h in range(1, H):
+        for h in range(1, x.shape[1] // HEAD_DIM):
             out = jnp.where(lane_head == h, x[h * L : (h + 1) * L], out)
         return out
 
-    def attend(s, carry):
-        keys = kvown[s, :, pl.ds(0, I)]
-        values = kvown[s, :, pl.ds(I, I)]
-        queries = qall[0, pl.ds(pl.multiple_of(s * L, L), L), :]
-        scores = nt(keys, spread(queries)) * scale_factor
+    for s in range(S):
+        keys = pairs[pl.ds(0, z.K), pl.ds(s * 2 * I, I)]
+        values = pairs[pl.ds(0, z.K), pl.ds(s * 2 * I + I, I)]
+        scores = nt(keys, spread(qall[pl.ds(s * L, L), pl.ds(0, I)])) * scale_factor
         slot = lax.broadcasted_iota(jnp.int32, (z.K, 1), 0)
         valid = (slot < counts[s] * PATCH) | (slot >= M)
         scores = jnp.where(valid, scores, NEGATIVE)
@@ -324,9 +347,6 @@
         probs = jnp.exp(scores - total).astype(BF16)
         att[0, s] = gather_heads(tn(probs, values)).astype(BF16)
         lse[0, pl.ds(s, 1), :] = total
-        return carry
-
-    lax.fori_loop(0, S, attend, 0)
 
     att_z = [remote(att.at[0], att.at[k], zs.at[2, k - 1], zr.at[2, k - 1], z_dev(k)) for k in range(1, T)]
     lse_z = [remote(lse.at[0], lse.at[k], zs.at[3, k - 1], zr.at[3, k - 1], z_dev(k)) for k in range(1, T)]
@@ -344,21 +364,15 @@
     for copy in att_z:
         copy.wait_recv()
 
-    def mat(ref, k, width):
-        return ref[k].reshape(D, width)
-
-    part = lat[...].astype(F32)
-    for k in range(T):
-        part = part + nt(att[k].reshape(S * L, I), mat(wo_b, k, I))
-    res[...] = part
-
-    def feed_norm(b, carry):
-        rows = pl.ds(pl.multiple_of(b * ROWS, ROWS), ROWS)
+    def heads_wo():
+        return jnp.concatenate([wo_b[k].reshape(D, I) for k in range(T)], axis=1)
+
+    att_all = jnp.concatenate([att[k].reshape(S * L, I) for k in range(T)], axis=1)
+    res[...] = lat[...].astype(F32) + nt(att_all, heads_wo())
+    for b in range(S * L // ROWS):
+        rows = pl.ds(b * ROWS, ROWS)
         unit, _ = unit_rows(res[rows, :])
         hin[rows, :] = (unit * fgain[...] + fshift[...]).astype(BF16)
-        return carry
-
-    lax.fori_loop(0, S * L // ROWS, feed_norm, 0)
 
     up_c.wait_recv()
     dn_c.wait_recv()
@@ -422,35 +436,43 @@
     own_copy.wait()
     wq_c.wait_recv()
 
-    def all_queries(k, carry):
-        qall[k] = nn(latn[...], wq_b[k, :, :, :, pl.ds(0, I)].reshape(D, I)).astype(BF16)
+    for k in range(1, T):
+        qall[:, pl.ds(k * I, I)] = nn(latn[...], wq_b[k, :, :, :, pl.ds(0, I)].reshape(D, I)).astype(BF16)
+    half_rows = S * Kt // 2
+
+    def all_pairs(i, carry):
+        k = lax.div(i, 2)
+        rows = pl.ds(pl.multiple_of(lax.rem(i, 2) * half_rows, 16), half_rows)
+        lanes = pl.ds(pl.multiple_of(k * I, I), I)
+        pair = nn(ctx[rows, :], wq_b[k, :, :, :, pl.ds(I, 2 * I)].reshape(D, 2 * I)).astype(BF16)
+        kall[rows, lanes] = pair[:, :I]
+        vall[rows, lanes] = pair[:, I:]
         return carry
 
-    lax.fori_loop(1, T, all_queries, 0)
-
-    def all_pairs(i, carry):
-        k, s = lax.div(i, S), lax.rem(i, S)
-        rows = pl.ds(pl.multiple_of(s * Kt, 16), Kt)
-        pair = nn(ctx[rows, :], wq_b[k, :, :, :, pl.ds(I, 2 * I)].reshape(D, 2 * I))
-        kvall[k, rows, :] = pair.astype(BF16)
-        return carry
-
-    lax.fori_loop(0, T * S, all_pairs, 0)
+    lax.fori_loop(0, 2 * T, all_pairs, 0)
     for copy in lse_z:
         copy.wait_recv()
     slot_of = lax.broadcasted_iota(jnp.int32, (Kt, 1), 0)
 
+    def group(i):
+        g, s = lax.div(i, S), lax.rem(i, S)
+        rows = pl.ds(pl.multiple_of(s * Kt, 16), Kt)
+        lanes = pl.ds(pl.multiple_of(g * GI, GI), GI)
+        lat_rows = pl.ds(pl.multiple_of(s * L, L), L)
+        return g, s, rows, lanes, lat_rows
+
+    def joined(g, pick):
+        return jnp.concatenate([pick(g * G + j) for j in range(G)], axis=1)
+
     def probabilities(i, carry):
-        k, s = lax.div(i, S), lax.rem(i, S)
-        rows = pl.ds(pl.multiple_of(s * Kt, 16), Kt)
-        queries = qall[k, pl.ds(pl.multiple_of(s * L, L), L), :]
-        scores = nt(kvall[k, rows, pl.ds(0, I)], spread(queries)) * scale_factor
+        g, s, rows, lanes, lat_rows = group(i)
+        scores = nt(kall[rows, lanes], spread(qall[lat_rows, lanes])) * scale_factor
         valid = (slot_of + t * Mt < counts[s] * PATCH) | (slot_of >= Mt)
         scores = jnp.where(valid, scores, NEGATIVE)
-        pall[i] = jnp.exp(scores - lse[k, pl.ds(s, 1), :])
+        pall[i] = jnp.exp(scores - joined(g, lambda k: lse[k, pl.ds(s, 1), :]))
         return carry
 
-    lax.fori_loop(0, T * S, probabilities, 0)
+    lax.fori_loop(0, T // G * S, probabilities, 0, unroll=2)
 
     for copy in hg_z:
         copy.wait_recv()
@@ -467,9 +489,9 @@
         feed_shift_part = feed_shift_part + jnp.sum(upstream, axis=0, keepdims=True)
         rgr[pl.ds(s * Lt, Lt), :] = back
         og[pl.ds(s * Lt, Lt), :] = back.astype(BF16)
+    grads_all = nn(og[...], heads_wo()).astype(BF16)
     for k in range(T):
-        grads = nn(og[...], mat(wo_b, k, I)).astype(BF16)
-        dob[head(k), :, my_rows(), :] = grads.reshape(S, Lt, I)
+        dob[head(k), :, my_rows(), :] = grads_all[:, k * I : (k + 1) * I].reshape(S, Lt, I)
     do_z = [
         remote(
             dob.at[:, :, my_rows(), :], dob.at[:, :, my_rows(), :], zs.at[6, k - 1], zr.at[6, k - 1], z_dev(k)
@@ -489,16 +511,11 @@
     for copy in do_z:
         copy.start()
 
-    for k in range(T):
-        mine = att[k, :, my_rows(), :].reshape(S * Lt, I)
-
-        def out_weights(b, carry, k=k, mine=mine):
-            cols = pl.ds(pl.multiple_of(b * BLOCK, BLOCK), BLOCK)
-            block = tn(og[:, cols], mine).astype(BF16)
-            st_o[k, pl.ds(b * n, n)] = block.reshape(n, 2, R, I)
-            return carry
-
-        lax.fori_loop(0, D // BLOCK, out_weights, 0)
+    att_own = jnp.concatenate([att[k, :, my_rows(), :].reshape(S * Lt, I) for k in range(T)], axis=1)
+    for b in range(D // BLOCK):
+        block = tn(og[:, pl.ds(b * BLOCK, BLOCK)], att_own).astype(BF16)
+        for k in range(T):
+            st_o[k, pl.ds(b * n, n)] = block[:, k * I : (k + 1) * I].reshape(n, 2, R, I)
     st_o_c = to_core(6, st_o.at[:, :, other], cr_o)
     st_o_c.start()
 
@@ -544,30 +561,30 @@
         copy.wait_recv()
 
     def attend_back(i, carry):
-        k, s = lax.div(i, S), lax.rem(i, S)
-        rows = pl.ds(pl.multiple_of(s * Kt, 16), Kt)
-        lanes = pl.multiple_of(k * 2 * I, 2 * I)
-        keys = kvall[k, rows, pl.ds(0, I)]
-        values = kvall[k, rows, pl.ds(I, I)]
-        queries = spread(qall[k, pl.ds(pl.multiple_of(s * L, L), L), :])
-        grads = spread(dob[head(k), s])
-        outs = spread(att[k, s])
+        g, s, rows, lanes, lat_rows = group(i)
+        values_at = pl.ds(pl.multiple_of(T * I + g * GI, GI), GI)
+        keys = kall[rows, lanes]
+        queries = spread(qall[lat_rows, lanes])
+        grads = spread(joined(g, lambda k: dob[head(k), s]))
+        outs = spread(joined(g, lambda k: att[k, s]))
         product = grads.astype(F32) * outs.astype(F32)
         inner = lax.dot_general(
-            jnp.ones((8, I), F32),
+            jnp.ones((8, GI), F32),
             product,
             (((1,), (1,)), ((), ())),
             preferred_element_type=F32,
             precision=lax.Precision.HIGHEST,
         )[:1]
         probs = pall[i]
-        score_grad = (probs * (nt(values, grads) - inner)).astype(BF16)
-        dkv[rows, pl.ds(lanes, I)] = (nn(score_grad, queries) * scale_factor).astype(BF16)
-        dkv[rows, pl.ds(lanes + I, I)] = nn(probs.astype(BF16), grads).astype(BF16)
-        dqb[head(k), s] = (gather_heads(tn(score_grad, keys)) * scale_factor).astype(BF16)
+        score_grad = (probs * (nt(vall[rows, lanes], grads) - inner)).astype(BF16)
+        pairs[rows, lanes] = (nn(score_grad, queries) * scale_factor).astype(BF16)
+        pairs[rows, values_at] = nn(probs.astype(BF16), grads).astype(BF16)
+        query_grad = (gather_heads(tn(score_grad, keys)) * scale_factor).astype(BF16)
+        for j in range(G):
+            dqb[head(g * G + j), s] = query_grad[:, j * I : (j + 1) * I]
         return carry
 
-    lax.fori_loop(0, T * S, attend_back, 0)
+    lax.fori_loop(0, T // G * S, attend_back, 0, unroll=2)
     dq_z = [
         remote(
             dqb.at[:, :, my_rows(k), :], dqr.at[k - 1], zs.at[7, k - 1], zr.at[7, k - 1], z_dev(k)
@@ -577,26 +594,16 @@
     for copy in dq_z:
         copy.start()
 
-    def pair_weights(b, carry):
-        cols = pl.ds(pl.multiple_of(b * BLOCK, BLOCK), BLOCK)
-        block = tn(ctx[:, cols], dkv[...]).astype(BF16)
+    dq_all = jnp.concatenate([dqb[head(k)].reshape(S * L, I) for k in range(T)], axis=1)
+    for b in range(D // BLOCK):
+        cols = pl.ds(b * BLOCK, BLOCK)
+        block = tn(ctx[:, cols], pairs[pl.ds(0, S * Kt), pl.ds(0, 2 * T * I)]).astype(BF16)
+        query_block = tn(latn[:, cols], dq_all).astype(BF16)
         for k in range(T):
-            st_qkv[k, pl.ds(b * n, n), :, :, pl.ds(I, 2 * I)] = block[:, k * 2 * I : (k + 1) * 2 * I].reshape(
-                n, 2, R, 2 * I
-            )
-        return carry
-
-    lax.fori_loop(0, D // BLOCK, pair_weights, 0)
-    for k in range(T):
-        mine = dqb[head(k)].reshape(S * L, I)
-
-        def query_weights(b, carry, k=k, mine=mine):
-            cols = pl.ds(pl.multiple_of(b * BLOCK, BLOCK), BLOCK)
-            block = tn(latn[:, cols], mine).astype(BF16)
-            st_qkv[k, pl.ds(b * n, n), :, :, pl.ds(0, I)] = block.reshape(n, 2, R, I)
-            return carry
-
-        lax.fori_loop(0, D // BLOCK, query_weights, 0)
+            lanes = slice(k * I, (k + 1) * I)
+            parts = (query_block[:, lanes], block[:, lanes], block[:, T * I :][:, lanes])
+            for m, part in enumerate(parts):
+                st_qkv[k, pl.ds(b * n, n), :, :, pl.ds(m * I, I)] = part.reshape(n, 2, R, I)
     st_qkv_c = to_core(7, st_qkv.at[:, :, other], cr_qkv)
     st_qkv_c.start()
     x_o = plane_heads(6, st_o_c, st_o, cr_o, xr_o)
@@ -634,34 +641,39 @@
 
     acc[...] = jnp.zeros_like(acc)
 
-    def media_back(s, carry):
-        base = pl.multiple_of(s * Kt, 16)
-
-        def width_block(b, inner):
-            cols = pl.ds(pl.multiple_of(b * BLOCK, BLOCK), BLOCK)
+    blocks = D // BLOCK
+
+    def width(s, rows):
+        return jnp.concatenate([pall[s % 2 * blocks + b, rows, :] for b in range(blocks)], axis=1)
+
+    def media_width(s):
+        for b in range(blocks):
             weights = jnp.concatenate(
-                [wq_b[k, pl.ds(b * n, n), :, :, pl.ds(I, 2 * I)].reshape(BLOCK, 2 * I) for k in range(T)], axis=1
+                [
+                    wq_b[k, pl.ds(b * n, n), :, :, pl.ds(m * I, I)].reshape(BLOCK, I)
+                    for m in (1, 2)
+                    for k in range(T)
+                ],
+                axis=1,
             )
-            mg[:, cols] = nt(dkv[pl.ds(base, Kt), :], weights)
-            return inner
-
-        lax.fori_loop(0, D // BLOCK, width_block, 0)
-
-        def rows_back(b, inner):
-            rows = pl.ds(pl.multiple_of(b * ROWS, ROWS), ROWS)
+            pall[s % 2 * blocks + b] = nt(pairs[pl.ds(s * Kt, Kt), pl.ds(0, 2 * T * I)], weights)
+
+    def media_rows(s):
+        for b in range(Mt // ROWS):
+            rows = pl.ds(b * ROWS, ROWS)
             unit, scale_inv = unit_rows(mown[s, rows, :].astype(F32))
-            upstream = mg[rows, :]
+            upstream = width(s, rows)
             mown[s, rows, :] = norm_back(unit, scale_inv, mgain[...], upstream).astype(BF16)
             acc[0] += fold(upstream * unit)
             acc[1] += fold(upstream)
-            return inner
-
-        lax.fori_loop(0, Mt // ROWS, rows_back, 0)
-        mgl[pl.ds(pl.multiple_of(s * Lt, Lt), Lt), :] = mg[pl.ds(Mt, Lt), :]
+        mgl[pl.ds(s * Lt, Lt), :] = width(s, pl.ds(Mt, Lt))
         pltpu.make_async_copy(mown.at[s], media_grad.at[s], osem.at[s]).start()
-        return carry
-
-    lax.fori_loop(0, S, media_back, 0)
+
+    media_width(0)
+    for s in range(S):
+        if s + 1 < S:
+            media_width(s + 1)
+        media_rows(s)
 
     for copy in dq_z:
         copy.wait_recv()
@@ -782,6 +794,37 @@
         pltpu.make_async_copy(mown.at[s], media_grad.at[s], osem.at[s]).wait()
 
 
+def hand_out(z, new_lat, media_grad, lat_grad, g_qkv, g_o, g_up, g_dn, g_vec, *refs):
+    outs, held, sem_in, sem_out = refs[:15], refs[15], refs[16], refs[17]
+    loads = [pltpu.make_async_copy(media_grad.at[s], held.at[s], sem_in.at[s]) for s in range(z.S)]
+    stores = [pltpu.make_async_copy(held.at[s], outs[1].at[s], sem_out.at[s]) for s in range(z.S)]
+    for copy in loads:
+        copy.start()
+    for load, store in zip(loads, stores):
+        load.wait()
+        store.start()
+    outs[0][...] = new_lat[...]
+    outs[2][...] = lat_grad[...]
+    for m in range(3):
+        outs[3 + m][...] = g_qkv[:, pl.ds(m * z.I, z.I)]
+    outs[6][...] = g_o[...].T
+    outs[7][...] = g_up[...]
+    outs[8][...] = g_dn[...].T
+    outs[9][...] = g_vec[pl.ds(0, 1), :]
+    outs[10][...] = g_vec[pl.ds(1, 1), :]
+    first = lax.axis_index("dp") * z.R
+    row = lax.broadcasted_iota(jnp.int32, (z.D, z.R), 0)
+    col = lax.broadcasted_iota(jnp.int32, (z.D, z.R), 1)
+    pick = jnp.where(row == col + first, 1.0, 0.0).astype(F32)
+    own = lax.dot_general(
+        g_vec[...], pick, (((1,), (0,)), ((), ())), preferred_element_type=F32, precision=lax.Precision.HIGHEST
+    )
+    for m in range(4):
+        outs[11 + m][...] = own[2 + m : 3 + m]
+    for store in stores:
+        store.wait()
+
+
 def solution(mesh):
     T, N = mesh.shape["tensor"], mesh.shape["dp"]
 
@@ -807,12 +850,9 @@
         z = Sizes(T, N, samples, latents.shape[1], slots, width, up_weight.shape[1], query_weight.shape[1])
         S, L, D, F, I, R, C = z.S, z.L, z.D, z.F, z.I, z.R, z.C
         row = lambda v: v.reshape(1, D)
-        wqkv = jnp.concatenate([query_weight, key_weight, value_weight], axis=1).reshape(C, 2, R, 3 * I)
-        wo = output_weight.T.reshape(C, 2, R, I)
         vmem = pl.BlockSpec(memory_space=pltpu.VMEM)
         hbm = pl.BlockSpec(memory_space=pl.ANY)
         V = pltpu.VMEM
-        heads_rows = max(z.K, 1)
         scratch = [
             V((T, C, 2, R, 3 * I), BF16),
             V((T, C, 2, R, I), BF16),
@@ -820,16 +860,16 @@
             V((C, 2, R, F), BF16),
             V((SLOTS_IN_FLIGHT, z.Mt, D), BF16),
             V((S, z.Mt, D), BF16),
-            V((z.Mt, D), BF16),
-            V((S, heads_rows, 2 * I), BF16),
+            V((2, z.Mt, D), BF16),
             V((S * z.Kt, D), BF16),
             V((S * L, D), BF16),
             V((T, S, L, I), BF16),
             V((T, max(S, 8), z.q), F32),
-            V((T, S * L, I), BF16),
-            V((T, S * z.Kt, 2 * I), BF16),
-            V((T * S, z.Kt, z.q), F32),
-            V((S * z.Kt, T * 2 * I), BF16),
+            V((S * L, T * I), BF16),
+            V((S * z.Kt, T * I), BF16),
+            V((S * z.Kt, T * I), BF16),
+            V((max(T // z.G * S, 2 * D // BLOCK), z.Kt, z.G * z.q), F32),
+            V((max(z.K, S * z.Kt), max(S, T) * 2 * I), BF16),
             V((S * L, D), F32),
             V((S * L, D), BF16),
             V((S * L, F), BF16),
@@ -857,7 +897,6 @@
             V((max(C - 1, 1), T, R, 3 * I), BF16),
             V((T - 1, R, I), BF16),
             V((T - 1, R, 3 * I), BF16),
-            V((z.Kt, D), F32),
             V((S * z.Lt, D), F32),
             V((2, 8, D), F32),
             V((8, D), F32),
@@ -886,11 +925,11 @@
                 shape((R, F), F32),
                 shape((8, D), F32),
             ],
-            in_specs=[pl.BlockSpec(memory_space=pltpu.SMEM), hbm] + [vmem] * 12,
+            in_specs=[pl.BlockSpec(memory_space=pltpu.SMEM), hbm] + [vmem] * 14,
             out_specs=[vmem, hbm] + [vmem] * 6,
             scratch_shapes=scratch,
             compiler_params=pltpu.CompilerParams(
-                collective_id=0, has_side_effects=True, vmem_limit_bytes=60 * 1024 * 1024
+                collective_id=0, has_side_effects=True, vmem_limit_bytes=63 * 1024 * 1024
             ),
             name="resampler_layer",
         )(
@@ -904,30 +943,35 @@
             row(latent_shift),
             row(feed_gain),
             row(feed_shift),
-            wqkv,
-            wo,
+            query_weight,
+            key_weight,
+            value_weight,
+            output_weight,
             up_weight,
-            down_weight.T,
+            down_weight,
         )
-        new_latents, media_grad, latent_grad, g_qkv, g_o, g_up, g_dn, g_vec = outs
-        own = lax.dynamic_slice_in_dim(g_vec, lax.axis_index("dp") * R, R, 1)
-        return (
-            new_latents,
-            media_grad,
-            latent_grad,
-            g_qkv[:, :I],
-            g_qkv[:, I : 2 * I],
-            g_qkv[:, 2 * I :],
-            g_o.T,
-            g_up,
-            g_dn.T,
-            g_vec[0],
-            g_vec[1],
-            own[2],
-            own[3],
-            own[4],
-            own[5],
-        )
+        final = pl.pallas_call(
+            functools.partial(hand_out, z),
+            out_shape=[
+                shape((S, L, D), BF16),
+                shape((S, z.Mt, D), BF16),
+                shape((S, L, D), BF16),
+                shape((R, I), F32),
+                shape((R, I), F32),
+                shape((R, I), F32),
+                shape((I, R), F32),
+                shape((R, F), F32),
+                shape((F, R), F32),
+                shape((1, D), F32),
+                shape((1, D), F32),
+            ]
+            + [shape((1, R), F32)] * 4,
+            in_specs=[vmem, hbm] + [vmem] * 6,
+            out_specs=[vmem, hbm] + [vmem] * 13,
+            scratch_shapes=[V((S, z.Mt, D), BF16), pltpu.SemaphoreType.DMA((S,)), pltpu.SemaphoreType.DMA((S,))],
+            name="hand_out",
+        )(*outs)
+        return tuple(final[:9]) + tuple(v.reshape(-1) for v in final[9:])
 
     placed = (
         P("dp", None, None),

time: 181 us -> 134 us (0.74)
  Pallas kernels: 161 us -> 131 us
  local copies, waits for them, and re-layouts: 16.5 us -> 0 us
  other arithmetic: 2.09 us -> 0 us
    pallas_call x1, Pallas kernels: 161 us -> 125 us  [on_device(): pl.pallas_call(functools.partial(layer_kernel, z), out_shape=[shape((S, L...]
    unnamed x13 -> x0, local copies, waits for them, and re-layouts: 10.3 us -> none
    pallas_call x0 -> x1, Pallas kernels: none -> 5.68 us  [on_device(): pl.pallas_call(functools.partial(hand_out, z), out_shape=[shape((S, L, D)...]
    slice x2 -> x0, local copies, waits for them, and re-layouts: 3.02 us -> none  [the longest x1 1.58 us: on_device(): g_qkv[:, 2 * I:]]
    concatenate x1 -> x0, other arithmetic: 2.09 us -> none  [on_device(): jnp.concatenate([query_weight, key_weight, value_weight], axis=1)]
where the time goes in v2:
time: 134 us; the launch traced here: 132 us
  Pallas kernels  131 us (98%)
    pallas_call x1, Pallas kernels, on_device(): pl.pallas_call(functools.partial(layer_kernel, z), out_shape=[shape((S, L...  125 us
    pallas_call x1, Pallas kernels, on_device(): pl.pallas_call(functools.partial(hand_out, z), out_shape=[shape((S, L, D)...  5.68 us

profile of v2, /device:TPU:0, one launch (start us, length us, event | category | flops | bytes accessed | tf_op | source)
XLA Modules:
  0.0 131.9 jit_solution(2129761709536104843)
XLA Ops:
  0.7 125.4 %resampler_layer.1 = (bf16[4,64,1024]{2,1,0:T(8,128)(2,1)}, bf16[4,320,1024]{2,1,0:T(8,128)(2,1)}, bf16[4,64,1024]{2,1,0:T(8,128)(2,1)}, f32[128,384]{1,0:T(8,12...) custom-call(s32[4]{0:T(128)} %counts.1, ...), custom_call_target="tpu_custom_call" | custom-call | tf_op jit(solution)/shard_map/resampler_layer/pallas_call | solution.py:916
  126.0 5.7 %hand_out.1 = (bf16[4,64,1024]{2,1,0:T(8,128)(2,1)}, bf16[4,320,1024]{2,1,0:T(8,128)(2,1)}, bf16[4,64,1024]{2,1,0:T(8,128)(2,1)}, f32[128,128]{1,0:T(8,128)}, f3...) custom-call(bf16[4,64,1024]{2,1,0:T(8,128)(2,1)} %get-tuple-element., ...), custom_call_target="tpu_custom_call" | custom-call | tf_op jit(solution)/shard_map/hand_out/pallas_call | solution.py:953

commit v3 on v2

--- a/solution.py
+++ b/solution.py
@@ -131,6 +131,8 @@
     xr_dn,
     xr_o,
     xr_qkv,
+    zb_o,
+    zb_qkv,
     zr_o,
     zr_qkv,
     mgl,
@@ -151,25 +153,38 @@
     T, N, C, S, L, M, D = z.T, z.N, z.C, z.S, z.L, z.M, z.D
     F, I, R, Lt, Mt, Kt, G = z.F, z.I, z.R, z.Lt, z.Mt, z.Kt, z.G
     GI = G * I
+    groups = T // G
     scale_factor = HEAD_DIM ** (-0.5)
     t = lax.axis_index("tensor")
     d = lax.axis_index("dp")
     c = lax.div(d, 2)
     core = lax.rem(d, 2)
     other = 1 - core
-    sib = d + 1 - 2 * core
     n = BLOCK // (2 * R)
+    blocks = D // BLOCK
+    count = {"z": 0, "x": 0, "c": 0}
+    started = []
+
+    def row(kind):
+        count[kind] += 1
+        return count[kind] - 1
+
+    def start(copies):
+        for copy in copies:
+            copy.start()
+        started.extend(copies)
+
+    def arrive(copies):
+        for copy in copies:
+            copy.wait_recv()
 
     def z_dev(k):
         return (d, lax.rem(t + k, T))
 
-    def x_chip(j):
-        return lax.rem(c + j, C)
-
     def x_dev(j):
-        return (2 * x_chip(j) + core, t)
-
-    core_dev = (sib, t)
+        return (2 * lax.rem(c + j, C) + core, t)
+
+    core_dev = (d + 1 - 2 * core, t)
 
     def head(k):
         return lax.rem(t - k + T, T)
@@ -182,35 +197,99 @@
             src_ref=src, dst_ref=dst, send_sem=send, recv_sem=recv, device_id=dev, device_id_type=MESH
         )
 
-    def over_chips(body):
-        lax.fori_loop(1, C, lambda j, carry: (body(j), carry)[1], 0)
-
-    def gather_z(i, buf):
-        return [
-            remote(buf.at[0, c, core], buf.at[k, c, core], zs.at[i, k - 1], zr.at[i, k - 1], z_dev(k))
+    def over_z(pick):
+        i = row("z")
+        return [remote(*pick(k), zs.at[i, k - 1], zr.at[i, k - 1], z_dev(k)) for k in range(1, T)]
+
+    def share_rows(pick):
+        out = over_z(lambda k: (pick(my_rows()), pick(my_rows())))
+        i = count["z"] - 1
+        came = [
+            remote(pick(my_rows(T - k)), pick(my_rows(T - k)), zs.at[i, k - 1], zr.at[i, k - 1], z_dev(k))
             for k in range(1, T)
         ]
-
-    def gather_x(i, src, dst):
-        def one(j):
-            return remote(src, dst, xs.at[i, j - 1], xr.at[i, j - 1], x_dev(j))
-
-        return one
-
-    wo_z = gather_z(0, wo_b)
-    wq_z = gather_z(1, wq_b)
-    wo_x = gather_x(0, wo_b.at[pl.ds(1, T - 1), c, core], wo_b.at[pl.ds(1, T - 1), c, core])
-    wq_x = gather_x(1, wq_b.at[pl.ds(1, T - 1), c, core], wq_b.at[pl.ds(1, T - 1), c, core])
-    up_x = gather_x(2, up, up_b.at[c, core])
-    dn_x = gather_x(3, dn_b.at[c, core], dn_b.at[c, core])
-
-    def relay(i, ref):
-        return remote(ref, ref, cs.at[i], cr.at[i], core_dev)
-
-    wo_c = relay(0, wo_b.at[pl.ds(1, T - 1), :, core])
-    wq_c = relay(1, wq_b.at[pl.ds(1, T - 1), :, core])
-    up_c = relay(2, up_b.at[:, core])
-    dn_c = relay(3, dn_b.at[:, core])
+        return out, came
+
+    def line_share(pick):
+        ways = []
+        for step in (1, -1):
+            i = row("z")
+            hops = []
+            for h in range(1, T):
+                owner, fresh = t - step * (h - 1), t - step * h
+                beyond = t + step
+                sends = (owner >= 0) & (owner < T) & (beyond >= 0) & (beyond < T)
+                comes = (fresh >= 0) & (fresh < T)
+                mine, theirs = pick(my_rows(T - step * (h - 1))), pick(my_rows(T - step * h))
+                dev = (d, lax.rem(t + step + T, T))
+                sems = (zs.at[i, h - 1], zr.at[i, h - 1])
+                hops.append((sends, remote(mine, mine, *sems, dev), comes, remote(theirs, theirs, *sems, dev)))
+            ways.append(hops)
+
+        def hop(h, last=False):
+            if h >= T and not last:
+                return
+            for hops in ways:
+                if h > 1:
+                    pl.when(hops[h - 2][2])(hops[h - 2][3].wait_recv)
+                if h < T:
+                    pl.when(hops[h - 1][0])(hops[h - 1][1].start)
+
+        def end():
+            hop(T, last=True)
+            for hops in ways:
+                for sends, copy, _, _ in hops:
+                    pl.when(sends)(copy.wait_send)
+
+        return hop, end
+
+    def over_core(src, dst):
+        i = row("c")
+        return [remote(src, dst, cs.at[i], cr.at[i], core_dev)]
+
+    bits = C.bit_length() - 1
+    x_first = list(range(bits))
+    y_first = x_first[::-1]
+
+    def flip(chip, mask):
+        for bit in range(bits):
+            if mask >> bit & 1:
+                chip = chip + (1 - 2 * lax.rem(lax.div(chip, 1 << bit), 2)) * (1 << bit)
+        return chip
+
+    def subsets(order):
+        masks = [0]
+        for bit in order:
+            masks = masks + [m | 1 << bit for m in masks]
+        return masks
+
+    def gather_steps(view, order):
+        i, at, steps = row("x"), 0, []
+        for step, bit in enumerate(order):
+            peer = flip(c, 1 << bit)
+            dev = (2 * peer + core, t)
+            out, came = [], []
+            for m in subsets(order[:step]):
+                sems = (xs.at[i, at], xr.at[i, at])
+                mine, theirs = view(flip(c, m)), view(flip(peer, m))
+                out.append(remote(mine, mine, *sems, dev))
+                came.append(remote(theirs, theirs, *sems, dev))
+                at += 1
+            steps.append((out, came))
+        return steps
+
+    def scatter_steps(view, land, order):
+        i, at, steps = row("x"), 0, []
+        for step, bit in enumerate(order):
+            peer = flip(c, 1 << bit)
+            dev = (2 * peer + core, t)
+            out, keep = [], []
+            for m in subsets(order[step + 1 :]):
+                out.append(remote(view(flip(peer, m)), land(at), xs.at[i, at], xr.at[i, at], dev))
+                keep.append((flip(c, m), at))
+                at += 1
+            steps.append((out, keep))
+        return steps
 
     n_tiles = S * T
 
@@ -226,28 +305,45 @@
     )
     for i in range(min(SLOTS_IN_FLIGHT, n_tiles)):
         tile_copy(i).start()
-    own_copy.start()
-
+    barrier = pltpu.get_barrier_semaphore()
+
+    def greet(dev):
+        pl.semaphore_signal(barrier, inc=1, device_id=dev, device_id_type=MESH)
+
+    for k in range(1, T):
+        greet(z_dev(k))
+    lax.fori_loop(1, C, lambda j, carry: (greet(x_dev(j)), carry)[1], 0)
+    greet(core_dev)
+    up_b[c, core] = up[...]
+    dn_b[c, core] = dn[...].T
     wo_b[0] = wo[...].T.reshape(C, 2, R, I)
     for m, weight in enumerate((wq, wk, wv)):
         wq_b[0, :, :, :, pl.ds(m * I, I)] = weight[...].reshape(C, 2, R, I)
-    up_b[c, core] = up[...]
-    dn_b[c, core] = dn[...].T
-    barrier = pltpu.get_barrier_semaphore()
-
-    def greet(dev):
-        pl.semaphore_signal(barrier, inc=1, device_id=dev, device_id_type=MESH)
-
-    for k in range(1, T):
-        greet(z_dev(k))
-    over_chips(lambda j: greet(x_dev(j)))
-    greet(core_dev)
     pl.semaphore_wait(barrier, T + C - 1)
 
-    for copy in wo_z + wq_z:
-        copy.start()
-    over_chips(lambda j: up_x(j).start())
-    over_chips(lambda j: dn_x(j).start())
+    foreign = pl.ds(1, T - 1)
+    up_x = gather_steps(lambda chip: up_b.at[chip, core], x_first)
+    dn_x = gather_steps(lambda chip: dn_b.at[chip, core], y_first)
+    wo_x = gather_steps(lambda chip: wo_b.at[foreign, chip, core], x_first)
+    qk_x = gather_steps(lambda chip: wq_b.at[foreign, chip, core, :, pl.ds(0, 2 * I)], x_first)
+    v_x = gather_steps(lambda chip: wq_b.at[foreign, chip, core, :, pl.ds(2 * I, I)], y_first)
+    wo_z = over_z(lambda k: (wo_b.at[0, c, core], wo_b.at[k, c, core]))
+    wq_z = over_z(lambda k: (wq_b.at[0, c, core], wq_b.at[k, c, core]))
+    up_c = over_core(up_b.at[:, core], up_b.at[:, core])
+    dn_c = over_core(dn_b.at[:, core], dn_b.at[:, core])
+    wo_c = over_core(wo_b.at[foreign, :, core], wo_b.at[foreign, :, core])
+    wq_c = over_core(wq_b.at[foreign, :, core], wq_b.at[foreign, :, core])
+
+    def gather_rest(steps):
+        for step in range(1, len(steps)):
+            arrive(steps[step - 1][1])
+            start(steps[step][0])
+
+    start(up_x[0][0])
+    start(dn_x[0][0])
+    start(wo_z)
+    start(wq_z)
+    own_copy.start()
 
     for b in range(S * L // ROWS):
         rows = pl.ds(b * ROWS, ROWS)
@@ -304,22 +400,17 @@
         tile_norm(lax.rem(i + 2, n_tiles), 0)
         tile_next(i + 1)
         tile_next(i + 2)
-
-        @pl.when(j == n_tiles // 8)
-        def _():
-            for copy in wo_z:
-                copy.wait_recv()
-            over_chips(lambda j: wo_x(j).start())
-
-        @pl.when(j == n_tiles // 4)
-        def _():
-            for copy in wq_z:
-                copy.wait_recv()
-            over_chips(lambda j: wq_x(j).start())
-
         return carry
 
-    lax.fori_loop(0, n_tiles // 2, two_tiles, 0)
+    first, second = n_tiles // 8, 3 * n_tiles // 8
+    lax.fori_loop(0, first, two_tiles, 0)
+    arrive(wo_z)
+    start(wo_x[0][0])
+    lax.fori_loop(first, second, two_tiles, 0)
+    gather_rest(up_x)
+    gather_rest(dn_x)
+    lax.fori_loop(second, n_tiles // 2, two_tiles, 0)
+    gather_rest(wo_x)
 
     def spread(x):
         lane_head = lax.broadcasted_iota(jnp.int32, (1, x.shape[1]), 1) // HEAD_DIM
@@ -335,6 +426,7 @@
             out = jnp.where(lane_head == h, x[h * L : (h + 1) * L], out)
         return out
 
+    att_z = []
     for s in range(S):
         keys = pairs[pl.ds(0, z.K), pl.ds(s * 2 * I, I)]
         values = pairs[pl.ds(0, z.K), pl.ds(s * 2 * I + I, I)]
@@ -347,26 +439,35 @@
         probs = jnp.exp(scores - total).astype(BF16)
         att[0, s] = gather_heads(tn(probs, values)).astype(BF16)
         lse[0, pl.ds(s, 1), :] = total
-
-    att_z = [remote(att.at[0], att.at[k], zs.at[2, k - 1], zr.at[2, k - 1], z_dev(k)) for k in range(1, T)]
-    lse_z = [remote(lse.at[0], lse.at[k], zs.at[3, k - 1], zr.at[3, k - 1], z_dev(k)) for k in range(1, T)]
-    for copy in att_z + lse_z:
-        copy.start()
-
-    over_chips(lambda j: wo_x(j).wait_recv())
-    wo_c.start()
-    over_chips(lambda j: up_x(j).wait_recv())
-    up_c.start()
-    over_chips(lambda j: dn_x(j).wait_recv())
-    dn_c.start()
-
-    wo_c.wait_recv()
-    for copy in att_z:
-        copy.wait_recv()
+        if s % 2 == 1:
+            now = over_z(lambda k, s=s: (att.at[0, pl.ds(s - 1, 2)], att.at[k, pl.ds(s - 1, 2)]))
+            start(now)
+            att_z += now
+    lse_z = over_z(lambda k: (lse.at[0], lse.at[k]))
+    start(lse_z)
+
+    for s in range(S):
+        lanes = s * 2 * I
+        own_slots = pl.ds(pl.multiple_of(t * Mt, Mt), Mt)
+        own_lat = pl.ds(pl.multiple_of(M + t * Lt, Lt), Lt)
+        for m, ref in enumerate((kall, vall)):
+            ref[pl.ds(s * Kt, Mt), pl.ds(0, I)] = pairs[own_slots, pl.ds(lanes + m * I, I)]
+            ref[pl.ds(s * Kt + Mt, Lt), pl.ds(0, I)] = pairs[own_lat, pl.ds(lanes + m * I, I)]
+    arrive(wo_x[-1][1])
+    start(wo_c)
+    arrive(up_x[-1][1])
+    start(up_c)
+    arrive(dn_x[-1][1])
+    start(dn_c)
+    arrive(wq_z)
+    start(qk_x[0][0])
+    start(v_x[0][0])
 
     def heads_wo():
         return jnp.concatenate([wo_b[k].reshape(D, I) for k in range(T)], axis=1)
 
+    arrive(wo_c)
+    arrive(att_z)
     att_all = jnp.concatenate([att[k].reshape(S * L, I) for k in range(T)], axis=1)
     res[...] = lat[...].astype(F32) + nt(att_all, heads_wo())
     for b in range(S * L // ROWS):
@@ -374,8 +475,8 @@
         unit, _ = unit_rows(res[rows, :])
         hin[rows, :] = (unit * fgain[...] + fshift[...]).astype(BF16)
 
-    up_c.wait_recv()
-    dn_c.wait_recv()
+    arrive(up_c)
+    arrive(dn_c)
 
     def feed(b, carry):
         cols = pl.ds(pl.multiple_of(b * BLOCK, BLOCK), BLOCK)
@@ -387,95 +488,63 @@
         bgr[:, cols] = (act_grad.astype(F32) * slope).astype(BF16)
         return carry
 
-    lax.fori_loop(0, F // BLOCK, feed, 0)
-
-    def back_to_width(left, weight, out):
-        def one(b, carry):
-            cols = pl.ds(pl.multiple_of(b * BLOCK, BLOCK), BLOCK)
-            block = nt(left[...], weight[pl.ds(b * n, n)].reshape(BLOCK, F))
-            out[:, :, cols] = block.astype(BF16).reshape(S, L, BLOCK)
-            return carry
-
-        lax.fori_loop(0, D // BLOCK, one, 0)
-
-    back_to_width(bgr, up_b, hg)
-    hg_z = [
-        remote(hg.at[:, my_rows(k)], hgr.at[k - 1], zs.at[4, k - 1], zr.at[4, k - 1], z_dev(k)) for k in range(1, T)
-    ]
-    for copy in hg_z:
-        copy.start()
-    back_to_width(act, dn_b, fp)
-    fp_z = [
-        remote(fp.at[:, my_rows(k)], fpr.at[k - 1], zs.at[5, k - 1], zr.at[5, k - 1], z_dev(k)) for k in range(1, T)
-    ]
-    for copy in fp_z:
-        copy.start()
-
-    def feed_weights(left, right, out):
-        def one(b, carry):
-            cols = pl.ds(pl.multiple_of(b * BLOCK, BLOCK), BLOCK)
-            block = tn(left[:, cols], right[...]).astype(BF16)
-            out[pl.ds(b * n, n)] = block.reshape(n, 2, R, F)
-            return carry
-
-        lax.fori_loop(0, D // BLOCK, one, 0)
-
-    def to_core(i, src, dst):
-        return remote(src, dst, cs.at[i], cr.at[i], core_dev)
-
-    feed_weights(hin, bgr, st_up)
-    st_up_c = to_core(4, st_up.at[:, other], cr_up)
-    st_up_c.start()
-    feed_weights(cot, act, st_dn)
-    st_dn_c = to_core(5, st_dn.at[:, other], cr_dn)
-    st_dn_c.start()
-
-    over_chips(lambda j: wq_x(j).wait_recv())
-    wq_c.start()
-
-    own_copy.wait()
-    wq_c.wait_recv()
-
-    for k in range(1, T):
-        qall[:, pl.ds(k * I, I)] = nn(latn[...], wq_b[k, :, :, :, pl.ds(0, I)].reshape(D, I)).astype(BF16)
-    half_rows = S * Kt // 2
-
-    def all_pairs(i, carry):
-        k = lax.div(i, 2)
-        rows = pl.ds(pl.multiple_of(lax.rem(i, 2) * half_rows, 16), half_rows)
-        lanes = pl.ds(pl.multiple_of(k * I, I), I)
-        pair = nn(ctx[rows, :], wq_b[k, :, :, :, pl.ds(I, 2 * I)].reshape(D, 2 * I)).astype(BF16)
-        kall[rows, lanes] = pair[:, :I]
-        vall[rows, lanes] = pair[:, I:]
-        return carry
-
-    lax.fori_loop(0, 2 * T, all_pairs, 0)
-    for copy in lse_z:
-        copy.wait_recv()
-    slot_of = lax.broadcasted_iota(jnp.int32, (Kt, 1), 0)
-
-    def group(i):
-        g, s = lax.div(i, S), lax.rem(i, S)
-        rows = pl.ds(pl.multiple_of(s * Kt, 16), Kt)
-        lanes = pl.ds(pl.multiple_of(g * GI, GI), GI)
-        lat_rows = pl.ds(pl.multiple_of(s * L, L), L)
-        return g, s, rows, lanes, lat_rows
-
-    def joined(g, pick):
-        return jnp.concatenate([pick(g * G + j) for j in range(G)], axis=1)
-
-    def probabilities(i, carry):
-        g, s, rows, lanes, lat_rows = group(i)
-        scores = nt(kall[rows, lanes], spread(qall[lat_rows, lanes])) * scale_factor
-        valid = (slot_of + t * Mt < counts[s] * PATCH) | (slot_of >= Mt)
-        scores = jnp.where(valid, scores, NEGATIVE)
-        pall[i] = jnp.exp(scores - joined(g, lambda k: lse[k, pl.ds(s, 1), :]))
-        return carry
-
-    lax.fori_loop(0, T // G * S, probabilities, 0, unroll=2)
-
-    for copy in hg_z:
-        copy.wait_recv()
+    lax.fori_loop(0, F // BLOCK, feed, 0, unroll=2)
+
+    def back_to_width(left, weight, out, b):
+        block = nt(left[...], weight[pl.ds(b * n, n)].reshape(BLOCK, F))
+        out[:, :, pl.ds(b * BLOCK, BLOCK)] = block.astype(BF16).reshape(S, L, BLOCK)
+
+    hg_z = []
+    for b in range(blocks):
+        cols = pl.ds(b * BLOCK, BLOCK)
+        back_to_width(bgr, up_b, hg, b)
+        now = over_z(lambda k, cols=cols: (hg.at[:, my_rows(k), cols], hgr.at[k - 1, :, :, cols]))
+        start(now)
+        hg_z += now
+    gather_rest(qk_x)
+    gather_rest(v_x)
+
+    def feed_weights(left, right, out, b):
+        block = tn(left[:, pl.ds(b * BLOCK, BLOCK)], right[...]).astype(BF16)
+        out[pl.ds(b * n, n)] = block.reshape(n, 2, R, F)
+
+    for b in range(blocks):
+        feed_weights(hin, bgr, st_up, b)
+    st_up_c = over_core(st_up.at[:, other], cr_up)
+    start(st_up_c)
+    for b in range(blocks):
+        feed_weights(cot, act, st_dn, b)
+    st_dn_c = over_core(st_dn.at[:, other], cr_dn)
+    start(st_dn_c)
+    for b in range(blocks):
+        back_to_width(act, dn_b, fp, b)
+
+    up_g = scatter_steps(lambda chip: st_up.at[chip, core], lambda at: xr_up.at[at], y_first)
+    dn_g = scatter_steps(lambda chip: st_dn.at[chip, core], lambda at: xr_dn.at[at], x_first)
+
+    def feed_core(copy, st, came, steps):
+        arrive(copy)
+        sent = steps[0][0]
+        for m in subsets(range(bits)):
+            chip = flip(c, m)
+            st[chip, core] = (st[chip, core].astype(F32) + came[chip].astype(F32)).astype(BF16)
+        start(sent)
+
+    def feed_step(st, land, steps):
+        for step in range(1, len(steps)):
+            arrive(steps[step - 1][0])
+            for chip, at in steps[step - 1][1]:
+                st[chip, core] = (st[chip, core].astype(F32) + land[at].astype(F32)).astype(BF16)
+            start(steps[step][0])
+
+    def feed_last(st, land, steps, out):
+        arrive(steps[-1][0])
+        out[...] = st[c, core].astype(F32) + land[steps[-1][1][0][1]].astype(F32)
+
+    feed_core(st_up_c, st_up, cr_up, up_g)
+    feed_core(st_dn_c, st_dn, cr_dn, dn_g)
+
+    arrive(hg_z)
     feed_gain_part = jnp.zeros((1, D), F32)
     feed_shift_part = jnp.zeros((1, D), F32)
     for s in range(S):
@@ -489,80 +558,114 @@
         feed_shift_part = feed_shift_part + jnp.sum(upstream, axis=0, keepdims=True)
         rgr[pl.ds(s * Lt, Lt), :] = back
         og[pl.ds(s * Lt, Lt), :] = back.astype(BF16)
+    vst[...] = jnp.concatenate(
+        [jnp.zeros((4, D), F32), feed_gain_part, feed_shift_part, jnp.zeros((2, D), F32)], axis=0
+    )
     grads_all = nn(og[...], heads_wo()).astype(BF16)
     for k in range(T):
         dob[head(k), :, my_rows(), :] = grads_all[:, k * I : (k + 1) * I].reshape(S, Lt, I)
-    do_z = [
-        remote(
-            dob.at[:, :, my_rows(), :], dob.at[:, :, my_rows(), :], zs.at[6, k - 1], zr.at[6, k - 1], z_dev(k)
-        )
-        for k in range(1, T)
-    ]
-    do_in = [
-        remote(
-            dob.at[:, :, my_rows(T - k), :],
-            dob.at[:, :, my_rows(T - k), :],
-            zs.at[6, k - 1],
-            zr.at[6, k - 1],
-            z_dev(k),
-        )
-        for k in range(1, T)
-    ]
-    for copy in do_z:
-        copy.start()
+    do_z, do_in = share_rows(lambda rows: dob.at[:, :, rows, :])
+    start(do_z)
 
     att_own = jnp.concatenate([att[k, :, my_rows(), :].reshape(S * Lt, I) for k in range(T)], axis=1)
-    for b in range(D // BLOCK):
+    for b in range(blocks):
         block = tn(og[:, pl.ds(b * BLOCK, BLOCK)], att_own).astype(BF16)
         for k in range(T):
             st_o[k, pl.ds(b * n, n)] = block[:, k * I : (k + 1) * I].reshape(n, 2, R, I)
-    st_o_c = to_core(6, st_o.at[:, :, other], cr_o)
-    st_o_c.start()
-
-    def plane_feed(i, arrive, st, came, land):
-        arrive.wait_recv()
-
-        def add(chip):
-            st[chip, core] = (st[chip, core].astype(F32) + came[chip].astype(F32)).astype(BF16)
-
-        def copy(j):
-            return remote(st.at[x_chip(j), core], land.at[j - 1], xs.at[i, j - 1], xr.at[i, j - 1], x_dev(j))
-
-        def one(j):
-            add(x_chip(j))
-            copy(j).start()
-
-        over_chips(one)
-        add(c)
-        return copy
-
-    def plane_heads(i, arrive, st, came, land):
-        arrive.wait_recv()
-
-        def add(chip):
-            for k in range(T):
+    st_o_c = over_core(st_o.at[:, :, other], cr_o)
+    start(st_o_c)
+
+    arrive(qk_x[-1][1])
+    arrive(v_x[-1][1])
+    start(wq_c)
+    own_copy.wait()
+    arrive(wq_c)
+    for k in range(1, T):
+        qall[:, pl.ds(k * I, I)] = nn(latn[...], wq_b[k, :, :, :, pl.ds(0, I)].reshape(D, I)).astype(BF16)
+    half_rows = S * Kt // 2
+
+    def all_pairs(i, carry):
+        k = lax.div(i, 2)
+        rows = pl.ds(pl.multiple_of(lax.rem(i, 2) * half_rows, 16), half_rows)
+        lanes = pl.ds(pl.multiple_of(k * I, I), I)
+        pair = nn(ctx[rows, :], wq_b[k, :, :, :, pl.ds(I, 2 * I)].reshape(D, 2 * I)).astype(BF16)
+        kall[rows, lanes] = pair[:, :I]
+        vall[rows, lanes] = pair[:, I:]
+        return carry
+
+    lax.fori_loop(2, 2 * T, all_pairs, 0)
+    arrive(lse_z)
+    slot_of = lax.broadcasted_iota(jnp.int32, (Kt, 1), 0)
+
+    def group(g, s):
+        rows = pl.ds(pl.multiple_of(s * Kt, 16), Kt)
+        lat_rows = pl.ds(pl.multiple_of(s * L, L), L)
+        return rows, pl.ds(g * GI, GI), lat_rows
+
+    def joined(g, pick):
+        return jnp.concatenate([pick(g * G + j) for j in range(G)], axis=1)
+
+    for g in range(groups):
+
+        def probabilities(s, carry, g=g):
+            rows, lanes, lat_rows = group(g, s)
+            scores = nt(kall[rows, lanes], spread(qall[lat_rows, lanes])) * scale_factor
+            valid = (slot_of + t * Mt < counts[s] * PATCH) | (slot_of >= Mt)
+            scores = jnp.where(valid, scores, NEGATIVE)
+            pall[g * S + s] = jnp.exp(scores - joined(g, lambda k: lse[k, pl.ds(s, 1), :]))
+            return carry
+
+        lax.fori_loop(0, S, probabilities, 0, unroll=2)
+
+    def heads_core(st, came, ks, steps):
+        for m in subsets(range(bits)):
+            chip = flip(c, m)
+            for k in ks:
                 st[k, chip, core] = (st[k, chip, core].astype(F32) + came[k, chip].astype(F32)).astype(BF16)
-
-        def copy(j):
-            return remote(st.at[:, x_chip(j), core], land.at[j - 1], xs.at[i, j - 1], xr.at[i, j - 1], x_dev(j))
-
-        def one(j):
-            add(x_chip(j))
-            copy(j).start()
-
-        over_chips(one)
-        add(c)
-        return copy
-
-    x_up = plane_feed(4, st_up_c, st_up, cr_up, xr_up)
-    x_dn = plane_feed(5, st_dn_c, st_dn, cr_dn, xr_dn)
-
-    for copy in do_in:
-        copy.wait_recv()
-
-    def attend_back(i, carry):
-        g, s, rows, lanes, lat_rows = group(i)
-        values_at = pl.ds(pl.multiple_of(T * I + g * GI, GI), GI)
+        start(steps[0][0])
+
+    def heads_step(st, land, ks, steps):
+        for step in range(1, len(steps)):
+            arrive(steps[step - 1][0])
+            for chip, at in steps[step - 1][1]:
+                for j, k in enumerate(ks):
+                    st[k, chip, core] = (st[k, chip, core].astype(F32) + land[at, j].astype(F32)).astype(BF16)
+            start(steps[step][0])
+
+    def heads_last(st, land, ks, steps, held, came):
+        arrive(steps[-1][0])
+        at = steps[-1][1][0][1]
+        for j, k in enumerate(ks):
+            held[k] = (st[k, c, core].astype(F32) + land[at, j].astype(F32)).astype(BF16)
+        i = row("z")
+        copies = [
+            remote(held.at[k], came.at[T - k - 1], zs.at[i, k - 1], zr.at[i, T - k - 1], (d, head(k)))
+            for k in ks
+            if k
+        ]
+        start(copies)
+        return copies
+
+    orders = (x_first, y_first)
+    o_heads = [range(g * T // 2, (g + 1) * T // 2) for g in range(2)]
+    o_steps = [
+        scatter_steps(
+            lambda chip, g=g: st_o.at[pl.ds(g * T // 2, T // 2), chip, core], lambda at, g=g: xr_o.at[g, at], orders[g]
+        )
+        for g in range(2)
+    ]
+    arrive(st_o_c)
+    for g in range(2):
+        heads_core(st_o, cr_o, o_heads[g], o_steps[g])
+
+    arrive(do_in)
+    fp_z = over_z(lambda k: (fp.at[:, my_rows(k)], fpr.at[k - 1]))
+    start(fp_z)
+    feed_step(st_up, xr_up, up_g)
+    feed_step(st_dn, xr_dn, dn_g)
+
+    def attend_back(s, carry, g):
+        rows, lanes, lat_rows = group(g, s)
         keys = kall[rows, lanes]
         queries = spread(qall[lat_rows, lanes])
         grads = spread(joined(g, lambda k: dob[head(k), s]))
@@ -575,73 +678,71 @@
             preferred_element_type=F32,
             precision=lax.Precision.HIGHEST,
         )[:1]
-        probs = pall[i]
+        probs = pall[g * S + s]
         score_grad = (probs * (nt(vall[rows, lanes], grads) - inner)).astype(BF16)
         pairs[rows, lanes] = (nn(score_grad, queries) * scale_factor).astype(BF16)
-        pairs[rows, values_at] = nn(probs.astype(BF16), grads).astype(BF16)
+        pairs[rows, pl.ds(T * I + g * GI, GI)] = nn(probs.astype(BF16), grads).astype(BF16)
         query_grad = (gather_heads(tn(score_grad, keys)) * scale_factor).astype(BF16)
         for j in range(G):
-            dqb[head(g * G + j), s] = query_grad[:, j * I : (j + 1) * I]
+            dqb[g * G + j, s] = query_grad[:, j * I : (j + 1) * I]
         return carry
 
-    lax.fori_loop(0, T // G * S, attend_back, 0, unroll=2)
-    dq_z = [
-        remote(
-            dqb.at[:, :, my_rows(k), :], dqr.at[k - 1], zs.at[7, k - 1], zr.at[7, k - 1], z_dev(k)
+    def group_weights(g):
+        query_part = jnp.concatenate([dqb[g * G + j].reshape(S * L, I) for j in range(G)], axis=1)
+        all_rows = pl.ds(0, S * Kt)
+        part = jnp.concatenate(
+            [pairs[all_rows, pl.ds(g * GI, GI)], pairs[all_rows, pl.ds(T * I + g * GI, GI)]], axis=1
         )
-        for k in range(1, T)
+        for b in range(blocks):
+            cols = pl.ds(b * BLOCK, BLOCK)
+            block = tn(ctx[:, cols], part).astype(BF16)
+            query_block = tn(latn[:, cols], query_part).astype(BF16)
+            for j in range(G):
+                lanes = slice(j * I, (j + 1) * I)
+                pieces = (query_block[:, lanes], block[:, lanes], block[:, GI:][:, lanes])
+                for m, piece in enumerate(pieces):
+                    st_qkv[g * G + j, pl.ds(b * n, n), :, :, pl.ds(m * I, I)] = piece.reshape(n, 2, R, I)
+        ks = pl.ds(g * G, G)
+        copy = over_core(st_qkv.at[ks, :, other], cr_qkv.at[ks])
+        start(copy)
+        return copy
+
+    q_steps = [
+        scatter_steps(lambda chip, k=k: st_qkv.at[pl.ds(k, 1), chip, core], lambda at, k=k: xr_qkv.at[k, at], orders[k % 2])
+        for k in range(T)
     ]
-    for copy in dq_z:
-        copy.start()
-
-    dq_all = jnp.concatenate([dqb[head(k)].reshape(S * L, I) for k in range(T)], axis=1)
-    for b in range(D // BLOCK):
-        cols = pl.ds(b * BLOCK, BLOCK)
-        block = tn(ctx[:, cols], pairs[pl.ds(0, S * Kt), pl.ds(0, 2 * T * I)]).astype(BF16)
-        query_block = tn(latn[:, cols], dq_all).astype(BF16)
-        for k in range(T):
-            lanes = slice(k * I, (k + 1) * I)
-            parts = (query_block[:, lanes], block[:, lanes], block[:, T * I :][:, lanes])
-            for m, part in enumerate(parts):
-                st_qkv[k, pl.ds(b * n, n), :, :, pl.ds(m * I, I)] = part.reshape(n, 2, R, I)
-    st_qkv_c = to_core(7, st_qkv.at[:, :, other], cr_qkv)
-    st_qkv_c.start()
-    x_o = plane_heads(6, st_o_c, st_o, cr_o, xr_o)
-    x_qkv = plane_heads(7, st_qkv_c, st_qkv, cr_qkv, xr_qkv)
-
-    for copy in fp_z:
-        copy.wait_recv()
-    for s in range(S):
-        own = pl.ds(pl.multiple_of(s * L + t * Lt, Lt), Lt)
-        total = fp[s, my_rows(), :].astype(F32)
-        for k in range(1, T):
-            total = total + fpr[k - 1, s].astype(F32)
-        new_lat[s, my_rows(), :] = (res[own, :] + total).astype(BF16)
-
-    def share_rows(i, ref):
-        out = [
-            remote(ref.at[:, my_rows(), :], ref.at[:, my_rows(), :], zs.at[i, k - 1], zr.at[i, k - 1], z_dev(k))
-            for k in range(1, T)
-        ]
-        came = [
-            remote(
-                ref.at[:, my_rows(T - k), :],
-                ref.at[:, my_rows(T - k), :],
-                zs.at[i, k - 1],
-                zr.at[i, k - 1],
-                z_dev(k),
-            )
-            for k in range(1, T)
-        ]
-        return out, came
-
-    nl_z, nl_in = share_rows(8, new_lat)
-    for copy in nl_z:
-        copy.start()
+    group_heads = [range(g * G, (g + 1) * G) for g in range(groups)]
+    q_c, dq_z = [], []
+
+    def group_core(g):
+        arrive(q_c[g])
+        for k in group_heads[g]:
+            heads_core(st_qkv, cr_qkv, (k,), q_steps[k])
+
+    def group_step(g):
+        for k in group_heads[g]:
+            heads_step(st_qkv, xr_qkv.at[k], (k,), q_steps[k])
+
+    def group_last(g):
+        out = []
+        for k in group_heads[g]:
+            out += heads_last(st_qkv, xr_qkv.at[k], (k,), q_steps[k], zb_qkv, zr_qkv)
+        return out
+
+    for g in range(groups):
+        lax.fori_loop(0, S, functools.partial(attend_back, g=g), 0, unroll=2)
+        for j in range(G):
+            k = g * G + j
+            now = over_z(lambda m, k=k: (dqb.at[k, :, my_rows(m), :], dqr.at[m - 1, (m + k) % T]))
+            start(now)
+            dq_z += now
+        if g:
+            group_core(g - 1)
+        q_c.append(group_weights(g))
+    for g in range(2):
+        heads_step(st_o, xr_o.at[g], o_heads[g], o_steps[g])
 
     acc[...] = jnp.zeros_like(acc)
-
-    blocks = D // BLOCK
 
     def width(s, rows):
         return jnp.concatenate([pall[s % 2 * blocks + b, rows, :] for b in range(blocks)], axis=1)
@@ -674,14 +775,31 @@
         if s + 1 < S:
             media_width(s + 1)
         media_rows(s)
-
-    for copy in dq_z:
-        copy.wait_recv()
+        if s == 0:
+            group_core(groups - 1)
+        if s == S // 2:
+            for g in range(groups - 1):
+                group_step(g)
+
+    arrive(fp_z)
+    for s in range(S):
+        own = pl.ds(pl.multiple_of(s * L + t * Lt, Lt), Lt)
+        total = fp[s, my_rows(), :].astype(F32)
+        for k in range(1, T):
+            total = total + fpr[k - 1, s].astype(F32)
+        new_lat[s, my_rows(), :] = (res[own, :] + total).astype(BF16)
+    nl_hop, nl_end = line_share(lambda rows: new_lat.at[:, rows, :])
+    nl_hop(1)
+    o_z = []
+    for g in range(2):
+        o_z += heads_last(st_o, xr_o.at[g], o_heads[g], o_steps[g], zb_o, zr_o)
+
+    arrive(dq_z)
     upstream_all = mgl[...]
     for k in range(T):
-        total = dqb[head(k), :, my_rows(), :].astype(F32)
+        total = dqb[k, :, my_rows(), :].astype(F32)
         for m in range(1, T):
-            total = total + dqr[m - 1, head(k)].astype(F32)
+            total = total + dqr[m - 1, k].astype(F32)
         weights = wq_b[k, :, :, :, pl.ds(0, I)].reshape(D, I)
         upstream_all = upstream_all + nt(total.astype(BF16).reshape(S * Lt, I), weights)
     mgl[...] = upstream_all
@@ -695,101 +813,66 @@
         lat_grad[s, my_rows(), :] = back.astype(BF16)
         lat_gain_part = lat_gain_part + jnp.sum(upstream * unit, axis=0, keepdims=True)
         lat_shift_part = lat_shift_part + jnp.sum(upstream, axis=0, keepdims=True)
-    lg_z, lg_in = share_rows(9, lat_grad)
-    for copy in lg_z:
-        copy.start()
-
-    vst[...] = jnp.concatenate(
+    lg_hop, lg_end = line_share(lambda rows: lat_grad.at[:, rows, :])
+    lg_hop(1)
+
+    vst[...] += jnp.concatenate(
         [
             jnp.sum(acc[0], axis=0, keepdims=True),
             jnp.sum(acc[1], axis=0, keepdims=True),
             lat_gain_part,
             lat_shift_part,
-            feed_gain_part,
-            feed_shift_part,
-            jnp.zeros((2, D), F32),
+            jnp.zeros((4, D), F32),
         ],
         axis=0,
     )
-    v_c = to_core(8, vst, vcr)
-    v_c.start()
-    v_c.wait_recv()
+    vec_c = over_core(vst, vcr)
+    start(vec_c)
+    arrive(vec_c)
     vx[c] = vst[...] + vcr[...]
-
-    def v_x(j):
-        return remote(vx.at[c], vx.at[c], xs.at[8, j - 1], xr.at[8, j - 1], x_dev(j))
-
-    def v_x_in(j):
-        chip = lax.rem(c - j + C, C)
-        return remote(vx.at[chip], vx.at[chip], xs.at[8, j - 1], xr.at[8, j - 1], x_dev(j))
-
-    over_chips(lambda j: v_x(j).start())
-
-    def sum_heads(x_copy, st, land):
-        over_chips(lambda j: x_copy(j).wait_recv())
-        for k in range(T):
-            total = lax.fori_loop(
-                1, C, lambda j, value, k=k: value + land[j - 1, k].astype(F32), st[k, c, core].astype(F32)
-            )
-            land[0, k] = total.astype(BF16)
-
-    def z_sum(i, land, came):
-        return [
-            remote(land.at[0, k], came.at[T - k - 1], zs.at[i, k - 1], zr.at[i, T - k - 1], (d, head(k)))
-            for k in range(1, T)
-        ]
-
-    sum_heads(x_o, st_o, xr_o)
-    o_z = z_sum(10, xr_o, zr_o)
-    for copy in o_z:
-        copy.start()
-    sum_heads(x_qkv, st_qkv, xr_qkv)
-    q_z = z_sum(11, xr_qkv, zr_qkv)
-    for copy in q_z:
-        copy.start()
-
-    over_chips(lambda j: v_x_in(j).wait_recv())
+    vec_row = row("x")
+
+    def vec_x(j, chip):
+        return remote(vx.at[chip], vx.at[chip], xs.at[vec_row, j - 1], xr.at[vec_row, j - 1], x_dev(j))
+
+    lax.fori_loop(1, C, lambda j, carry: (vec_x(j, c).start(), carry)[1], 0)
+
+    group_step(groups - 1)
+    nl_hop(2)
+    q_z = []
+    for g in range(groups - 1):
+        q_z += group_last(g)
+    feed_last(st_up, xr_up, up_g, g_up)
+    feed_last(st_dn, xr_dn, dn_g, g_dn)
+    lax.fori_loop(1, C, lambda j, carry: (vec_x(j, lax.rem(c - j + C, C)).wait_recv(), carry)[1], 0)
     vz[t] = lax.fori_loop(1, C, lambda j, value: value + vx[j], vx[0])
-    v_z = [remote(vz.at[t], vz.at[t], zs.at[12, k - 1], zr.at[12, k - 1], z_dev(k)) for k in range(1, T)]
-    v_z_in = [
-        remote(vz.at[head(k)], vz.at[head(k)], zs.at[12, k - 1], zr.at[12, k - 1], z_dev(k)) for k in range(1, T)
-    ]
-    for copy in v_z:
-        copy.start()
-
-    def sum_feed(x_copy, st, land, out):
-        over_chips(lambda j: x_copy(j).wait_recv())
-        out[...] = lax.fori_loop(
-            1, C, lambda j, value: value + land[j - 1].astype(F32), st[c, core].astype(F32)
-        )
-
-    sum_feed(x_up, st_up, xr_up, g_up)
-    sum_feed(x_dn, st_dn, xr_dn, g_dn)
-
-    for copy in v_z_in:
-        copy.wait_recv()
+    v_z = over_z(lambda k: (vz.at[t], vz.at[t]))
+    i = count["z"] - 1
+    v_in = [remote(vz.at[head(k)], vz.at[head(k)], zs.at[i, k - 1], zr.at[i, k - 1], z_dev(k)) for k in range(1, T)]
+    start(v_z)
+    lg_hop(2)
+    q_z += group_last(groups - 1)
+    for h in range(3, T):
+        nl_hop(h)
+        lg_hop(h)
+    arrive(v_in)
     g_vec[...] = lax.fori_loop(1, T, lambda k, value: value + vz[k], vz[0])
-    for copy in o_z:
-        copy.wait_recv()
-    total = xr_o[0, 0].astype(F32)
+    arrive(o_z)
+    total = zb_o[0].astype(F32)
     for k in range(1, T):
         total = total + zr_o[k - 1].astype(F32)
     g_o[...] = total
-    for copy in q_z:
-        copy.wait_recv()
-    total = xr_qkv[0, 0].astype(F32)
+    arrive(q_z)
+    total = zb_qkv[0].astype(F32)
     for k in range(1, T):
         total = total + zr_qkv[k - 1].astype(F32)
     g_qkv[...] = total
 
-    for copy in nl_in + lg_in:
-        copy.wait_recv()
-    for copy in wo_z + wq_z + att_z + lse_z + hg_z + fp_z + do_z + dq_z + nl_z + lg_z + o_z + q_z + v_z:
+    nl_end()
+    lg_end()
+    for copy in started:
         copy.wait_send()
-    for one in (wo_x, wq_x, up_x, dn_x, x_up, x_dn, x_o, x_qkv, v_x):
-        over_chips(lambda j, one=one: one(j).wait_send())
-    for copy in (wo_c, wq_c, up_c, dn_c, st_up_c, st_dn_c, st_o_c, st_qkv_c, v_c):
-        copy.wait_send()
+    lax.fori_loop(1, C, lambda j, carry: (vec_x(j, c).wait_send(), carry)[1], 0)
     for s in range(S):
         pltpu.make_async_copy(mown.at[s], media_grad.at[s], osem.at[s]).wait()
 
@@ -893,8 +976,10 @@
             V((T, C, R, 3 * I), BF16),
             V((max(C - 1, 1), R, F), BF16),
             V((max(C - 1, 1), R, F), BF16),
-            V((max(C - 1, 1), T, R, I), BF16),
-            V((max(C - 1, 1), T, R, 3 * I), BF16),
+            V((2, max(C - 1, 1), T // 2, R, I), BF16),
+            V((T, max(C - 1, 1), 1, R, 3 * I), BF16),
+            V((T, R, I), BF16),
+            V((T, R, 3 * I), BF16),
             V((T - 1, R, I), BF16),
             V((T - 1, R, 3 * I), BF16),
             V((S * z.Lt, D), F32),
@@ -905,12 +990,12 @@
             V((T, 8, D), F32),
             pltpu.SemaphoreType.DMA((SLOTS_IN_FLIGHT + 1,)),
             pltpu.SemaphoreType.DMA((S,)),
-            pltpu.SemaphoreType.DMA((13, T - 1)),
-            pltpu.SemaphoreType.DMA((13, T - 1)),
-            pltpu.SemaphoreType.DMA((9, max(C - 1, 1))),
-            pltpu.SemaphoreType.DMA((9, max(C - 1, 1))),
-            pltpu.SemaphoreType.DMA((9,)),
-            pltpu.SemaphoreType.DMA((9,)),
+            pltpu.SemaphoreType.DMA((26, T - 1)),
+            pltpu.SemaphoreType.DMA((26, T - 1)),
+            pltpu.SemaphoreType.DMA((14, max(C - 1, 1))),
+            pltpu.SemaphoreType.DMA((14, max(C - 1, 1))),
+            pltpu.SemaphoreType.DMA((10,)),
+            pltpu.SemaphoreType.DMA((10,)),
         ]
         shape = jax.ShapeDtypeStruct
         outs = pl.pallas_call(

time: 134 us -> 123 us (0.918); the launches traced: 132 us -> 123 us
  Pallas kernels: 131 us -> 122 us
    pallas_call x1, Pallas kernels: 125 us -> 116 us  [on_device(): pl.pallas_call(functools.partial(layer_kernel, z), out_shape=[shape((S, L...]
where the time goes in v3:
time: 123 us
  Pallas kernels  122 us (99%)
    pallas_call x1, Pallas kernels, on_device(): pl.pallas_call(functools.partial(layer_kernel, z), out_shape=[shape((S, L...  116 us
    pallas_call x1, Pallas kernels, on_device(): pl.pallas_call(functools.partial(hand_out, z), out_shape=[shape((S, L, D)...  5.68 us

profile of v3, /device:TPU:0, one launch (start us, length us, event | category | flops | bytes accessed | tf_op | source)
XLA Modules:
  0.0 122.8 jit_solution(5626621090364260719)
XLA Ops:
  0.7 116.3 %resampler_layer.1 = (bf16[4,64,1024]{2,1,0:T(8,128)(2,1)}, bf16[4,320,1024]{2,1,0:T(8,128)(2,1)}, bf16[4,64,1024]{2,1,0:T(8,128)(2,1)}, f32[128,384]{1,0:T(8,12...) custom-call(s32[4]{0:T(128)} %counts.1, ...), custom_call_target="tpu_custom_call" | custom-call | tf_op jit(solution)/shard_map/resampler_layer/pallas_call | solution.py:1001
  116.9 5.7 %hand_out.1 = (bf16[4,64,1024]{2,1,0:T(8,128)(2,1)}, bf16[4,320,1024]{2,1,0:T(8,128)(2,1)}, bf16[4,64,1024]{2,1,0:T(8,128)(2,1)}, f32[128,128]{1,0:T(8,128)}, f3...) custom-call(bf16[4,64,1024]{2,1,0:T(8,128)(2,1)} %get-tuple-element., ...), custom_call_target="tpu_custom_call" | custom-call | tf_op jit(solution)/shard_map/hand_out/pallas_call | solution.py:1038

commit v4 on v3

--- a/solution.py
+++ b/solution.py
@@ -68,8 +68,8 @@
     z,
     counts,
     media,
-    lat,
-    cot,
+    lat_h,
+    cot_h,
     mgain,
     mshift,
     lgain,
@@ -90,6 +90,10 @@
     g_up,
     g_dn,
     g_vec,
+    lat,
+    cot,
+    dn_v,
+    wo_v,
     wq_b,
     wo_b,
     up_b,
@@ -141,6 +145,7 @@
     vcr,
     vx,
     vz,
+    lsem,
     msem,
     osem,
     zs,
@@ -264,19 +269,37 @@
         return masks
 
     def gather_steps(view, order):
-        i, at, steps = row("x"), 0, []
+        i, at, rests = row("x"), 0, []
+        firsts = ([], [])
         for step, bit in enumerate(order):
             peer = flip(c, 1 << bit)
             dev = (2 * peer + core, t)
-            out, came = [], []
+            rest = ([], [])
             for m in subsets(order[:step]):
                 sems = (xs.at[i, at], xr.at[i, at])
                 mine, theirs = view(flip(c, m)), view(flip(peer, m))
+                out, came = rest if m else firsts
                 out.append(remote(mine, mine, *sems, dev))
                 came.append(remote(theirs, theirs, *sems, dev))
                 at += 1
-            steps.append((out, came))
-        return steps
+            if step:
+                rests.append(rest)
+        return firsts, rests
+
+    def gather_rest(gather):
+        firsts, rests = gather
+        for step, rest in enumerate(rests):
+            arrive([firsts[1][step]])
+            if step:
+                arrive(rests[step - 1][1])
+            start(rest[0])
+
+    def gather_near(gather):
+        arrive([gather[0][1][-1]])
+
+    def gather_done(gather):
+        if gather[1]:
+            arrive(gather[1][-1][1])
 
     def scatter_steps(view, land, order):
         i, at, steps = row("x"), 0, []
@@ -303,8 +326,6 @@
     own_copy = pltpu.make_async_copy(
         media.at[:, pl.ds(pl.multiple_of(t * Mt, Mt), Mt)], mown, msem.at[SLOTS_IN_FLIGHT]
     )
-    for i in range(min(SLOTS_IN_FLIGHT, n_tiles)):
-        tile_copy(i).start()
     barrier = pltpu.get_barrier_semaphore()
 
     def greet(dev):
@@ -314,11 +335,22 @@
         greet(z_dev(k))
     lax.fori_loop(1, C, lambda j, carry: (greet(x_dev(j)), carry)[1], 0)
     greet(core_dev)
-    up_b[c, core] = up[...]
-    dn_b[c, core] = dn[...].T
-    wo_b[0] = wo[...].T.reshape(C, 2, R, I)
-    for m, weight in enumerate((wq, wk, wv)):
-        wq_b[0, :, :, :, pl.ds(m * I, I)] = weight[...].reshape(C, 2, R, I)
+    loads = [
+        pltpu.make_async_copy(src, dst, lsem.at[i])
+        for i, (src, dst) in enumerate(
+            [(up, up_b.at[c, core]), (dn, dn_v), (wo, wo_v)]
+            + [(w, wq_b.at[0, :, :, :, pl.ds(m * I, I)]) for m, w in enumerate((wq, wk, wv))]
+            + [(lat_h, lat), (cot_h, cot)]
+        )
+    ]
+    for copy in loads:
+        copy.start()
+    for i in range(min(SLOTS_IN_FLIGHT, n_tiles)):
+        tile_copy(i).start()
+    for copy in loads[:3]:
+        copy.wait()
+    dn_b[c, core] = dn_v[...].T
+    wo_b[0] = wo_v[...].T.reshape(C, 2, R, I)
     pl.semaphore_wait(barrier, T + C - 1)
 
     foreign = pl.ds(1, T - 1)
@@ -329,19 +361,22 @@
     v_x = gather_steps(lambda chip: wq_b.at[foreign, chip, core, :, pl.ds(2 * I, I)], y_first)
     wo_z = over_z(lambda k: (wo_b.at[0, c, core], wo_b.at[k, c, core]))
     wq_z = over_z(lambda k: (wq_b.at[0, c, core], wq_b.at[k, c, core]))
-    up_c = over_core(up_b.at[:, core], up_b.at[:, core])
-    dn_c = over_core(dn_b.at[:, core], dn_b.at[:, core])
+    near = [0] + [1 << bit for bit in range(bits)]
+    far = [m for m in range(C) if m not in near]
+
+    def relay(ref, masks):
+        return [copy for m in masks for copy in over_core(ref.at[flip(c, m), core], ref.at[flip(c, m), core])]
+
+    feed_near = relay(up_b, near) + relay(dn_b, near)
+    feed_far = relay(up_b, far) + relay(dn_b, far)
     wo_c = over_core(wo_b.at[foreign, :, core], wo_b.at[foreign, :, core])
     wq_c = over_core(wq_b.at[foreign, :, core], wq_b.at[foreign, :, core])
 
-    def gather_rest(steps):
-        for step in range(1, len(steps)):
-            arrive(steps[step - 1][1])
-            start(steps[step][0])
-
-    start(up_x[0][0])
-    start(dn_x[0][0])
+    for way in range(bits):
+        start([up_x[0][0][way], dn_x[0][0][way]])
     start(wo_z)
+    for copy in loads[3:]:
+        copy.wait()
     start(wq_z)
     own_copy.start()
 
@@ -402,14 +437,13 @@
         tile_next(i + 2)
         return carry
 
-    first, second = n_tiles // 8, 3 * n_tiles // 8
+    first = n_tiles // 8
     lax.fori_loop(0, first, two_tiles, 0)
     arrive(wo_z)
     start(wo_x[0][0])
-    lax.fori_loop(first, second, two_tiles, 0)
+    lax.fori_loop(first, n_tiles // 2, two_tiles, 0)
     gather_rest(up_x)
     gather_rest(dn_x)
-    lax.fori_loop(second, n_tiles // 2, two_tiles, 0)
     gather_rest(wo_x)
 
     def spread(x):
@@ -453,13 +487,16 @@
         for m, ref in enumerate((kall, vall)):
             ref[pl.ds(s * Kt, Mt), pl.ds(0, I)] = pairs[own_slots, pl.ds(lanes + m * I, I)]
             ref[pl.ds(s * Kt + Mt, Lt), pl.ds(0, I)] = pairs[own_lat, pl.ds(lanes + m * I, I)]
-    arrive(wo_x[-1][1])
+    gather_near(wo_x)
+    gather_near(up_x)
+    gather_near(dn_x)
+    start(feed_near)
+    gather_done(wo_x)
     start(wo_c)
-    arrive(up_x[-1][1])
-    start(up_c)
-    arrive(dn_x[-1][1])
-    start(dn_c)
     arrive(wq_z)
+    gather_done(up_x)
+    gather_done(dn_x)
+    start(feed_far)
     start(qk_x[0][0])
     start(v_x[0][0])
 
@@ -475,8 +512,8 @@
         unit, _ = unit_rows(res[rows, :])
         hin[rows, :] = (unit * fgain[...] + fshift[...]).astype(BF16)
 
-    arrive(up_c)
-    arrive(dn_c)
+    arrive(feed_near)
+    arrive(feed_far)
 
     def feed(b, carry):
         cols = pl.ds(pl.multiple_of(b * BLOCK, BLOCK), BLOCK)
@@ -489,6 +526,8 @@
         return carry
 
     lax.fori_loop(0, F // BLOCK, feed, 0, unroll=2)
+    gather_rest(qk_x)
+    gather_rest(v_x)
 
     def back_to_width(left, weight, out, b):
         block = nt(left[...], weight[pl.ds(b * n, n)].reshape(BLOCK, F))
@@ -501,8 +540,6 @@
         now = over_z(lambda k, cols=cols: (hg.at[:, my_rows(k), cols], hgr.at[k - 1, :, :, cols]))
         start(now)
         hg_z += now
-    gather_rest(qk_x)
-    gather_rest(v_x)
 
     def feed_weights(left, right, out, b):
         block = tn(left[:, pl.ds(b * BLOCK, BLOCK)], right[...]).astype(BF16)
@@ -543,6 +580,49 @@
 
     feed_core(st_up_c, st_up, cr_up, up_g)
     feed_core(st_dn_c, st_dn, cr_dn, dn_g)
+
+    for gather in (qk_x, v_x):
+        gather_near(gather)
+        gather_done(gather)
+    start(wq_c)
+    own_copy.wait()
+    arrive(wq_c)
+    for k in range(1, T):
+        qall[:, pl.ds(k * I, I)] = nn(latn[...], wq_b[k, :, :, :, pl.ds(0, I)].reshape(D, I)).astype(BF16)
+    half_rows = S * Kt // 2
+
+    def all_pairs(i, carry):
+        k = lax.div(i, 2)
+        rows = pl.ds(pl.multiple_of(lax.rem(i, 2) * half_rows, 16), half_rows)
+        lanes = pl.ds(pl.multiple_of(k * I, I), I)
+        pair = nn(ctx[rows, :], wq_b[k, :, :, :, pl.ds(I, 2 * I)].reshape(D, 2 * I)).astype(BF16)
+        kall[rows, lanes] = pair[:, :I]
+        vall[rows, lanes] = pair[:, I:]
+        return carry
+
+    lax.fori_loop(2, 2 * T, all_pairs, 0)
+    arrive(lse_z)
+    slot_of = lax.broadcasted_iota(jnp.int32, (Kt, 1), 0)
+
+    def group(g, s):
+        rows = pl.ds(pl.multiple_of(s * Kt, 16), Kt)
+        lat_rows = pl.ds(pl.multiple_of(s * L, L), L)
+        return rows, pl.ds(g * GI, GI), lat_rows
+
+    def joined(g, pick):
+        return jnp.concatenate([pick(g * G + j) for j in range(G)], axis=1)
+
+    for g in range(groups):
+
+        def probabilities(s, carry, g=g):
+            rows, lanes, lat_rows = group(g, s)
+            scores = nt(kall[rows, lanes], spread(qall[lat_rows, lanes])) * scale_factor
+            valid = (slot_of + t * Mt < counts[s] * PATCH) | (slot_of >= Mt)
+            scores = jnp.where(valid, scores, NEGATIVE)
+            pall[g * S + s] = jnp.exp(scores - joined(g, lambda k: lse[k, pl.ds(s, 1), :]))
+            return carry
+
+        lax.fori_loop(0, S, probabilities, 0, unroll=2)
 
     arrive(hg_z)
     feed_gain_part = jnp.zeros((1, D), F32)
@@ -574,48 +654,6 @@
             st_o[k, pl.ds(b * n, n)] = block[:, k * I : (k + 1) * I].reshape(n, 2, R, I)
     st_o_c = over_core(st_o.at[:, :, other], cr_o)
     start(st_o_c)
-
-    arrive(qk_x[-1][1])
-    arrive(v_x[-1][1])
-    start(wq_c)
-    own_copy.wait()
-    arrive(wq_c)
-    for k in range(1, T):
-        qall[:, pl.ds(k * I, I)] = nn(latn[...], wq_b[k, :, :, :, pl.ds(0, I)].reshape(D, I)).astype(BF16)
-    half_rows = S * Kt // 2
-
-    def all_pairs(i, carry):
-        k = lax.div(i, 2)
-        rows = pl.ds(pl.multiple_of(lax.rem(i, 2) * half_rows, 16), half_rows)
-        lanes = pl.ds(pl.multiple_of(k * I, I), I)
-        pair = nn(ctx[rows, :], wq_b[k, :, :, :, pl.ds(I, 2 * I)].reshape(D, 2 * I)).astype(BF16)
-        kall[rows, lanes] = pair[:, :I]
-        vall[rows, lanes] = pair[:, I:]
-        return carry
-
-    lax.fori_loop(2, 2 * T, all_pairs, 0)
-    arrive(lse_z)
-    slot_of = lax.broadcasted_iota(jnp.int32, (Kt, 1), 0)
-
-    def group(g, s):
-        rows = pl.ds(pl.multiple_of(s * Kt, 16), Kt)
-        lat_rows = pl.ds(pl.multiple_of(s * L, L), L)
-        return rows, pl.ds(g * GI, GI), lat_rows
-
-    def joined(g, pick):
-        return jnp.concatenate([pick(g * G + j) for j in range(G)], axis=1)
-
-    for g in range(groups):
-
-        def probabilities(s, carry, g=g):
-            rows, lanes, lat_rows = group(g, s)
-            scores = nt(kall[rows, lanes], spread(qall[lat_rows, lanes])) * scale_factor
-            valid = (slot_of + t * Mt < counts[s] * PATCH) | (slot_of >= Mt)
-            scores = jnp.where(valid, scores, NEGATIVE)
-            pall[g * S + s] = jnp.exp(scores - joined(g, lambda k: lse[k, pl.ds(s, 1), :]))
-            return carry
-
-        lax.fori_loop(0, S, probabilities, 0, unroll=2)
 
     def heads_core(st, came, ks, steps):
         for m in subsets(range(bits)):
@@ -877,24 +915,40 @@
         pltpu.make_async_copy(mown.at[s], media_grad.at[s], osem.at[s]).wait()
 
 
-def hand_out(z, new_lat, media_grad, lat_grad, g_qkv, g_o, g_up, g_dn, g_vec, *refs):
-    outs, held, sem_in, sem_out = refs[:15], refs[15], refs[16], refs[17]
-    loads = [pltpu.make_async_copy(media_grad.at[s], held.at[s], sem_in.at[s]) for s in range(z.S)]
-    stores = [pltpu.make_async_copy(held.at[s], outs[1].at[s], sem_out.at[s]) for s in range(z.S)]
-    for copy in loads:
+def hand_out(z, *refs):
+    ins, outs, held, results, sem_in, sem_out = refs[:8], refs[8:23], refs[23:31], refs[31:38], refs[38], refs[39]
+    order = (1, 0, 2, 5, 6, 3, 4, 7)
+    loads = {i: pltpu.make_async_copy(ins[i], held[i], sem_in.at[i]) for i in order}
+    stores = []
+
+    def store(src, i):
+        copy = pltpu.make_async_copy(src, outs[i], sem_out.at[i])
         copy.start()
-    for load, store in zip(loads, stores):
-        load.wait()
-        store.start()
-    outs[0][...] = new_lat[...]
-    outs[2][...] = lat_grad[...]
+        stores.append(copy)
+
+    for i in order:
+        loads[i].start()
+    new_lat, media_grad, lat_grad, g_qkv, g_o, g_up, g_dn, g_vec = held
+    loads[5].wait()
+    store(g_up, 7)
+    loads[6].wait()
+    results[0][...] = g_dn[...].T
+    store(results[0], 8)
+    loads[0].wait()
+    store(new_lat, 0)
+    loads[2].wait()
+    store(lat_grad, 2)
+    loads[1].wait()
+    store(media_grad, 1)
+    loads[3].wait()
     for m in range(3):
-        outs[3 + m][...] = g_qkv[:, pl.ds(m * z.I, z.I)]
-    outs[6][...] = g_o[...].T
-    outs[7][...] = g_up[...]
-    outs[8][...] = g_dn[...].T
-    outs[9][...] = g_vec[pl.ds(0, 1), :]
-    outs[10][...] = g_vec[pl.ds(1, 1), :]
+        store(g_qkv.at[:, pl.ds(m * z.I, z.I)], 3 + m)
+    loads[4].wait()
+    results[1][...] = g_o[...].T
+    store(results[1], 6)
+    loads[7].wait()
+    for m in range(2):
+        store(g_vec.at[pl.ds(m, 1)], 9 + m)
     first = lax.axis_index("dp") * z.R
     row = lax.broadcasted_iota(jnp.int32, (z.D, z.R), 0)
     col = lax.broadcasted_iota(jnp.int32, (z.D, z.R), 1)
@@ -903,9 +957,10 @@
         g_vec[...], pick, (((1,), (0,)), ((), ())), preferred_element_type=F32, precision=lax.Precision.HIGHEST
     )
     for m in range(4):
-        outs[11 + m][...] = own[2 + m : 3 + m]
-    for store in stores:
-        store.wait()
+        results[2 + m][...] = own[2 + m : 3 + m]
+        store(results[2 + m], 11 + m)
+    for copy in stores:
+        copy.wait()
 
 
 def solution(mesh):
@@ -937,6 +992,10 @@
         hbm = pl.BlockSpec(memory_space=pl.ANY)
         V = pltpu.VMEM
         scratch = [
+            V((S * L, D), BF16),
+            V((S * L, D), BF16),
+            V((F, R), BF16),
+            V((I, D), BF16),
             V((T, C, 2, R, 3 * I), BF16),
             V((T, C, 2, R, I), BF16),
             V((C, 2, R, F), BF16),
@@ -988,14 +1047,15 @@
             V((8, D), F32),
             V((C, 8, D), F32),
             V((T, 8, D), F32),
+            pltpu.SemaphoreType.DMA((8,)),
             pltpu.SemaphoreType.DMA((SLOTS_IN_FLIGHT + 1,)),
             pltpu.SemaphoreType.DMA((S,)),
             pltpu.SemaphoreType.DMA((26, T - 1)),
             pltpu.SemaphoreType.DMA((26, T - 1)),
             pltpu.SemaphoreType.DMA((14, max(C - 1, 1))),
             pltpu.SemaphoreType.DMA((14, max(C - 1, 1))),
-            pltpu.SemaphoreType.DMA((10,)),
-            pltpu.SemaphoreType.DMA((10,)),
+            pltpu.SemaphoreType.DMA((8 + 2 * C,)),
+            pltpu.SemaphoreType.DMA((8 + 2 * C,)),
         ]
         shape = jax.ShapeDtypeStruct
         outs = pl.pallas_call(
@@ -1010,7 +1070,7 @@
                 shape((R, F), F32),
                 shape((8, D), F32),
             ],
-            in_specs=[pl.BlockSpec(memory_space=pltpu.SMEM), hbm] + [vmem] * 14,
+            in_specs=[pl.BlockSpec(memory_space=pltpu.SMEM)] + [hbm] * 3 + [vmem] * 6 + [hbm] * 6,
             out_specs=[vmem, hbm] + [vmem] * 6,
             scratch_shapes=scratch,
             compiler_params=pltpu.CompilerParams(
@@ -1028,9 +1088,9 @@
             row(latent_shift),
             row(feed_gain),
             row(feed_shift),
-            query_weight,
-            key_weight,
-            value_weight,
+            query_weight.reshape(C, 2, R, I),
+            key_weight.reshape(C, 2, R, I),
+            value_weight.reshape(C, 2, R, I),
             output_weight,
             up_weight,
             down_weight,
@@ -1051,9 +1111,12 @@
                 shape((1, D), F32),
             ]
             + [shape((1, R), F32)] * 4,
-            in_specs=[vmem, hbm] + [vmem] * 6,
-            out_specs=[vmem, hbm] + [vmem] * 13,
-            scratch_shapes=[V((S, z.Mt, D), BF16), pltpu.SemaphoreType.DMA((S,)), pltpu.SemaphoreType.DMA((S,))],
+            in_specs=[hbm] * 8,
+            out_specs=[hbm] * 15,
+            scratch_shapes=[V(out.shape, out.dtype) for out in outs]
+            + [V((F, R), F32), V((I, R), F32)]
+            + [V((1, R), F32)] * 5
+            + [pltpu.SemaphoreType.DMA((8,)), pltpu.SemaphoreType.DMA((15,))],
             name="hand_out",
         )(*outs)
         return tuple(final[:9]) + tuple(v.reshape(-1) for v in final[9:])

time: 123 us -> 119 us (0.967)
  Pallas kernels: 122 us -> 118 us
    pallas_call x1, Pallas kernels: 116 us -> 113 us  [on_device(): pl.pallas_call(functools.partial(layer_kernel, z), out_shape=[shape((S, L...]
where the time goes in v4:
time: 119 us; the launch traced here: 118 us
  Pallas kernels  118 us (99%)
    pallas_call x1, Pallas kernels, on_device(): pl.pallas_call(functools.partial(layer_kernel, z), out_shape=[shape((S, L...  113 us
    pallas_call x1, Pallas kernels, on_device(): pl.pallas_call(functools.partial(hand_out, z), out_shape=[shape((S, L, D)...  4.79 us

profile of v4, /device:TPU:0, one launch (start us, length us, event | category | flops | bytes accessed | tf_op | source)
XLA Modules:
  0.0 118.4 jit_solution(1473647786946597076)
XLA Ops:
  0.7 112.8 %resampler_layer.1 = (bf16[4,64,1024]{2,1,0:T(8,128)(2,1)}, bf16[4,320,1024]{2,1,0:T(8,128)(2,1)}, bf16[4,64,1024]{2,1,0:T(8,128)(2,1)}, f32[128,384]{1,0:T(8,12...) custom-call(s32[4]{0:T(128)} %counts.1, ...), custom_call_target="tpu_custom_call" | custom-call | tf_op jit(solution)/shard_map/resampler_layer/pallas_call | solution.py:1061
  113.4 4.8 %hand_out.1 = (bf16[4,64,1024]{2,1,0:T(8,128)(2,1)}, bf16[4,320,1024]{2,1,0:T(8,128)(2,1)}, bf16[4,64,1024]{2,1,0:T(8,128)(2,1)}, f32[128,128]{1,0:T(8,128)}, f3...) custom-call(bf16[4,64,1024]{2,1,0:T(8,128)(2,1)} %get-tuple-element., ...), custom_call_target="tpu_custom_call" | custom-call | tf_op jit(solution)/shard_map/hand_out/pallas_call | solution.py:1098

commit v5 on v4

--- a/solution.py
+++ b/solution.py
@@ -121,6 +121,7 @@
     og,
     rgr,
     dob,
+    dos,
     dqb,
     dqr,
     st_up,
@@ -206,15 +207,6 @@
         i = row("z")
         return [remote(*pick(k), zs.at[i, k - 1], zr.at[i, k - 1], z_dev(k)) for k in range(1, T)]
 
-    def share_rows(pick):
-        out = over_z(lambda k: (pick(my_rows()), pick(my_rows())))
-        i = count["z"] - 1
-        came = [
-            remote(pick(my_rows(T - k)), pick(my_rows(T - k)), zs.at[i, k - 1], zr.at[i, k - 1], z_dev(k))
-            for k in range(1, T)
-        ]
-        return out, came
-
     def line_share(pick):
         ways = []
         for step in (1, -1):
@@ -339,7 +331,7 @@
         pltpu.make_async_copy(src, dst, lsem.at[i])
         for i, (src, dst) in enumerate(
             [(up, up_b.at[c, core]), (dn, dn_v), (wo, wo_v)]
-            + [(w, wq_b.at[0, :, :, :, pl.ds(m * I, I)]) for m, w in enumerate((wq, wk, wv))]
+            + [(w, wq_b.at[0, m]) for m, w in enumerate((wq, wk, wv))]
             + [(lat_h, lat), (cot_h, cot)]
         )
     ]
@@ -357,10 +349,10 @@
     up_x = gather_steps(lambda chip: up_b.at[chip, core], x_first)
     dn_x = gather_steps(lambda chip: dn_b.at[chip, core], y_first)
     wo_x = gather_steps(lambda chip: wo_b.at[foreign, chip, core], x_first)
-    qk_x = gather_steps(lambda chip: wq_b.at[foreign, chip, core, :, pl.ds(0, 2 * I)], x_first)
-    v_x = gather_steps(lambda chip: wq_b.at[foreign, chip, core, :, pl.ds(2 * I, I)], y_first)
+    qk_x = gather_steps(lambda chip: wq_b.at[foreign, pl.ds(0, 2), chip, core], x_first)
+    v_x = gather_steps(lambda chip: wq_b.at[foreign, 2, chip, core], y_first)
     wo_z = over_z(lambda k: (wo_b.at[0, c, core], wo_b.at[k, c, core]))
-    wq_z = over_z(lambda k: (wq_b.at[0, c, core], wq_b.at[k, c, core]))
+    wq_z = over_z(lambda k: (wq_b.at[0, :, c, core], wq_b.at[k, :, c, core]))
     near = [0] + [1 << bit for bit in range(bits)]
     far = [m for m in range(C) if m not in near]
 
@@ -370,7 +362,7 @@
     feed_near = relay(up_b, near) + relay(dn_b, near)
     feed_far = relay(up_b, far) + relay(dn_b, far)
     wo_c = over_core(wo_b.at[foreign, :, core], wo_b.at[foreign, :, core])
-    wq_c = over_core(wq_b.at[foreign, :, core], wq_b.at[foreign, :, core])
+    wq_c = over_core(wq_b.at[foreign, :, :, core], wq_b.at[foreign, :, :, core])
 
     for way in range(bits):
         start([up_x[0][0][way], dn_x[0][0][way]])
@@ -384,7 +376,10 @@
         rows = pl.ds(b * ROWS, ROWS)
         unit, _ = unit_rows(lat[rows, :].astype(F32))
         latn[rows, :] = (unit * lgain[...] + lshift[...]).astype(BF16)
-    own_qkv = nn(latn[...], wq_b[0].reshape(D, 3 * I)).astype(BF16)
+    def head_weights(k, ms):
+        return jnp.concatenate([wq_b[k, m].reshape(D, I) for m in ms], axis=1)
+
+    own_qkv = nn(latn[...], head_weights(0, range(3))).astype(BF16)
     qall[:, pl.ds(0, I)] = own_qkv[:, :I]
     for s in range(S):
         pairs[pl.ds(M, L), pl.ds(s * 2 * I, 2 * I)] = own_qkv[s * L : (s + 1) * L, I:]
@@ -399,7 +394,7 @@
 
     def tile_pair(i, half):
         s, r = lax.div(i, T), lax.rem(i, T)
-        pair = nn(xn[half], wq_b[0, :, :, :, pl.ds(I, 2 * I)].reshape(D, 2 * I))
+        pair = nn(xn[half], head_weights(0, (1, 2)))
         lanes = pl.ds(pl.multiple_of(s * 2 * I, 2 * I), 2 * I)
         pairs[pl.ds(pl.multiple_of(r * Mt, Mt), Mt), lanes] = pair.astype(BF16)
 
@@ -494,11 +489,11 @@
     gather_done(wo_x)
     start(wo_c)
     arrive(wq_z)
+    start(qk_x[0][0])
+    start(v_x[0][0])
     gather_done(up_x)
     gather_done(dn_x)
     start(feed_far)
-    start(qk_x[0][0])
-    start(v_x[0][0])
 
     def heads_wo():
         return jnp.concatenate([wo_b[k].reshape(D, I) for k in range(T)], axis=1)
@@ -525,21 +520,22 @@
         bgr[:, cols] = (act_grad.astype(F32) * slope).astype(BF16)
         return carry
 
-    lax.fori_loop(0, F // BLOCK, feed, 0, unroll=2)
+    lax.fori_loop(0, F // BLOCK, feed, 0, unroll=4)
     gather_rest(qk_x)
     gather_rest(v_x)
 
     def back_to_width(left, weight, out, b):
         block = nt(left[...], weight[pl.ds(b * n, n)].reshape(BLOCK, F))
-        out[:, :, pl.ds(b * BLOCK, BLOCK)] = block.astype(BF16).reshape(S, L, BLOCK)
-
-    hg_z = []
+        block = block.astype(BF16)
+        for s in range(S):
+            for u in range(T):
+                first = s * L + u * Lt
+                out[u, pl.ds(s * Lt, Lt), pl.ds(b * BLOCK, BLOCK)] = block[first : first + Lt]
+
     for b in range(blocks):
-        cols = pl.ds(b * BLOCK, BLOCK)
         back_to_width(bgr, up_b, hg, b)
-        now = over_z(lambda k, cols=cols: (hg.at[:, my_rows(k), cols], hgr.at[k - 1, :, :, cols]))
-        start(now)
-        hg_z += now
+    hg_z = over_z(lambda k: (hg.at[lax.rem(t + k, T)], hgr.at[k - 1]))
+    start(hg_z)
 
     def feed_weights(left, right, out, b):
         block = tn(left[:, pl.ds(b * BLOCK, BLOCK)], right[...]).astype(BF16)
@@ -588,14 +584,14 @@
     own_copy.wait()
     arrive(wq_c)
     for k in range(1, T):
-        qall[:, pl.ds(k * I, I)] = nn(latn[...], wq_b[k, :, :, :, pl.ds(0, I)].reshape(D, I)).astype(BF16)
+        qall[:, pl.ds(k * I, I)] = nn(latn[...], head_weights(k, (0,))).astype(BF16)
     half_rows = S * Kt // 2
 
     def all_pairs(i, carry):
         k = lax.div(i, 2)
         rows = pl.ds(pl.multiple_of(lax.rem(i, 2) * half_rows, 16), half_rows)
         lanes = pl.ds(pl.multiple_of(k * I, I), I)
-        pair = nn(ctx[rows, :], wq_b[k, :, :, :, pl.ds(I, 2 * I)].reshape(D, 2 * I)).astype(BF16)
+        pair = nn(ctx[rows, :], head_weights(k, (1, 2))).astype(BF16)
         kall[rows, lanes] = pair[:, :I]
         vall[rows, lanes] = pair[:, I:]
         return carry
@@ -630,9 +626,9 @@
     for s in range(S):
         own = pl.ds(pl.multiple_of(s * L + t * Lt, Lt), Lt)
         unit, scale_inv = unit_rows(res[own, :])
-        upstream = hg[s, my_rows(), :].astype(F32)
+        upstream = hg[t, pl.ds(s * Lt, Lt), :].astype(F32)
         for k in range(1, T):
-            upstream = upstream + hgr[k - 1, s].astype(F32)
+            upstream = upstream + hgr[k - 1, pl.ds(s * Lt, Lt), :].astype(F32)
         back = cot[own, :].astype(F32) + norm_back(unit, scale_inv, fgain[...], upstream)
         feed_gain_part = feed_gain_part + jnp.sum(upstream * unit, axis=0, keepdims=True)
         feed_shift_part = feed_shift_part + jnp.sum(upstream, axis=0, keepdims=True)
@@ -641,10 +637,10 @@
     vst[...] = jnp.concatenate(
         [jnp.zeros((4, D), F32), feed_gain_part, feed_shift_part, jnp.zeros((2, D), F32)], axis=0
     )
-    grads_all = nn(og[...], heads_wo()).astype(BF16)
-    for k in range(T):
-        dob[head(k), :, my_rows(), :] = grads_all[:, k * I : (k + 1) * I].reshape(S, Lt, I)
-    do_z, do_in = share_rows(lambda rows: dob.at[:, :, rows, :])
+    dos[0] = nn(og[...], heads_wo()).astype(BF16)
+    turns = list(range(groups))[::-1]
+    group_heads = [range(g * G, (g + 1) * G) for g in range(groups)]
+    do_z = over_z(lambda k: (dos.at[0], dos.at[k]))
     start(do_z)
 
     att_own = jnp.concatenate([att[k, :, my_rows(), :].reshape(S * Lt, I) for k in range(T)], axis=1)
@@ -696,17 +692,17 @@
     for g in range(2):
         heads_core(st_o, cr_o, o_heads[g], o_steps[g])
 
-    arrive(do_in)
-    fp_z = over_z(lambda k: (fp.at[:, my_rows(k)], fpr.at[k - 1]))
-    start(fp_z)
-    feed_step(st_up, xr_up, up_g)
-    feed_step(st_dn, xr_dn, dn_g)
+    arrive(do_z)
+    for m in range(T):
+        for k in range(T):
+            lanes = pl.ds((k - m) % T * I, I)
+            dob[k, :, my_rows(T - m), :] = dos[m, :, lanes].reshape(S, Lt, I)
 
     def attend_back(s, carry, g):
         rows, lanes, lat_rows = group(g, s)
         keys = kall[rows, lanes]
         queries = spread(qall[lat_rows, lanes])
-        grads = spread(joined(g, lambda k: dob[head(k), s]))
+        grads = spread(joined(g, lambda k: dob[k, s]))
         outs = spread(joined(g, lambda k: att[k, s]))
         product = grads.astype(F32) * outs.astype(F32)
         inner = lax.dot_general(
@@ -722,11 +718,19 @@
         pairs[rows, pl.ds(T * I + g * GI, GI)] = nn(probs.astype(BF16), grads).astype(BF16)
         query_grad = (gather_heads(tn(score_grad, keys)) * scale_factor).astype(BF16)
         for j in range(G):
-            dqb[g * G + j, s] = query_grad[:, j * I : (j + 1) * I]
+            for u in range(T):
+                rows_u = pl.ds(pl.multiple_of(s * Lt, Lt), Lt)
+                dqb[u, g * G + j, rows_u, :] = query_grad[u * Lt : (u + 1) * Lt, j * I : (j + 1) * I]
         return carry
 
     def group_weights(g):
-        query_part = jnp.concatenate([dqb[g * G + j].reshape(S * L, I) for j in range(G)], axis=1)
+        query_part = jnp.concatenate(
+            [
+                jnp.concatenate([dqb[u, g * G + j, pl.ds(s * Lt, Lt), :] for s in range(S) for u in range(T)], axis=0)
+                for j in range(G)
+            ],
+            axis=1,
+        )
         all_rows = pl.ds(0, S * Kt)
         part = jnp.concatenate(
             [pairs[all_rows, pl.ds(g * GI, GI)], pairs[all_rows, pl.ds(T * I + g * GI, GI)]], axis=1
@@ -749,8 +753,7 @@
         scatter_steps(lambda chip, k=k: st_qkv.at[pl.ds(k, 1), chip, core], lambda at, k=k: xr_qkv.at[k, at], orders[k % 2])
         for k in range(T)
     ]
-    group_heads = [range(g * G, (g + 1) * G) for g in range(groups)]
-    q_c, dq_z = [], []
+    q_c, dq_z = {}, []
 
     def group_core(g):
         arrive(q_c[g])
@@ -767,16 +770,47 @@
             out += heads_last(st_qkv, xr_qkv.at[k], (k,), q_steps[k], zb_qkv, zr_qkv)
         return out
 
-    for g in range(groups):
-        lax.fori_loop(0, S, functools.partial(attend_back, g=g), 0, unroll=2)
-        for j in range(G):
-            k = g * G + j
-            now = over_z(lambda m, k=k: (dqb.at[k, :, my_rows(m), :], dqr.at[m - 1, (m + k) % T]))
-            start(now)
-            dq_z += now
-        if g:
-            group_core(g - 1)
-        q_c.append(group_weights(g))
+    fp_z = over_z(lambda k: (fp.at[lax.rem(t + k, T)], fpr.at[k - 1]))
+    if groups > 1:
+        start(fp_z)
+        feed_step(st_up, xr_up, up_g)
+        feed_step(st_dn, xr_dn, dn_g)
+    def new_rows():
+        arrive(fp_z)
+        for s in range(S):
+            own = pl.ds(pl.multiple_of(s * L + t * Lt, Lt), Lt)
+            total = fp[t, pl.ds(s * Lt, Lt), :].astype(F32)
+            for k in range(1, T):
+                total = total + fpr[k - 1, pl.ds(s * Lt, Lt), :].astype(F32)
+            new_lat[s, my_rows(), :] = (res[own, :] + total).astype(BF16)
+
+    nl_hop, nl_end = line_share(lambda rows: new_lat.at[:, rows, :])
+    for turn, g in enumerate(turns):
+        if turn <= 1:
+            if turn == 0 and groups > 1:
+                lax.fori_loop(0, S // 2, functools.partial(attend_back, g=g), 0, unroll=2)
+                lax.fori_loop(S // 2, S, functools.partial(attend_back, g=g), 0, unroll=2)
+            else:
+                lax.fori_loop(0, S // 2, functools.partial(attend_back, g=g), 0, unroll=2)
+                if turn:
+                    group_core(turns[turn - 1])
+                else:
+                    start(fp_z)
+                lax.fori_loop(S // 2, S, functools.partial(attend_back, g=g), 0, unroll=2)
+        else:
+            group_core(turns[turn - 1])
+            lax.fori_loop(0, S, functools.partial(attend_back, g=g), 0, unroll=2)
+        ks = pl.ds(g * G, G)
+        now = over_z(lambda m, ks=ks: (dqb.at[lax.rem(t + m, T), ks], dqr.at[m - 1, ks]))
+        start(now)
+        dq_z += now
+        if turn == groups - 1:
+            new_rows()
+            nl_hop(1)
+        q_c[g] = group_weights(g)
+    if groups == 1:
+        feed_step(st_up, xr_up, up_g)
+        feed_step(st_dn, xr_dn, dn_g)
     for g in range(2):
         heads_step(st_o, xr_o.at[g], o_heads[g], o_steps[g])
 
@@ -785,17 +819,20 @@
     def width(s, rows):
         return jnp.concatenate([pall[s % 2 * blocks + b, rows, :] for b in range(blocks)], axis=1)
 
+    def width_weights(b):
+        return jnp.concatenate(
+            [wq_b[k, m, pl.ds(b * n, n)].reshape(BLOCK, I) for m in (1, 2) for k in range(T)], axis=1
+        )
+
     def media_width(s):
         for b in range(blocks):
-            weights = jnp.concatenate(
-                [
-                    wq_b[k, pl.ds(b * n, n), :, :, pl.ds(m * I, I)].reshape(BLOCK, I)
-                    for m in (1, 2)
-                    for k in range(T)
-                ],
-                axis=1,
-            )
-            pall[s % 2 * blocks + b] = nt(pairs[pl.ds(s * Kt, Kt), pl.ds(0, 2 * T * I)], weights)
+            pall[s % 2 * blocks + b] = nt(pairs[pl.ds(s * Kt, Kt), pl.ds(0, 2 * T * I)], width_weights(b))
+
+    lat_pairs = jnp.concatenate(
+        [pairs[pl.ds(s * Kt + Mt, Lt), pl.ds(0, 2 * T * I)] for s in range(S)], axis=0
+    )
+    for b in range(blocks):
+        mgl[:, pl.ds(b * BLOCK, BLOCK)] = nt(lat_pairs, width_weights(b))
 
     def media_rows(s):
         for b in range(Mt // ROWS):
@@ -805,41 +842,22 @@
             mown[s, rows, :] = norm_back(unit, scale_inv, mgain[...], upstream).astype(BF16)
             acc[0] += fold(upstream * unit)
             acc[1] += fold(upstream)
-        mgl[pl.ds(s * Lt, Lt), :] = width(s, pl.ds(Mt, Lt))
         pltpu.make_async_copy(mown.at[s], media_grad.at[s], osem.at[s]).start()
 
     media_width(0)
-    for s in range(S):
-        if s + 1 < S:
-            media_width(s + 1)
-        media_rows(s)
-        if s == 0:
-            group_core(groups - 1)
-        if s == S // 2:
-            for g in range(groups - 1):
-                group_step(g)
-
-    arrive(fp_z)
-    for s in range(S):
-        own = pl.ds(pl.multiple_of(s * L + t * Lt, Lt), Lt)
-        total = fp[s, my_rows(), :].astype(F32)
-        for k in range(1, T):
-            total = total + fpr[k - 1, s].astype(F32)
-        new_lat[s, my_rows(), :] = (res[own, :] + total).astype(BF16)
-    nl_hop, nl_end = line_share(lambda rows: new_lat.at[:, rows, :])
-    nl_hop(1)
-    o_z = []
-    for g in range(2):
-        o_z += heads_last(st_o, xr_o.at[g], o_heads[g], o_steps[g], zb_o, zr_o)
+    media_width(1)
+    group_core(turns[-1])
+    media_rows(0)
+    nl_hop(2)
 
     arrive(dq_z)
     upstream_all = mgl[...]
     for k in range(T):
-        total = dqb[k, :, my_rows(), :].astype(F32)
+        total = dqb[t, k].astype(F32)
         for m in range(1, T):
-            total = total + dqr[m - 1, k].astype(F32)
-        weights = wq_b[k, :, :, :, pl.ds(0, I)].reshape(D, I)
-        upstream_all = upstream_all + nt(total.astype(BF16).reshape(S * Lt, I), weights)
+            total = total + dqr[m - 1, (k - m) % T].astype(F32)
+        weights = head_weights(k, (0,))
+        upstream_all = upstream_all + nt(total.astype(BF16), weights)
     mgl[...] = upstream_all
     lat_gain_part = jnp.zeros((1, D), F32)
     lat_shift_part = jnp.zeros((1, D), F32)
@@ -853,6 +871,23 @@
         lat_shift_part = lat_shift_part + jnp.sum(upstream, axis=0, keepdims=True)
     lg_hop, lg_end = line_share(lambda rows: lat_grad.at[:, rows, :])
     lg_hop(1)
+
+    for g in turns[:-1]:
+        group_step(g)
+    o_z = []
+    for g in range(2):
+        o_z += heads_last(st_o, xr_o.at[g], o_heads[g], o_steps[g], zb_o, zr_o)
+    for s in range(1, S):
+        if s + 1 < S:
+            media_width(s + 1)
+        media_rows(s)
+    for h in range(3, T):
+        nl_hop(h)
+    group_step(turns[-1])
+    q_z = []
+    for g in turns[:-1]:
+        q_z += group_last(g)
+    lg_hop(2)
 
     vst[...] += jnp.concatenate(
         [
@@ -875,23 +910,16 @@
 
     lax.fori_loop(1, C, lambda j, carry: (vec_x(j, c).start(), carry)[1], 0)
 
-    group_step(groups - 1)
-    nl_hop(2)
-    q_z = []
-    for g in range(groups - 1):
-        q_z += group_last(g)
     feed_last(st_up, xr_up, up_g, g_up)
     feed_last(st_dn, xr_dn, dn_g, g_dn)
+    q_z += group_last(turns[-1])
     lax.fori_loop(1, C, lambda j, carry: (vec_x(j, lax.rem(c - j + C, C)).wait_recv(), carry)[1], 0)
     vz[t] = lax.fori_loop(1, C, lambda j, value: value + vx[j], vx[0])
     v_z = over_z(lambda k: (vz.at[t], vz.at[t]))
     i = count["z"] - 1
     v_in = [remote(vz.at[head(k)], vz.at[head(k)], zs.at[i, k - 1], zr.at[i, k - 1], z_dev(k)) for k in range(1, T)]
     start(v_z)
-    lg_hop(2)
-    q_z += group_last(groups - 1)
     for h in range(3, T):
-        nl_hop(h)
         lg_hop(h)
     arrive(v_in)
     g_vec[...] = lax.fori_loop(1, T, lambda k, value: value + vz[k], vz[0])
@@ -996,7 +1024,7 @@
             V((S * L, D), BF16),
             V((F, R), BF16),
             V((I, D), BF16),
-            V((T, C, 2, R, 3 * I), BF16),
+            V((T, 3, C, 2, R, I), BF16),
             V((T, C, 2, R, I), BF16),
             V((C, 2, R, F), BF16),
             V((C, 2, R, F), BF16),
@@ -1016,15 +1044,16 @@
             V((S * L, D), BF16),
             V((S * L, F), BF16),
             V((S * L, F), BF16),
-            V((S, L, D), BF16),
-            V((T - 1, S, z.Lt, D), BF16),
-            V((S, L, D), BF16),
-            V((T - 1, S, z.Lt, D), BF16),
+            V((T, S * z.Lt, D), BF16),
+            V((T - 1, S * z.Lt, D), BF16),
+            V((T, S * z.Lt, D), BF16),
+            V((T - 1, S * z.Lt, D), BF16),
             V((S * z.Lt, D), BF16),
             V((S * z.Lt, D), F32),
             V((T, S, L, I), BF16),
-            V((T, S, L, I), BF16),
-            V((T - 1, T, S, z.Lt, I), BF16),
+            V((T, S * z.Lt, T * I), BF16),
+            V((T, T, S * z.Lt, I), BF16),
+            V((T - 1, T, S * z.Lt, I), BF16),
             V((C, 2, R, F), BF16),
             V((C, 2, R, F), BF16),
             V((T, C, 2, R, I), BF16),
@@ -1050,8 +1079,8 @@
             pltpu.SemaphoreType.DMA((8,)),
             pltpu.SemaphoreType.DMA((SLOTS_IN_FLIGHT + 1,)),
             pltpu.SemaphoreType.DMA((S,)),
-            pltpu.SemaphoreType.DMA((26, T - 1)),
-            pltpu.SemaphoreType.DMA((26, T - 1)),
+            pltpu.SemaphoreType.DMA((24, T - 1)),
+            pltpu.SemaphoreType.DMA((24, T - 1)),
             pltpu.SemaphoreType.DMA((14, max(C - 1, 1))),
             pltpu.SemaphoreType.DMA((14, max(C - 1, 1))),
             pltpu.SemaphoreType.DMA((8 + 2 * C,)),

time: 119 us -> 117 us (0.983)
  Pallas kernels: 118 us -> 116 us
    pallas_call x1, Pallas kernels: 113 us -> 111 us  [on_device(): pl.pallas_call(functools.partial(layer_kernel, z), out_shape=[shape((S, L...]
where the time goes in v5:
time: 117 us
  Pallas kernels  116 us (99%)
    pallas_call x1, Pallas kernels, on_device(): pl.pallas_call(functools.partial(layer_kernel, z), out_shape=[shape((S, L...  111 us
    pallas_call x1, Pallas kernels, on_device(): pl.pallas_call(functools.partial(hand_out, z), out_shape=[shape((S, L, D)...  4.79 us

profile of v5, /device:TPU:0, one launch (start us, length us, event | category | flops | bytes accessed | tf_op | source)
XLA Modules:
  0.0 116.9 jit_solution(8982418404014451964)
XLA Ops:
  0.7 111.3 %resampler_layer.1 = (bf16[4,64,1024]{2,1,0:T(8,128)(2,1)}, bf16[4,320,1024]{2,1,0:T(8,128)(2,1)}, bf16[4,64,1024]{2,1,0:T(8,128)(2,1)}, f32[128,384]{1,0:T(8,12...) custom-call(s32[4]{0:T(128)} %counts.1, ...), custom_call_target="tpu_custom_call" | custom-call | tf_op jit(solution)/shard_map/resampler_layer/pallas_call | solution.py:1090
  111.9 4.8 %hand_out.1 = (bf16[4,64,1024]{2,1,0:T(8,128)(2,1)}, bf16[4,320,1024]{2,1,0:T(8,128)(2,1)}, bf16[4,64,1024]{2,1,0:T(8,128)(2,1)}, f32[128,128]{1,0:T(8,128)}, f3...) custom-call(bf16[4,64,1024]{2,1,0:T(8,128)(2,1)} %get-tuple-element., ...), custom_call_target="tpu_custom_call" | custom-call | tf_op jit(solution)/shard_map/hand_out/pallas_call | solution.py:1127

commit v6 on v5

--- a/solution.py
+++ b/solution.py
@@ -520,7 +520,7 @@
         bgr[:, cols] = (act_grad.astype(F32) * slope).astype(BF16)
         return carry
 
-    lax.fori_loop(0, F // BLOCK, feed, 0, unroll=4)
+    lax.fori_loop(0, F // BLOCK, feed, 0, unroll=2)
     gather_rest(qk_x)
     gather_rest(v_x)
 

time: 117 us -> 116 us (level); the launches traced: 117 us -> 115 us
  Pallas kernels: 116 us -> 114 us
    pallas_call x1, Pallas kernels: 111 us -> 109 us  [on_device(): pl.pallas_call(functools.partial(layer_kernel, z), out_shape=[shape((S, L...]
where the time goes in v6:
time: 116 us; the launch traced here: 115 us
  Pallas kernels  114 us (98%)
    pallas_call x1, Pallas kernels, on_device(): pl.pallas_call(functools.partial(layer_kernel, z), out_shape=[shape((S, L...  109 us
    pallas_call x1, Pallas kernels, on_device(): pl.pallas_call(functools.partial(hand_out, z), out_shape=[shape((S, L, D)...  4.79 us

profile of v6, /device:TPU:0, one launch (start us, length us, event | category | flops | bytes accessed | tf_op | source)
XLA Modules:
  0.0 114.6 jit_solution(17319681613150391481)
XLA Ops:
  0.7 109.0 %resampler_layer.1 = (bf16[4,64,1024]{2,1,0:T(8,128)(2,1)}, bf16[4,320,1024]{2,1,0:T(8,128)(2,1)}, bf16[4,64,1024]{2,1,0:T(8,128)(2,1)}, f32[128,384]{1,0:T(8,12...) custom-call(s32[4]{0:T(128)} %counts.1, ...), custom_call_target="tpu_custom_call" | custom-call | tf_op jit(solution)/shard_map/resampler_layer/pallas_call | solution.py:1090
  109.6 4.8 %hand_out.1 = (bf16[4,64,1024]{2,1,0:T(8,128)(2,1)}, bf16[4,320,1024]{2,1,0:T(8,128)(2,1)}, bf16[4,64,1024]{2,1,0:T(8,128)(2,1)}, f32[128,128]{1,0:T(8,128)}, f3...) custom-call(bf16[4,64,1024]{2,1,0:T(8,128)(2,1)} %get-tuple-element., ...), custom_call_target="tpu_custom_call" | custom-call | tf_op jit(solution)/shard_map/hand_out/pallas_call | solution.py:1127
